TPU v7x, 32 devices: a whole 2x2x4 slice. The times are simulated.
32 devices in a mesh: groups: 2 (over x), gx: 16 (over z, y, core).
Axes of the slice: x: 2, y: 2, z: 4, core: 2. Of those that a mesh axis runs over, the one named last changes fastest.
Arguments:
- samples: bfloat16 [2, 2048, 67328], P(None, ('groups', 'gx')), parts along dimension 1, may hold values from -6 to 6
- flags: int32 [1024], P('gx'), may hold values 0 or 1
- kept_channels: int32 [192], replicated, may hold values from 0 to 255, as said below
- beam_order: int32 [256], replicated, may hold values from 0 to 255, each once
- dm_bins: int32 [512], P('groups'), parts along dimension 0, may hold values from 0 to 4095
- delays: float32 [512, 1024], P('groups'), parts along dimension 0, may hold values from -64 to 64
Outputs:
- visibilities: bfloat16 [384, 1024, 1024], P(('groups', 'gx')), parts along dimension 0
- beam_series: float32 [2, 512, 256, 256], P(None, ('groups', 'gx')), parts along dimension 1
There are 2 independent parts, one for each index of `groups`. A program takes and returns all parts, laid end to end along the dimension named above; an argument that names none is the same for every part. Nothing has to cross between parts.
Inputs may be any that keep to these rules, and one draw needn't show every extreme that they name: `kept_channels`: 192 different bins in increasing order, always including 0 and 255.
All inputs are finite; a program needn't handle non-finite values. No bound on the sum of `flags` on one device may be relied on, other than what follows from the above.
Results may differ from a plain program's by a relative error of at most 0.0075.
Values may be sent and summed in bfloat16 or wider, within the bound.
No kernel may reach another device: no remote copies, remote signals or barrier semaphores. Data moves between devices by JAX's collectives and lax.ppermute only.
A program may use at most 320 MiB of HBM per device.

v0:
```python
import math

import jax
import jax.numpy as jnp
from jax import lax
from jax.sharding import PartitionSpec as P

INPUTS = 1024
POINTS = 256
CHANNELS = 192
BEAMS = 256
TAPS = 8
TICKS = 2
SPEC_TICK = 128


def prototype_taper(tap_count, point_count):
    spots = jnp.arange(tap_count * point_count, dtype=jnp.float32)
    length = float(tap_count * point_count)
    shaped = jnp.sinc((spots - length / 2.0 + 0.5) / point_count) * (
        0.5 - 0.5 * jnp.cos(2.0 * math.pi * (spots + 0.5) / length)
    )
    return shaped.reshape(tap_count, point_count)


def filterbank(samples, taper, start, count):
    point_count = taper.shape[1]
    blocks = samples.reshape(samples.shape[0], samples.shape[1], -1, point_count)
    summed = jnp.zeros((blocks.shape[0], blocks.shape[1], count, point_count), jnp.float32)
    for tap_index in range(taper.shape[0]):
        window = blocks[:, :, start + tap_index : start + tap_index + count, :]
        summed = summed + window.astype(jnp.float32) * taper[tap_index]
    return summed.astype(jnp.bfloat16)


def dft_tables(kept, point_count):
    spots = jnp.arange(point_count, dtype=jnp.int32)
    turns = kept[:, None] * spots[None, :] % point_count
    angle = turns.astype(jnp.float32) * (2.0 * math.pi / point_count)
    scale = 1.0 / math.sqrt(point_count)
    cosine = jnp.cos(angle) * scale
    sine = jnp.sin(angle) * scale
    analysis = jnp.stack([jnp.stack([cosine, sine], 1), jnp.stack([-sine, cosine], 1)], 1).astype(
        jnp.bfloat16
    )
    synthesis = jnp.stack([jnp.stack([cosine, -sine], 0), jnp.stack([sine, cosine], 0)], 0).astype(
        jnp.bfloat16
    )
    return (analysis, synthesis)


def beam_weights(kept_part, tau_rows, point_count, input_count):
    angle = (
        kept_part.astype(jnp.float32)[:, None, None]
        * tau_rows[None, :, :]
        * (2.0 * math.pi / point_count)
    )
    scale = 1.0 / math.sqrt(input_count)
    return (
        (jnp.cos(angle) * scale).astype(jnp.bfloat16),
        (-jnp.sin(angle) * scale).astype(jnp.bfloat16),
    )


def rotation(dm_rows, kept):
    squares = kept * kept % 4096
    turns = squares[:, None] * dm_rows[None, :] % 4096
    angle = turns.astype(jnp.float32) * (2.0 * math.pi / 4096.0)
    return (jnp.cos(angle), jnp.sin(angle))


def rotate(beam_sums, cosine, sine):
    real_part = beam_sums[:, 0].astype(jnp.float32)
    imag_part = beam_sums[:, 1].astype(jnp.float32)
    cos_wide = cosine[:, :, None]
    sin_wide = sine[:, :, None]
    first = real_part * cos_wide + imag_part * sin_wide
    second = imag_part * cos_wide - real_part * sin_wide
    return jnp.stack([first, second], 1).astype(jnp.bfloat16)


def packed_sum(turned):
    input_count = turned.shape[2]
    real_sum = jnp.einsum("cxis,cxjs->cij", turned, turned, preferred_element_type=jnp.float32)
    mixed = jnp.einsum(
        "cis,cjs->cij", turned[:, 1], turned[:, 0], preferred_element_type=jnp.float32
    )
    upper_mask = jnp.arange(input_count)[:, None] <= jnp.arange(input_count)[None, :]
    return jnp.where(upper_mask[None], real_sum, mixed - jnp.transpose(mixed, (0, 2, 1)))


def form_beams(weight_real, weight_imag, turned):
    first = jnp.einsum("cbi,cxis->cxbs", weight_real, turned, preferred_element_type=jnp.float32)
    second = jnp.einsum("cbi,cxis->cxbs", weight_imag, turned, preferred_element_type=jnp.float32)
    return jnp.stack([first[:, 0] - second[:, 1], first[:, 1] + second[:, 0]], 1).astype(
        jnp.bfloat16
    )


def shards(samples, flags, kept_channels, beam_order, dm_bins, delays):
    gx_count = lax.axis_size("gx")
    my_index = lax.axis_index("gx")
    chan_dev = CHANNELS // gx_count
    beam_dev = BEAMS // gx_count
    spectra_all = TICKS * SPEC_TICK
    taper = prototype_taper(TAPS, POINTS)
    analysis, synthesis = dft_tables(kept_channels, POINTS)
    input_gain = flags.astype(jnp.float32)[None, None, :, None]
    my_kept = lax.dynamic_slice_in_dim(kept_channels, my_index * chan_dev, chan_dev)
    weight_real, weight_imag = beam_weights(
        my_kept, jnp.take(delays, beam_order, axis=0), POINTS, INPUTS
    )
    frames = filterbank(samples, taper, 0, spectra_all)
    spectra = jnp.einsum("coxn,xisn->cois", analysis, frames, preferred_element_type=jnp.float32)
    turned = lax.all_to_all(
        (spectra * input_gain).astype(jnp.bfloat16), "gx", split_axis=0, concat_axis=2, tiled=True
    )
    packed = packed_sum(turned)
    beam_sums = form_beams(weight_real, weight_imag, turned)
    visibilities = (packed / spectra_all).astype(jnp.bfloat16)
    own_beams = jnp.take(beam_order, my_index * beam_dev + jnp.arange(beam_dev, dtype=jnp.int32))
    cosine, sine = rotation(jnp.take(dm_bins, own_beams), kept_channels)
    rotated = rotate(
        lax.all_to_all(beam_sums, "gx", split_axis=2, concat_axis=0, tiled=True), cosine, sine
    )
    series = jnp.einsum("oxcn,cxbs->obsn", synthesis, rotated, preferred_element_type=jnp.float32)
    return (visibilities, series)


def solution(mesh):
    placed = (P(None, ("groups", "gx"), None), P("gx"), P(), P(), P("groups"), P("groups", None))
    return jax.shard_map(
        shards,
        mesh=mesh,
        in_specs=placed,
        out_specs=(P(("groups", "gx"), None, None), P(None, ("groups", "gx"), None, None)),
        check_vma=False,
    )
```

profile of v0, /device:TPU:13, one launch (start us, length us, event | category | flops | bytes accessed | tf_op | source)
XLA Modules:
  0.0 661.6 jit_solution(16490591929981354611)
XLA Ops:
  0.6 0.0 copy-start
  0.6 0.1 fusion.63
  0.7 0.7 convert_element_type.119
  1.4 1.6 fusion.54
  3.0 21.1 %reshape.372 = bf16[2,64,263,256]{3,2,1,0:T(8,128)(2,1)} reshape(bf16[2,64,67328]{2,1,0:T(8,128)(2,1)} %param.8) | data formatting | bytes 34471936 | tf_op jit(solution)/shard_map/reshape | solution.py:28
  24.2 63.1 %fusion.3 = bf16[192,2,64,256]{3,0,2,1:T(8,128)(2,1)} fusion(f32[64]{0:T(128)S(1)} %convert_element_type.119, bf16[192,1,2,256]{3,0,2,1:T(8,128)(2,1)S(1)} %get-tuple-element.18, bf16[192,1,2,256]{3,0,2,1:T(8,128)(2,1)S(1)} %get-tuple-element.17, bf16[2,64,263,256]{3,2,1,0:T(8,128)(2,1)} %reshape.372, f32[256]{0:T(256)S(1)} %get-tuple-element.20, ...), kind=kOutput, calls=%fused_computation.9 | convolution fusion | flops 6657146880 | bytes 147202304 | tf_op jit(solution)/shard_map/coxn,xisn->cois/dot_general | solution.py:114
  87.3 14.0 %copy.34 = bf16[192,2,64,256]{3,2,1,0:T(8,128)(2,1)} copy(bf16[192,2,64,256]{3,0,2,1:T(8,128)(2,1)} %fusion.3) | data formatting | bytes 25165824 | tf_op jit(solution)/shard_map/convert_element_type | solution.py:116
  101.3 0.0 copy-start.3
  101.3 0.0 copy-start.4
  101.3 0.0 copy-start.7
  101.3 7.0 %all-to-all-start = ((bf16[192,2,64,256]{3,2,1,0:T(8,128)(2,1)}), bf16[192,2,64,256]{3,2,1,0:T(8,128)(2,1)}, u32[]{:S(2)}, u32[]{:S(2)}) async-start(bf16[192,2,64,256]{3,2,1,0:T(8,128)(2,1)} %copy.34), calls=%async_computation | async-start | bytes 25165824 | tf_op jit(solution)/shard_map/all_to_all | solution.py:115
  108.4 0.0 copy-done.3
  108.4 0.7 gather_fusion.1
  109.1 0.0 copy-done.4
  109.1 0.7 gather_fusion.2
  109.8 0.0 copy-done
  109.8 1.1 gather_fusion
  110.9 0.0 copy-done.7
  110.9 0.1 dynamic-slice_convert_fusion
  111.0 0.9 negate_convert_fusion
  111.9 0.3 iota_compare_fusion
  112.3 0.8 fusion.89
  113.0 0.1 broadcast_select_fusion
  113.2 267.3 %all-to-all-done = bf16[192,2,64,256]{3,2,1,0:T(8,128)(2,1)} async-done(((bf16[192,2,64,256]{3,2,1,0:T(8,128)(2,1)}), bf16[192,2,64,256]{3,2,1,0:T(8,128)(2,1)}, u32[]{:S(2)}, u32[]{:S(2)}) %all-to-all-start) | async-done | bytes 12582944 | tf_op jit(solution)/shard_map/all_to_all | solution.py:115
  380.4 10.7 %copy.35 = bf16[12,2,16,64,256]{4,3,2,1,0:T(8,128)(2,1)} copy(bf16[12,2,16,64,256]{4,3,1,0,2:T(8,128)(2,1)} %bitcast.8) | data formatting | bytes 25165824 | tf_op jit(solution)/shard_map/all_to_all | solution.py:115
  391.1 22.2 %fusion.13 = f32[12,1024,1024]{2,1,0:T(8,128)} fusion(bf16[12,2,1024,256]{3,2,1,0:T(8,128)(2,1)} %bitcast.99), kind=kOutput, calls=%fused_computation.21 | convolution fusion | flops 6442450944 | bytes 62914560 | tf_op jit(solution)/shard_map/cis,cjs->cij/dot_general | solution.py:85
  413.4 0.0 copy-start.2
  413.4 49.2 %fusion.35 = f32[12,2,256,256]{2,3,1,0:T(8,128)} fusion(bf16[12,2,1024,256]{3,2,1,0:T(8,128)(2,1)} %bitcast.100, f32[256,1024]{1,0:T(8,128)S(1)} %broadcast_select_fusion, f32[12]{0:T(128)S(1)} %dynamic-slice_convert_fusion), kind=kOutput, calls=%fused_computation.50 | convolution fusion | flops 3236954112 | bytes 19922992 | tf_op jit(solution)/shard_map/cbi,cxis->cxbs/dot_general | solution.py:94
  462.5 0.0 copy-done.2
  462.5 47.0 %fusion.32 = f32[12,2,256,256]{2,3,1,0:T(8,128)} fusion(bf16[12,2,1024,256]{3,2,1,0:T(8,128)(2,1)S(1)} %bitcast.102, f32[256,1024]{1,0:T(8,128)S(1)} %broadcast_select_fusion, f32[12]{0:T(128)S(1)} %dynamic-slice_convert_fusion), kind=kOutput, calls=%fused_computation.49 | convolution fusion | flops 3233808384 | bytes 19922992 | tf_op jit(solution)/shard_map/cbi,cxis->cxbs/dot_general | solution.py:93
  509.5 49.1 %copy.36 = f32[12,1024,1024]{1,2,0:T(8,128)} copy(f32[12,1024,1024]{2,1,0:T(8,128)} %fusion.13) | data formatting | bytes 100663296 | tf_op jit(solution)/shard_map/cis,cjs->cij/dot_general | solution.py:85
  558.7 5.7 fusion.29
  564.4 1.9 pad_maximum_fusion
  566.3 8.7 %copy.39 = bf16[12,2,256,256]{3,1,0,2:T(2,128)(2,1)} copy(bf16[12,2,256,256]{2,3,1,0:T(8,128)(2,1)} %pad_maximum_fusion) | data formatting | bytes 6291456 | tf_op jit(solution)/shard_map/stack | solution.py:95
  575.0 4.9 all-to-all-start.1
  579.9 48.8 %fusion.2 = bf16[12,1024,1024]{2,1,0:T(8,128)(2,1)} fusion(f32[12,1024,1024]{2,1,0:T(8,128)} %fusion.13, f32[12,1024,1024]{1,2,0:T(8,128)} %copy.36, pred[1024,1024]{1,0:T(8,128)(4,1)S(1)} %iota_compare_fusion, bf16[12,2,1024,256]{3,2,1,0:T(8,128)(2,1)} %bitcast.101), kind=kOutput, calls=%fused_computation.6 | convolution fusion | flops 12935233536 | bytes 139460608 | tf_op jit(solution)/shard_map/cxis,cxjs->cij/dot_general | solution.py:84
  628.7 0.0 copy-start.5
  628.7 0.0 copy-start.6
  628.7 21.2 %all-to-all-done.1 = bf16[12,2,256,256]{3,1,0,2:T(2,128)(2,1)} async-done(((bf16[12,2,256,256]{3,1,0,2:T(2,128)(2,1)}), bf16[12,2,256,256]{3,1,0,2:T(2,128)(2,1)}, u32[]{:S(2)}, u32[]{:S(2)}) %all-to-all-start.1) | async-done | bytes 3145760 | tf_op jit(solution)/shard_map/all_to_all | solution.py:124
  649.9 2.6 copy.40
  652.5 0.5 copy.41
  653.0 0.2 fusion.97
  653.2 0.0 copy-done.5
  653.2 0.0 copy-done.6
  653.2 1.5 fusion.25
  654.8 0.0 copy-start.1
  654.8 2.4 convolution_bitcast_fusion
  657.2 4.0 copy.44
  661.2 0.0 copy-done.1
  (12 shorter events, 0.1 us)
Async XLA Ops:
  0.6 109.1 %copy-start = (f32[256,1024]{1,0:T(8,128)S(1)}, f32[256,1024]{1,0:T(8,128)}, u32[]{:S(2)}) copy-start(f32[256,1024]{1,0:T(8,128)} %param.13) | copy-start | bytes 3145732
  101.3 7.1 %copy-start.3 = (s32[256]{0:T(256)S(1)}, s32[256]{0:T(256)}, u32[]{:S(2)}) copy-start(s32[256]{0:T(256)} %param.11) | copy-start | bytes 3076
  101.3 7.8 %copy-start.4 = (s32[256]{0:T(256)S(1)}, s32[256]{0:T(256)}, u32[]{:S(2)}) copy-start(s32[256]{0:T(256)} %param.12) | copy-start | bytes 3076
  101.3 9.5 %copy-start.7 = (s32[192]{0:T(256)S(1)}, s32[192]{0:T(256)}, u32[]{:S(2)}) copy-start(s32[192]{0:T(256)} %param.10) | copy-start | bytes 2308
  101.3 279.1 %all-to-all-start = ((bf16[192,2,64,256]{3,2,1,0:T(8,128)(2,1)}), bf16[192,2,64,256]{3,2,1,0:T(8,128)(2,1)}, u32[]{:S(2)}, u32[]{:S(2)}) async-start(bf16[192,2,64,256]{3,2,1,0:T(8,128)(2,1)} %copy.34), calls=%async_computation | async-start | bytes 25165824 | tf_op jit(solution)/shard_map/all_to_all | solution.py:115
  413.4 49.2 %copy-start.2 = (bf16[12,2,16,64,256]{4,3,2,1,0:T(8,128)(2,1)S(1)}, bf16[12,2,16,64,256]{4,3,2,1,0:T(8,128)(2,1)}, u32[]{:S(2)}) copy-start(bf16[12,2,16,64,256]{4,3,2,1,0:T(8,128)(2,1)} %copy.35) | copy-start | bytes 37748740
  575.0 74.9 %all-to-all-start.1 = ((bf16[12,2,256,256]{3,1,0,2:T(2,128)(2,1)}), bf16[12,2,256,256]{3,1,0,2:T(2,128)(2,1)}, u32[]{:S(2)}, u32[]{:S(2)}) async-start(bf16[12,2,256,256]{3,1,0,2:T(2,128)(2,1)} %copy.39), calls=%async_computation.1 | async-start | bytes 6291456 | tf_op jit(solution)/shard_map/all_to_all | solution.py:124
  628.7 24.5 %copy-start.5 = (f32[192,16]{0,1:T(8,128)S(1)}, f32[192,16]{0,1:T(8,128)}, u32[]{:S(2)}) copy-start(f32[192,16]{0,1:T(8,128)} %get-tuple-element.27) | copy-start | bytes 36868
  628.7 24.5 %copy-start.6 = (f32[192,16]{0,1:T(8,128)S(1)}, f32[192,16]{0,1:T(8,128)}, u32[]{:S(2)}) copy-start(f32[192,16]{0,1:T(8,128)} %get-tuple-element.28) | copy-start | bytes 36868
  654.8 6.4 copy-start.1
where the time goes:
time: 671 us; the launch traced here: 662 us
  waiting for transfers between devices  288 us (43%)
  matrix products  233 us (35%)
  local copies, waits for them, and re-layouts  113 us (17%)
  other arithmetic  13.8 us (2%)
  starting transfers between devices  11.9 us (2%)
    all_to_all x1, waiting for transfers between devices, shards(): lax.all_to_all((spectra * input_gain).astype(jnp.bfloat16), 'gx', split_a...  267 us
    dot_general x1, matrix products, shards(): jnp.einsum('coxn,xisn->cois', analysis, frames, preferred_element_type=jn...  63.1 us
    dot_general x1, matrix products, form_beams(): jnp.einsum('cbi,cxis->cxbs', weight_imag, turned, preferred_element_type=...  49.2 us
    dot_general x1, local copies, waits for them, and re-layouts, packed_sum(): jnp.einsum('cis,cjs->cij', turned[:, 1], turned[:, 0], preferred_element_...  49.1 us
    dot_general x1, matrix products, packed_sum(): jnp.einsum('cxis,cxjs->cij', turned, turned, preferred_element_type=jnp.f...  48.8 us
    dot_general x1, matrix products, form_beams(): jnp.einsum('cbi,cxis->cxbs', weight_real, turned, preferred_element_type=...  47 us
    dot_general x1, matrix products, packed_sum(): jnp.einsum('cis,cjs->cij', turned[:, 1], turned[:, 0], preferred_element_...  22.2 us
    all_to_all x1, waiting for transfers between devices, shards(): lax.all_to_all(beam_sums, 'gx', split_axis=2, concat_axis=0, tiled=True)  21.2 us
  transfers between devices with their start and end apart: 2, of which 2 were waited for; matrix products, arithmetic and copies ran while one was open for 8% of the time, Pallas kernels for 0%

commit v1 on v0

v1 whole, which is shorter than its diff:
```python
import functools
import math

import jax
import jax.numpy as jnp
import numpy as np
from jax import lax
from jax.experimental import pallas as pl
from jax.experimental.pallas import tpu as pltpu
from jax.sharding import PartitionSpec as P

POINTS = 256
TAPS = 8
ROWS = 16
STRETCH = 8
F32 = jnp.float32
BF16 = jnp.bfloat16
VMEM = 60 * 1024 * 1024


def fit_tables():
    spots = np.cos(np.pi * (np.arange(4000) + 0.5) / 4000) * 0.125 + 0.125
    powers = np.stack([spots ** (2 * k) for k in range(6)], 1)
    weight = np.ones_like(spots)
    sine = np.linalg.lstsq(powers[:, :5] * spots[:, None], np.sin(2 * np.pi * spots), rcond=None)[0]
    cosine = np.linalg.lstsq(powers, np.cos(2 * np.pi * spots) * weight, rcond=None)[0]
    return [float(v) for v in sine], [float(v) for v in cosine]


SINE_FIT, COSINE_FIT = fit_tables()


def prototype_taper(tap_count, point_count):
    spots = jnp.arange(tap_count * point_count, dtype=F32)
    length = float(tap_count * point_count)
    shaped = jnp.sinc((spots - length / 2.0 + 0.5) / point_count) * (
        0.5 - 0.5 * jnp.cos(2.0 * math.pi * (spots + 0.5) / length)
    )
    return shaped.reshape(tap_count, point_count)


def dft_tables(kept, point_count):
    spots = jnp.arange(point_count, dtype=jnp.int32)
    turns = kept[:, None] * spots[None, :] % point_count
    angle = turns.astype(F32) * (2.0 * math.pi / point_count)
    scale = 1.0 / math.sqrt(point_count)
    return jnp.cos(angle) * scale, jnp.sin(angle) * scale


def rotation(dm_rows, kept):
    squares = kept * kept % 4096
    turns = squares[:, None] * dm_rows[None, :] % 4096
    angle = turns.astype(F32) * (2.0 * math.pi / 4096.0)
    return (jnp.cos(angle), jnp.sin(angle))


def pieces(count, least):
    parts = min(least, count)
    edges = [count * k // parts for k in range(parts + 1)]
    return [(edges[k], edges[k + 1]) for k in range(parts)]


def spectra_kernel(counts, flags_ref, samples_ref, taper_ref, analysis_ref, *refs):
    out_refs, (frames_ref, wide_ref) = refs[: len(counts)], refs[len(counts) :]
    spectra_all = frames_ref.shape[1] // ROWS
    co_rows = analysis_ref.shape[0]

    def form_frames(step, carry):
        first = step * STRETCH
        for x in range(2):
            for half in range(POINTS // 128):
                lanes = pl.ds(half * 128, 128)
                tapers = [
                    jnp.broadcast_to(taper_ref[pl.ds(t, 1), lanes], (ROWS, 128)) for t in range(TAPS)
                ]
                tiles = []
                for k in range(STRETCH + TAPS - 1):
                    spot = pl.multiple_of((first + k) * POINTS + half * 128, 128)
                    tiles.append(samples_ref[x, :, pl.ds(spot, 128)].astype(F32))
                for s in range(STRETCH):
                    total = tiles[s] * tapers[0]
                    for t in range(1, TAPS):
                        total = total + tiles[s + t] * tapers[t]
                    row = pl.multiple_of((first + s) * ROWS, ROWS)
                    frames_ref[x * (POINTS // 128) + half, pl.ds(row, ROWS), :] = total
        return carry

    lax.fori_loop(0, spectra_all // STRETCH, form_frames, 0)

    group = pl.program_id(0)

    def transform(i, carry):
        frame = jnp.concatenate(
            [
                frames_ref[k, pl.ds(i, spectra_all, stride=ROWS), :].astype(BF16)
                for k in range(2 * POINTS // 128)
            ],
            axis=1,
        )
        product = lax.dot_general(
            analysis_ref[...], frame, (((1,), (1,)), ((), ())), preferred_element_type=F32
        )
        product = product * flags_ref[group * ROWS + i].astype(F32)
        for k in range(spectra_all // 128):
            wide_ref[k, pl.ds(i, co_rows, stride=ROWS), :] = product[:, k * 128 : (k + 1) * 128]
        return carry

    lax.fori_loop(0, ROWS, transform, 0)

    base = 0
    for count, out_ref in zip(counts, out_refs):
        gx_count = out_ref.shape[0]
        per = 2 * count

        def send_rows(d, carry, base=base, per=per, out_ref=out_ref):
            for k in range(per):
                row = pl.multiple_of((base + d * per + k) * ROWS, ROWS)
                for part in range(wide_ref.shape[0]):
                    out_ref[d, k // 2, k % 2, :, part * 128 : (part + 1) * 128] = wide_ref[
                        part, pl.ds(row, ROWS), :
                    ].astype(BF16)
            return carry

        lax.fori_loop(0, gx_count, send_rows, 0)
        base += gx_count * per


def spectra_of(samples, flags, taper, analysis, gx_count, counts, first, groups, spectra_all):
    co_rows = analysis.shape[0]
    return pl.pallas_call(
        functools.partial(spectra_kernel, counts),
        out_shape=[
            jax.ShapeDtypeStruct((gx_count, n, 2, groups * ROWS, spectra_all), BF16) for n in counts
        ],
        grid=(groups,),
        in_specs=[
            pl.BlockSpec(memory_space=pltpu.SMEM),
            pl.BlockSpec((2, ROWS, samples.shape[2]), lambda g: (0, g + first, 0)),
            pl.BlockSpec((TAPS, POINTS), lambda g: (0, 0)),
            pl.BlockSpec((co_rows, 2 * POINTS), lambda g: (0, 0)),
        ],
        out_specs=[
            pl.BlockSpec((gx_count, n, 2, ROWS, spectra_all), lambda g: (0, 0, 0, g, 0))
            for n in counts
        ],
        scratch_shapes=[
            pltpu.VMEM((2 * POINTS // 128, spectra_all * ROWS, 128), F32),
            pltpu.VMEM((spectra_all // 128, co_rows * ROWS, 128), F32),
        ],
        compiler_params=pltpu.CompilerParams(vmem_limit_bytes=VMEM),
        cost_estimate=pl.CostEstimate(
            flops=groups * ROWS * spectra_all * co_rows * 4 * POINTS,
            bytes_accessed=groups * ROWS * (samples.shape[2] * 4 + co_rows * spectra_all * 2),
            transcendentals=0,
        ),
        name="spectra",
    )(lax.dynamic_slice_in_dim(flags, first * ROWS, groups * ROWS), samples, taper, analysis)


def weights_kernel(kept_ref, delays_ref, out_ref):
    scale = kept_ref[pl.program_id(0)].astype(F32) * (1.0 / POINTS)
    input_scale = 1.0 / math.sqrt(delays_ref.shape[1])

    def rows(step, carry):
        at = pl.ds(pl.multiple_of(step * 16, 16), 16)
        turns = delays_ref[at, :] * scale
        turns = turns - jnp.floor(turns + 0.5)
        size = jnp.abs(turns)
        near = jnp.minimum(size, 0.5 - size)
        square = near * near
        sine = square * SINE_FIT[-1] + SINE_FIT[-2]
        for value in SINE_FIT[-3::-1]:
            sine = sine * square + value
        sine = sine * (near * input_scale)
        cosine = square * COSINE_FIT[-1] + COSINE_FIT[-2]
        for value in COSINE_FIT[-3::-1]:
            cosine = cosine * square + value
        cosine = cosine * input_scale
        out_ref[0, 0, at, :] = jnp.where(size > 0.25, -cosine, cosine).astype(BF16)
        out_ref[0, 1, at, :] = jnp.where(turns > 0.0, -sine, sine).astype(BF16)
        return carry

    lax.fori_loop(0, delays_ref.shape[0] // 16, rows, 0)


def weights_of(kept, delays):
    beams, inputs = delays.shape
    return pl.pallas_call(
        weights_kernel,
        out_shape=jax.ShapeDtypeStruct((kept.shape[0], 2, beams, inputs), BF16),
        grid=(kept.shape[0],),
        in_specs=[
            pl.BlockSpec(memory_space=pltpu.SMEM),
            pl.BlockSpec((beams, inputs), lambda c: (0, 0)),
        ],
        out_specs=pl.BlockSpec((1, 2, beams, inputs), lambda c: (c, 0, 0, 0)),
        compiler_params=pltpu.CompilerParams(vmem_limit_bytes=VMEM),
        cost_estimate=pl.CostEstimate(
            flops=kept.shape[0] * beams * inputs * 40,
            bytes_accessed=kept.shape[0] * beams * inputs * 4,
            transcendentals=0,
        ),
        name="weights",
    )(kept, delays)


def assemble(parts, joined_ref):
    span = sum(part.shape[3] for part in parts)
    for src in range(parts[0].shape[0]):
        at = src * span
        for part in parts:
            rows = part.shape[3]
            for o in range(2):
                joined_ref[o, at : at + rows, :] = part[src, 0, o]
            at += rows


def beams_kernel(part_count, *refs):
    parts, (weights_ref, turn_ref, out_ref, joined_ref) = refs[:part_count], refs[part_count:]
    assemble(parts, joined_ref)
    beams = weights_ref.shape[2]
    weights = weights_ref[0].reshape(2 * beams, weights_ref.shape[3])
    products = [
        jnp.dot(weights, joined_ref[o], preferred_element_type=F32) for o in range(2)
    ]
    real_part = (products[0][:beams] - products[1][beams:]).astype(BF16).astype(F32)
    imag_part = (products[1][:beams] + products[0][beams:]).astype(BF16).astype(F32)
    cosine, sine = turn_ref[0, :, 0:1], turn_ref[0, :, 1:2]
    first = (real_part * cosine + imag_part * sine).astype(BF16)
    second = (imag_part * cosine - real_part * sine).astype(BF16)
    if len(out_ref.shape) == 5:
        out_ref[:, 0, 0] = first.reshape(out_ref.shape[0], out_ref.shape[3], out_ref.shape[4])
        out_ref[:, 0, 1] = second.reshape(out_ref.shape[0], out_ref.shape[3], out_ref.shape[4])
    else:
        out_ref[0, 0] = first
        out_ref[0, 1] = second


def part_specs(arrays, firsts):
    return [
        pl.BlockSpec(
            (a.shape[0], 1, 2, a.shape[3], a.shape[4]),
            functools.partial(lambda c, first: (0, c + first, 0, 0, 0), first=first),
        )
        for a, first in zip(arrays, firsts)
    ]


def beams_of(arrays, firsts, weights, turns, first, count, gx_count):
    beams, inputs = weights.shape[2:]
    spectra_all = arrays[0].shape[4]
    beam_dev = beams // gx_count
    if beam_dev % 16 == 0:
        out_shape = (gx_count, count, 2, beam_dev, spectra_all)
        out_spec = pl.BlockSpec((gx_count, 1, 2, beam_dev, spectra_all), lambda c: (0, c, 0, 0, 0))
    else:
        out_shape = (count, 2, beams, spectra_all)
        out_spec = pl.BlockSpec((1, 2, beams, spectra_all), lambda c: (c, 0, 0, 0))
    out = pl.pallas_call(
        functools.partial(beams_kernel, len(arrays)),
        out_shape=jax.ShapeDtypeStruct(out_shape, BF16),
        grid=(count,),
        in_specs=part_specs(arrays, firsts)
        + [
            pl.BlockSpec((1, 2, beams, inputs), lambda c: (c + first, 0, 0, 0)),
            pl.BlockSpec((1, beams, 2), lambda c: (c + first, 0, 0)),
        ],
        out_specs=out_spec,
        scratch_shapes=[pltpu.VMEM((2, inputs, spectra_all), BF16)],
        compiler_params=pltpu.CompilerParams(vmem_limit_bytes=VMEM),
        cost_estimate=pl.CostEstimate(
            flops=count * beams * inputs * spectra_all * 8,
            bytes_accessed=count * inputs * (spectra_all * 4 + beams * 4),
            transcendentals=0,
        ),
        name="beams",
    )(*arrays, weights, turns)
    if beam_dev % 16:
        out = out.reshape(count, 2, gx_count, beam_dev, spectra_all).transpose(2, 0, 1, 3, 4)
    return out


def gram_kernel(part_count, *refs):
    parts, (out_ref, joined_ref) = refs[:part_count], refs[-2:]
    assemble(parts, joined_ref)
    inputs, spectra_all = joined_ref.shape[1:]
    side = 256
    scale = 1.0 / spectra_all
    contract = (((1,), (1,)), ((), ()))

    def product(left, right, rows, columns):
        return lax.dot_general(
            joined_ref[left, rows], joined_ref[right, columns], contract, preferred_element_type=F32
        )

    for j in range(inputs // side):
        columns = slice(j * side, (j + 1) * side)
        above = slice(0, (j + 1) * side)
        below = slice(j * side, inputs)
        real_sum = product(0, 0, above, columns) + product(1, 1, above, columns)
        mixed = product(1, 0, below, columns) - product(0, 1, below, columns)
        if j:
            out_ref[0, : j * side, columns] = (real_sum[: j * side] * scale).astype(BF16)
        upper = lax.broadcasted_iota(jnp.int32, (side, side), 0) <= lax.broadcasted_iota(
            jnp.int32, (side, side), 1
        )
        out_ref[0, columns, columns] = (
            jnp.where(upper, real_sum[j * side :], mixed[:side]) * scale
        ).astype(BF16)
        if (j + 1) * side < inputs:
            out_ref[0, (j + 1) * side :, columns] = (mixed[side:] * scale).astype(BF16)


def gram_of(arrays, firsts, first, count, channels, held):
    spectra_all = arrays[0].shape[4]
    inputs = arrays[0].shape[0] * sum(a.shape[3] for a in arrays)
    more = [] if held is None else [held]
    return pl.pallas_call(
        functools.partial(gram_kernel, len(arrays)),
        out_shape=jax.ShapeDtypeStruct((channels, inputs, inputs), BF16),
        grid=(count,),
        in_specs=part_specs(arrays, firsts) + [pl.BlockSpec(memory_space=pl.ANY)] * len(more),
        out_specs=pl.BlockSpec((1, inputs, inputs), lambda c: (c + first, 0, 0)),
        scratch_shapes=[pltpu.VMEM((2, inputs, spectra_all), BF16)],
        input_output_aliases={len(arrays): 0} if more else {},
        compiler_params=pltpu.CompilerParams(vmem_limit_bytes=VMEM),
        cost_estimate=pl.CostEstimate(
            flops=count * inputs * inputs * spectra_all * 5,
            bytes_accessed=count * inputs * (spectra_all * 4 + inputs * 2),
            transcendentals=0,
        ),
        name="gram",
    )(*arrays, *more)


def series_kernel(part_count, *refs):
    parts, (synthesis_ref, out_ref, wide_ref) = refs[:part_count], refs[part_count:]
    beam = pl.program_id(0)
    beam_dev, spectra_all = parts[0].shape[3:]
    rows = synthesis_ref.shape[0]

    @pl.when(beam == 0)
    def _():
        base = 0
        for part in parts:
            sources, count = part.shape[:2]

            def widen(d, carry, base=base, part=part, count=count):
                for k in range(2 * count):
                    row = pl.multiple_of((base + d * 2 * count + k) * beam_dev, beam_dev)
                    for half in range(spectra_all // 128):
                        wide_ref[half, pl.ds(row, beam_dev), :] = part[
                            d, k // 2, k % 2, :, half * 128 : (half + 1) * 128
                        ].astype(F32)
                return carry

            lax.fori_loop(0, sources, widen, 0)
            base += sources * count * 2

    turned = jnp.concatenate(
        [
            wide_ref[k, pl.ds(beam, rows, stride=beam_dev), :].astype(BF16)
            for k in range(spectra_all // 128)
        ],
        axis=1,
    )
    product = lax.dot_general(
        turned, synthesis_ref[...], (((0,), (0,)), ((), ())), preferred_element_type=F32
    )
    for o in range(2):
        out_ref[o, 0] = product[:, o * POINTS : (o + 1) * POINTS]


def series_of(arrays, synthesis):
    gx_count, _, _, beam_dev, spectra_all = arrays[0].shape
    rows = synthesis.shape[0]
    return pl.pallas_call(
        functools.partial(series_kernel, len(arrays)),
        out_shape=jax.ShapeDtypeStruct((2, beam_dev, spectra_all, POINTS), F32),
        grid=(beam_dev,),
        in_specs=[pl.BlockSpec(a.shape, lambda b: (0, 0, 0, 0, 0)) for a in arrays]
        + [pl.BlockSpec(synthesis.shape, lambda b: (0, 0))],
        out_specs=pl.BlockSpec((2, 1, spectra_all, POINTS), lambda b: (0, b, 0, 0)),
        scratch_shapes=[pltpu.VMEM((spectra_all // 128, rows * beam_dev, 128), F32)],
        compiler_params=pltpu.CompilerParams(vmem_limit_bytes=VMEM),
        cost_estimate=pl.CostEstimate(
            flops=2 * beam_dev * rows * spectra_all * 2 * POINTS,
            bytes_accessed=beam_dev * spectra_all * (rows * 2 + POINTS * 8),
            transcendentals=0,
        ),
        name="series",
    )(*arrays, synthesis)


def exchange(array):
    return lax.all_to_all(array, "gx", split_axis=0, concat_axis=0, tiled=True)


def shards(samples, flags, kept_channels, beam_order, dm_bins, delays):
    gx_count = lax.axis_size("gx")
    my_index = lax.axis_index("gx")
    channels = kept_channels.shape[0]
    chan_dev = channels // gx_count
    spectra_all = samples.shape[2] // POINTS - TAPS + 1
    groups = samples.shape[1] // ROWS

    taper = prototype_taper(TAPS, POINTS)
    cosine, sine = dft_tables(kept_channels, POINTS)
    table = jnp.stack(
        [jnp.concatenate([cosine, sine], 1), jnp.concatenate([-sine, cosine], 1)], 1
    ).astype(BF16)
    by_owner = jnp.reshape(table, (gx_count, chan_dev, 2, 2 * POINTS))
    chunks = pieces(chan_dev, 3)

    def ordered(table, cuts):
        return jnp.concatenate(
            [table[:, a:b].reshape(-1, 2 * POINTS) for a, b in cuts], 0
        )

    lead = 1 if groups > 1 else 0
    parts = []
    if lead:
        (head,) = spectra_of(
            samples, flags, taper, ordered(by_owner, [(0, chan_dev)]), gx_count, [chan_dev], 0, 1,
            spectra_all,
        )
        head = exchange(head)
    rest = spectra_of(
        samples, flags, taper, ordered(by_owner, chunks), gx_count, [b - a for a, b in chunks],
        lead, groups - lead, spectra_all,
    )
    rest = [exchange(r) for r in rest]

    my_kept = lax.dynamic_slice_in_dim(kept_channels, my_index * chan_dev, chan_dev)
    weights = weights_of(my_kept, jnp.take(delays, beam_order, axis=0))
    turns = jnp.stack(rotation(jnp.take(dm_bins, beam_order), my_kept), 2)

    visibilities = None
    sums = []
    for (a, b), block in zip(chunks, rest):
        arrays, firsts = ([head, block], [a, 0]) if lead else ([block], [0])
        sums.append(exchange(beams_of(arrays, firsts, weights, turns, a, b - a, gx_count)))
        visibilities = gram_of(arrays, firsts, a, b - a, chan_dev, visibilities)
    series = series_of(
        sums, ordered(by_owner, chunks)
    )
    return (visibilities, series)


def solution(mesh):
    placed = (P(None, ("groups", "gx"), None), P("gx"), P(), P(), P("groups"), P("groups", None))
    return jax.shard_map(
        shards,
        mesh=mesh,
        in_specs=placed,
        out_specs=(P(("groups", "gx"), None, None), P(None, ("groups", "gx"), None, None)),
        check_vma=False,
    )
```

time: 671 us -> 434 us (0.65); the launches traced: 662 us -> 432 us
  matrix products: 233 us -> 0 us
  waiting for transfers between devices: 288 us -> 91.5 us
  blocking collectives: 0 us -> 150 us
  Pallas kernels: 0 us -> 148 us
  local copies, waits for them, and re-layouts: 113 us -> 9.18 us
  starting transfers between devices: 11.9 us -> 26.8 us
  other arithmetic: 13.8 us -> 5.47 us
    dot_general x6 -> x0, matrix products: 233 us -> none  [the longest x1 63.1 us: shards(): jnp.einsum('coxn,xisn->cois', analysis, frames, preferred_element_type=jn...]
    all_to_all x2 -> x5, waiting for transfers between devices: 288 us -> 91.5 us  [exchange(): return lax.all_to_all(array, 'gx', split_axis=0, concat_axis=0, tiled=True)]
    all_to_all x0 -> x2, blocking collectives: none -> 150 us  [exchange(): return lax.all_to_all(array, 'gx', split_axis=0, concat_axis=0, tiled=True)]
    pallas_call x0 -> x10, Pallas kernels: none -> 148 us  [the longest x2 69.2 us: spectra_of(): pl.pallas_call(functools.partial(spectra_kernel, counts), out_shape=[jax....]
    dot_general x1 -> x0, local copies, waits for them, and re-layouts: 49.1 us -> none  [packed_sum(): jnp.einsum('cis,cjs->cij', turned[:, 1], turned[:, 0], preferred_element_...]
    reshape x1 -> x3, local copies, waits for them, and re-layouts: 21.1 us -> 0.17 us  [ordered(): table[:, a:b].reshape(-1, 2 * POINTS)]
    all_to_all x2 -> x5, starting transfers between devices: 11.9 us -> 26.8 us  [exchange(): return lax.all_to_all(array, 'gx', split_axis=0, concat_axis=0, tiled=True)]
    all_to_all x3 -> x0, local copies, waits for them, and re-layouts: 13.8 us -> none  [the longest x1 10.7 us: shards(): lax.all_to_all((spectra * input_gain).astype(jnp.bfloat16), 'gx', split_a...]
  transfers between devices with their start and end apart: 2 -> 5, of which waited for: 2 -> 4; matrix products, arithmetic and copies ran while one was open for 8% -> 2% of each run, Pallas kernels for 0% -> 27%
where the time goes in v1:
time: 434 us; the launch traced here: 432 us
  blocking collectives  150 us (35%)
  Pallas kernels  148 us (34%)
  waiting for transfers between devices  91.5 us (21%)
  starting transfers between devices  26.8 us (6%)
  local copies, waits for them, and re-layouts  9.18 us (2%)
  other arithmetic  5.47 us (1%)
    all_to_all x2, blocking collectives, exchange(): return lax.all_to_all(array, 'gx', split_axis=0, concat_axis=0, tiled=True)  150 us
    all_to_all x5, waiting for transfers between devices, exchange(): return lax.all_to_all(array, 'gx', split_axis=0, concat_axis=0, tiled=True)  91.5 us
    pallas_call x2, Pallas kernels, spectra_of(): pl.pallas_call(functools.partial(spectra_kernel, counts), out_shape=[jax....  69.2 us
    pallas_call x3, Pallas kernels, gram_of(): pl.pallas_call(functools.partial(gram_kernel, len(arrays)), out_shape=jax...  28.1 us
    all_to_all x5, starting transfers between devices, exchange(): return lax.all_to_all(array, 'gx', split_axis=0, concat_axis=0, tiled=True)  26.8 us
    pallas_call x3, Pallas kernels, beams_of(): pl.pallas_call(functools.partial(beams_kernel, len(arrays)), out_shape=ja...  19.3 us
    pallas_call x1, Pallas kernels, weights_of(): pl.pallas_call(weights_kernel, out_shape=jax.ShapeDtypeStruct((kept.shape...  18.7 us
    pallas_call x1, Pallas kernels, series_of(): pl.pallas_call(functools.partial(series_kernel, len(arrays)), out_shape=j...  12.8 us
  transfers between devices with their start and end apart: 5, of which 4 were waited for; matrix products, arithmetic and copies ran while one was open for 2% of the time, Pallas kernels for 27%

profile of v1, /device:TPU:13, one launch (start us, length us, event | category | flops | bytes accessed | tf_op | source)
XLA Modules:
  0.0 431.8 jit_solution(4751540907812904300)
XLA Ops:
  0.6 0.0 copy-start
  0.6 0.7 fusion.21.taper_ref
  1.3 1.6 fusion.12
  3.0 0.4 copy.23
  3.4 0.9 convert_element_type.43.analysis_ref
  4.3 19.1 %spectra.2 = bf16[16,12,2,16,256]{4,3,2,1,0:T(8,128)(2,1)} custom-call(s32[16]{0:T(128)} %bitcast.5, bf16[2,64,67328]{2,1,0:T(8,128)(2,1)} %samples_ref.3, f32[8,256]{1,0:T(8,128)} %fusion.21.taper_ref, bf16[384,512]{1,0:T(8,128)(2,1)} %convert_element_type.43.analysis_ref), custom_call_target="tpu_custom_call" | custom-call | flops 1610612736 | bytes 7454720 | tf_op jit(solution)/shard_map/spectra/pallas_call | solution.py:130
  23.4 0.0 copy-start.10
  23.4 0.0 copy-start.8
  23.4 6.7 %all-to-all-start = ((bf16[16,12,2,16,256]{4,3,2,1,0:T(8,128)(2,1)}), bf16[16,12,2,16,256]{4,3,2,1,0:T(8,128)(2,1)}, u32[]{:S(2)}, u32[]{:S(2)}) async-start(bf16[16,12,2,16,256]{4,3,2,1,0:T(8,128)(2,1)} %spectra.2), calls=%async_computation | async-start | bytes 6291456 | tf_op jit(solution)/shard_map/all_to_all | solution.py:396
  30.1 0.0 copy-done.10
  30.1 0.6 dynamic_slice.10.flags_ref
  30.7 0.0 copy-done.8
  30.7 0.1 mul.242
  30.8 0.1 copy.24
  30.9 0.9 fusion.13
  31.9 0.1 copy.25
  32.0 0.1 reshape.238
  32.1 0.1 copy.26
  32.2 0.1 reshape.239
  32.3 0.1 copy.27
  32.4 0.1 reshape.240
  32.5 0.0 copy-start.7
  32.5 0.7 copy-done.7
  33.3 50.1 %spectra.3 = (bf16[16,4,2,48,256]{4,3,2,1,0:T(8,128)(2,1)}, bf16[16,4,2,48,256]{4,3,2,1,0:T(8,128)(2,1)}, bf16[16,4,2,48,256]{4,3,2,1,0:T(8,128)(2,1)}) custom-call(s32[48]{0:T(128)} %dynamic_slice.10.flags_ref, bf16[2,64,67328]{2,1,0:T(8,128)(2,1)} %samples_ref.3, f32[8,256]{1,0:T(8,128)} %fusion.21.taper_ref, bf16[384,512]{1,0:T(8,128)(2,1)} %copy-done.7), custom_call_target="tpu_custom_call" | custom-call | flops 4831838208 | bytes 22364160 | tf_op jit(solution)/shard_map/spectra/pallas_call | solution.py:130
  83.4 16.7 %all-to-all-done.refs_0_ = bf16[16,12,2,16,256]{4,3,2,1,0:T(8,128)(2,1)} async-done(((bf16[16,12,2,16,256]{4,3,2,1,0:T(8,128)(2,1)}), bf16[16,12,2,16,256]{4,3,2,1,0:T(8,128)(2,1)}, u32[]{:S(2)}, u32[]{:S(2)}) %all-to-all-start) | async-done | bytes 3145760 | tf_op jit(solution)/shard_map/all_to_all | solution.py:396
  100.1 0.0 copy-start.6
  100.1 75.0 %all_to_all.35.refs_1_ = bf16[16,4,2,48,256]{4,3,2,1,0:T(8,128)(2,1)} all-to-all(bf16[16,4,2,48,256]{4,3,2,1,0:T(8,128)(2,1)} %get-tuple-element.5), channel_id=1, replica_groups=mesh['groups'=2,'gx'=16] {'gx'}, dimensions={0} | all-to-all | bytes 6291456 | tf_op jit(solution)/shard_map/all_to_all | solution.py:396
  175.2 0.0 copy-done.6
  175.2 74.9 %all_to_all.36.refs_1_ = bf16[16,4,2,48,256]{4,3,2,1,0:T(8,128)(2,1)} all-to-all(bf16[16,4,2,48,256]{4,3,2,1,0:T(8,128)(2,1)S(1)} %copy-done.6), channel_id=1, replica_groups=mesh['groups'=2,'gx'=16] {'gx'}, dimensions={0} | all-to-all | bytes 6291456 | tf_op jit(solution)/shard_map/all_to_all | solution.py:396
  250.0 0.0 copy-start.9
  250.0 5.3 %all-to-all-start.2 = ((bf16[16,4,2,48,256]{4,3,2,1,0:T(8,128)(2,1)}), bf16[16,4,2,48,256]{4,3,2,1,0:T(8,128)(2,1)}, u32[]{:S(2)}, u32[]{:S(2)}) async-start(bf16[16,4,2,48,256]{4,3,2,1,0:T(8,128)(2,1)} %get-tuple-element.6), calls=%async_computation.2 | async-start | bytes 6291456 | tf_op jit(solution)/shard_map/all_to_all | solution.py:396
  255.4 0.0 copy-done.9
  255.4 0.0 copy-done
  255.4 0.0 copy-start.2
  255.4 1.1 gather_fusion
  256.5 0.0 copy-done.2
  256.5 1.9 gather_fusion.1
  258.5 0.6 and_select_fusion.1
  259.1 0.5 fusion.32
  259.6 1.7 copy.28.refs_3_
  261.2 1.1 broadcast_select_fusion.delays_ref
  262.4 18.7 %weights.1.refs_2_ = bf16[12,2,256,1024]{3,2,1,0:T(8,128)(2,1)} custom-call(s32[12]{0:T(128)} %get-tuple-element.9.kept_ref, f32[256,1024]{1,0:T(8,128)} %broadcast_select_fusion.delays_ref), custom_call_target="tpu_custom_call" | custom-call | flops 125829120 | bytes 12582912 | tf_op jit(solution)/shard_map/weights/pallas_call | solution.py:188
  281.1 6.4 %beams.3 = bf16[16,4,2,16,256]{4,3,2,1,0:T(8,128)(2,1)} custom-call(bf16[16,12,2,16,256]{4,3,2,1,0:T(8,128)(2,1)} %all-to-all-done.refs_0_, bf16[16,4,2,48,256]{4,3,2,1,0:T(8,128)(2,1)} %all_to_all.36.refs_1_, bf16[12,2,256,1024]{3,2,1,0:T(8,128)(2,1)} %weights.1.refs_2_, f32[12,256,2]{2,1,0:T(8,128)} %copy.28.refs_3_), custom_call_target="tpu_custom_call" | custom-call | flops 2147483648 | bytes 8388608 | tf_op jit(solution)/shard_map/beams/pallas_call | solution.py:259
  287.5 37.9 %all-to-all-done.2.refs_1_ = bf16[16,4,2,48,256]{4,3,2,1,0:T(8,128)(2,1)} async-done(((bf16[16,4,2,48,256]{4,3,2,1,0:T(8,128)(2,1)}), bf16[16,4,2,48,256]{4,3,2,1,0:T(8,128)(2,1)}, u32[]{:S(2)}, u32[]{:S(2)}) %all-to-all-start.2) | async-done | bytes 3145760 | tf_op jit(solution)/shard_map/all_to_all | solution.py:396
  325.4 4.9 %all-to-all-start.4 = ((bf16[16,4,2,16,256]{4,3,2,1,0:T(8,128)(2,1)}), bf16[16,4,2,16,256]{4,3,2,1,0:T(8,128)(2,1)S(1)}, u32[]{:S(2)}, u32[]{:S(2)}) async-start(bf16[16,4,2,16,256]{4,3,2,1,0:T(8,128)(2,1)} %beams.3), calls=%async_computation.4 | async-start | bytes 2097152 | tf_op jit(solution)/shard_map/all_to_all | solution.py:396
  330.3 6.4 %beams.4 = bf16[16,4,2,16,256]{4,3,2,1,0:T(8,128)(2,1)} custom-call(bf16[16,12,2,16,256]{4,3,2,1,0:T(8,128)(2,1)} %all-to-all-done.refs_0_, bf16[16,4,2,48,256]{4,3,2,1,0:T(8,128)(2,1)} %all-to-all-done.2.refs_1_, bf16[12,2,256,1024]{3,2,1,0:T(8,128)(2,1)} %weights.1.refs_2_, f32[12,256,2]{2,1,0:T(8,128)} %copy.28.refs_3_), custom_call_target="tpu_custom_call" | custom-call | flops 2147483648 | bytes 8388608 | tf_op jit(solution)/shard_map/beams/pallas_call | solution.py:259
  336.7 18.5 %all-to-all-done.4.refs_0_ = bf16[16,4,2,16,256]{4,3,2,1,0:T(8,128)(2,1)S(1)} async-done(((bf16[16,4,2,16,256]{4,3,2,1,0:T(8,128)(2,1)}), bf16[16,4,2,16,256]{4,3,2,1,0:T(8,128)(2,1)S(1)}, u32[]{:S(2)}, u32[]{:S(2)}) %all-to-all-start.4) | async-done | bytes 1048608 | tf_op jit(solution)/shard_map/all_to_all | solution.py:396
  355.1 0.0 copy-start.3
  355.1 4.9 %all-to-all-start.5 = ((bf16[16,4,2,16,256]{4,3,2,1,0:T(8,128)(2,1)}), bf16[16,4,2,16,256]{4,3,2,1,0:T(8,128)(2,1)S(1)}, u32[]{:S(2)}, u32[]{:S(2)}) async-start(bf16[16,4,2,16,256]{4,3,2,1,0:T(8,128)(2,1)} %beams.4), calls=%async_computation.5 | async-start | bytes 2097152 | tf_op jit(solution)/shard_map/all_to_all | solution.py:396
  360.1 6.4 %beams.5 = bf16[16,4,2,16,256]{4,3,2,1,0:T(8,128)(2,1)} custom-call(bf16[16,12,2,16,256]{4,3,2,1,0:T(8,128)(2,1)} %all-to-all-done.refs_0_, bf16[16,4,2,48,256]{4,3,2,1,0:T(8,128)(2,1)} %all_to_all.35.refs_1_, bf16[12,2,256,1024]{3,2,1,0:T(8,128)(2,1)} %weights.1.refs_2_, f32[12,256,2]{2,1,0:T(8,128)} %copy.28.refs_3_), custom_call_target="tpu_custom_call" | custom-call | flops 2147483648 | bytes 8388608 | tf_op jit(solution)/shard_map/beams/pallas_call | solution.py:259
  366.5 0.0 copy-done.3
  366.5 18.4 %all-to-all-done.5.refs_1_ = bf16[16,4,2,16,256]{4,3,2,1,0:T(8,128)(2,1)S(1)} async-done(((bf16[16,4,2,16,256]{4,3,2,1,0:T(8,128)(2,1)}), bf16[16,4,2,16,256]{4,3,2,1,0:T(8,128)(2,1)S(1)}, u32[]{:S(2)}, u32[]{:S(2)}) %all-to-all-start.5) | async-done | bytes 1048608 | tf_op jit(solution)/shard_map/all_to_all | solution.py:396
  385.0 0.0 copy-start.4
  385.0 4.9 %all-to-all-start.6 = ((bf16[16,4,2,16,256]{4,3,2,1,0:T(8,128)(2,1)}), bf16[16,4,2,16,256]{4,3,2,1,0:T(8,128)(2,1)S(1)}, u32[]{:S(2)}, u32[]{:S(2)}) async-start(bf16[16,4,2,16,256]{4,3,2,1,0:T(8,128)(2,1)} %beams.5), calls=%async_computation.6 | async-start | bytes 2097152 | tf_op jit(solution)/shard_map/all_to_all | solution.py:396
  389.9 9.3 %gram.3.refs_2_ = bf16[12,1024,1024]{2,1,0:T(8,128)(2,1)} custom-call(bf16[16,12,2,16,256]{4,3,2,1,0:T(8,128)(2,1)} %all-to-all-done.refs_0_, bf16[16,4,2,48,256]{4,3,2,1,0:T(8,128)(2,1)} %all_to_all.36.refs_1_), custom_call_target="tpu_custom_call" | custom-call | flops 5368709120 | bytes 12582912 | tf_op jit(solution)/shard_map/gram/pallas_call | solution.py:318
  399.2 0.0 copy-done.4
  399.2 9.3 %gram.4.refs_2_ = bf16[12,1024,1024]{2,1,0:T(8,128)(2,1)} custom-call(bf16[16,12,2,16,256]{4,3,2,1,0:T(8,128)(2,1)} %all-to-all-done.refs_0_, bf16[16,4,2,48,256]{4,3,2,1,0:T(8,128)(2,1)} %all-to-all-done.2.refs_1_, bf16[12,1024,1024]{2,1,0:T(8,128)(2,1)} %gram.3.refs_2_), custom_call_target="tpu_custom_call", output_to_operand_aliasing={{}: (2, {})} | custom-call | flops 5368709120 | bytes 12582912 | tf_op jit(solution)/shard_map/gram/pallas_call | solution.py:318
  408.6 0.0 copy-start.1
  408.6 9.4 %gram.5 = bf16[12,1024,1024]{2,1,0:T(8,128)(2,1)} custom-call(bf16[16,12,2,16,256]{4,3,2,1,0:T(8,128)(2,1)} %all-to-all-done.refs_0_, bf16[16,4,2,48,256]{4,3,2,1,0:T(8,128)(2,1)} %all_to_all.35.refs_1_, bf16[12,1024,1024]{2,1,0:T(8,128)(2,1)} %gram.4.refs_2_), custom_call_target="tpu_custom_call", output_to_operand_aliasing={{}: (2, {})} | custom-call | flops 5368709120 | bytes 12582912 | tf_op jit(solution)/shard_map/gram/pallas_call | solution.py:318
  418.0 0.0 all-to-all-done.6.refs_2_
  418.0 0.0 copy-start.5
  418.0 1.0 copy-done.5
  419.0 12.8 %series.1 = f32[2,16,256,256]{3,2,1,0:T(8,128)} custom-call(bf16[16,4,2,16,256]{4,3,2,1,0:T(8,128)(2,1)} %copy-done.3, bf16[16,4,2,16,256]{4,3,2,1,0:T(8,128)(2,1)} %copy-done.4, bf16[16,4,2,16,256]{4,3,2,1,0:T(8,128)(2,1)} %copy-done.5, bf16[384,512]{1,0:T(8,128)(2,1)} %copy-done.7), custom_call_target="tpu_custom_call" | custom-call | flops 1610612736 | bytes 11534336 | tf_op jit(solution)/shard_map/series/pallas_call | solution.py:377
  431.8 0.0 copy-done.1
  (11 shorter events, 0.2 us)
Async XLA Ops:
  0.6 254.8 %copy-start = (f32[256,1024]{1,0:T(8,128)S(1)}, f32[256,1024]{1,0:T(8,128)}, u32[]{:S(2)}) copy-start(f32[256,1024]{1,0:T(8,128)} %param.11) | copy-start | bytes 3145732
  23.4 6.7 %copy-start.10 = (s32[64]{0:T(128)S(1)}, s32[64]{0:T(128)}, u32[]{:S(2)}) copy-start(s32[64]{0:T(128)} %param.7) | copy-start | bytes 772
  23.4 7.3 %copy-start.8 = (s32[192]{0:T(256)S(1)}, s32[192]{0:T(256)}, u32[]{:S(2)}) copy-start(s32[192]{0:T(256)} %param.8) | copy-start | bytes 2308
  23.4 76.7 %all-to-all-start = ((bf16[16,12,2,16,256]{4,3,2,1,0:T(8,128)(2,1)}), bf16[16,12,2,16,256]{4,3,2,1,0:T(8,128)(2,1)}, u32[]{:S(2)}, u32[]{:S(2)}) async-start(bf16[16,12,2,16,256]{4,3,2,1,0:T(8,128)(2,1)} %spectra.2), calls=%async_computation | async-start | bytes 6291456 | tf_op jit(solution)/shard_map/all_to_all | solution.py:396
  32.5 0.8 copy-start.7
  100.1 75.1 %copy-start.6 = (bf16[16,4,2,48,256]{4,3,2,1,0:T(8,128)(2,1)S(1)}, bf16[16,4,2,48,256]{4,3,2,1,0:T(8,128)(2,1)}, u32[]{:S(2)}) copy-start(bf16[16,4,2,48,256]{4,3,2,1,0:T(8,128)(2,1)} %get-tuple-element.7) | copy-start | bytes 9437188
  250.0 5.3 %copy-start.9 = (s32[256]{0:T(256)S(1)}, s32[256]{0:T(256)}, u32[]{:S(2)}) copy-start(s32[256]{0:T(256)} %param.9) | copy-start | bytes 3076
  250.0 75.3 %all-to-all-start.2 = ((bf16[16,4,2,48,256]{4,3,2,1,0:T(8,128)(2,1)}), bf16[16,4,2,48,256]{4,3,2,1,0:T(8,128)(2,1)}, u32[]{:S(2)}, u32[]{:S(2)}) async-start(bf16[16,4,2,48,256]{4,3,2,1,0:T(8,128)(2,1)} %get-tuple-element.6), calls=%async_computation.2 | async-start | bytes 6291456 | tf_op jit(solution)/shard_map/all_to_all | solution.py:396
  255.4 1.1 copy-start.2
  325.4 29.8 %all-to-all-start.4 = ((bf16[16,4,2,16,256]{4,3,2,1,0:T(8,128)(2,1)}), bf16[16,4,2,16,256]{4,3,2,1,0:T(8,128)(2,1)S(1)}, u32[]{:S(2)}, u32[]{:S(2)}) async-start(bf16[16,4,2,16,256]{4,3,2,1,0:T(8,128)(2,1)} %beams.3), calls=%async_computation.4 | async-start | bytes 2097152 | tf_op jit(solution)/shard_map/all_to_all | solution.py:396
  355.1 11.4 %copy-start.3 = (bf16[16,4,2,16,256]{4,3,2,1,0:T(8,128)(2,1)}, bf16[16,4,2,16,256]{4,3,2,1,0:T(8,128)(2,1)S(1)}, u32[]{:S(2)}) copy-start(bf16[16,4,2,16,256]{4,3,2,1,0:T(8,128)(2,1)S(1)} %all-to-all-done.4.refs_0_) | copy-start | bytes 3145732
  355.1 29.8 %all-to-all-start.5 = ((bf16[16,4,2,16,256]{4,3,2,1,0:T(8,128)(2,1)}), bf16[16,4,2,16,256]{4,3,2,1,0:T(8,128)(2,1)S(1)}, u32[]{:S(2)}, u32[]{:S(2)}) async-start(bf16[16,4,2,16,256]{4,3,2,1,0:T(8,128)(2,1)} %beams.4), calls=%async_computation.5 | async-start | bytes 2097152 | tf_op jit(solution)/shard_map/all_to_all | solution.py:396
  385.0 14.3 %copy-start.4 = (bf16[16,4,2,16,256]{4,3,2,1,0:T(8,128)(2,1)}, bf16[16,4,2,16,256]{4,3,2,1,0:T(8,128)(2,1)S(1)}, u32[]{:S(2)}) copy-start(bf16[16,4,2,16,256]{4,3,2,1,0:T(8,128)(2,1)S(1)} %all-to-all-done.5.refs_1_) | copy-start | bytes 3145732
  385.0 33.0 %all-to-all-start.6 = ((bf16[16,4,2,16,256]{4,3,2,1,0:T(8,128)(2,1)}), bf16[16,4,2,16,256]{4,3,2,1,0:T(8,128)(2,1)S(1)}, u32[]{:S(2)}, u32[]{:S(2)}) async-start(bf16[16,4,2,16,256]{4,3,2,1,0:T(8,128)(2,1)} %beams.5), calls=%async_computation.6 | async-start | bytes 2097152 | tf_op jit(solution)/shard_map/all_to_all | solution.py:396
  408.6 23.2 %copy-start.1 = (f32[256,1024]{1,0:T(8,128)S(1)}, f32[256,1024]{1,0:T(8,128)}, u32[]{:S(2)}) copy-start(f32[256,1024]{1,0:T(8,128)} %param.11) | copy-start | bytes 3145732
  418.0 1.0 copy-start.5

commit v2 on v1

v2 whole, which is shorter than its diff:
```python
import functools
import math

import jax
import jax.numpy as jnp
import numpy as np
from jax import lax
from jax.experimental import pallas as pl
from jax.experimental.pallas import tpu as pltpu
from jax.sharding import PartitionSpec as P

POINTS = 256
TAPS = 8
ROWS = 16
EACH = 3
SHARE = 4
APART = 12
LEAD = 1
STRETCH = 16
F32 = jnp.float32
BF16 = jnp.bfloat16
VMEM = 60 * 1024 * 1024
BEAMS_VMEM = VMEM


def fit_tables():
    spots = np.cos(np.pi * (np.arange(4000) + 0.5) / 4000) * 0.125 + 0.125
    powers = np.stack([spots ** (2 * k) for k in range(6)], 1)
    sine = np.linalg.lstsq(powers[:, :5] * spots[:, None], np.sin(2 * np.pi * spots), rcond=None)[0]
    cosine = np.linalg.lstsq(powers, np.cos(2 * np.pi * spots), rcond=None)[0]
    return [float(v) for v in sine], [float(v) for v in cosine]


SINE_FIT, COSINE_FIT = fit_tables()


def prototype_taper(tap_count, point_count):
    spots = np.arange(tap_count * point_count, dtype=np.float64)
    length = float(tap_count * point_count)
    shaped = np.sinc((spots - length / 2.0 + 0.5) / point_count) * (
        0.5 - 0.5 * np.cos(2.0 * math.pi * (spots + 0.5) / length)
    )
    return shaped.reshape(tap_count, point_count).astype(np.float32)


def dft_tables(kept, point_count):
    spots = jnp.arange(point_count, dtype=jnp.int32)
    turns = kept[:, None] * spots[None, :] % point_count
    angle = turns.astype(F32) * (2.0 * math.pi / point_count)
    scale = 1.0 / math.sqrt(point_count)
    return jnp.cos(angle) * scale, jnp.sin(angle) * scale


def rotation(dm_rows, kept):
    squares = kept * kept % 4096
    turns = squares[:, None] * dm_rows[None, :] % 4096
    angle = turns.astype(F32) * (2.0 * math.pi / 4096.0)
    return (jnp.cos(angle), jnp.sin(angle))


def spectra_kernel(first, counts, *refs):
    me_ref, flags_ref, samples_ref, taper_ref, analysis_ref = refs[:5]
    out_refs, (frames_ref, wide_ref) = refs[5:-2], refs[-2:]
    span = frames_ref.shape[1] // ROWS
    co_rows = analysis_ref.shape[0]
    step = pl.program_id(0) + first
    group, begin = step // 2, (step % 2) * span

    def form_frames(stretch, carry):
        at = stretch * STRETCH
        for x in range(2):
            for half in range(POINTS // 128):
                lanes = pl.ds(half * 128, 128)
                tapers = [
                    jnp.broadcast_to(taper_ref[pl.ds(t, 1), lanes], (ROWS, 128)) for t in range(TAPS)
                ]
                tiles = []
                for k in range(STRETCH + TAPS - 1):
                    spot = pl.multiple_of((begin + at + k) * POINTS + half * 128, 128)
                    tiles.append(samples_ref[x, :, pl.ds(spot, 128)].astype(F32))
                for s in range(STRETCH):
                    total = tiles[s] * tapers[0]
                    for t in range(1, TAPS):
                        total = total + tiles[s + t] * tapers[t]
                    row = pl.multiple_of((at + s) * ROWS, ROWS)
                    frames_ref[x * (POINTS // 128) + half, pl.ds(row, ROWS), :] = total
        return carry

    lax.fori_loop(0, span // STRETCH, form_frames, 0)

    def transform(pair, carry):
        frame = jnp.concatenate(
            [
                jnp.concatenate(
                    [
                        frames_ref[k, pl.ds(2 * pair + i, span, stride=ROWS), :].astype(BF16)
                        for k in range(2 * POINTS // 128)
                    ],
                    axis=1,
                )
                for i in range(2)
            ],
            axis=0,
        )
        product = lax.dot_general(
            analysis_ref[...], frame, (((1,), (1,)), ((), ())), preferred_element_type=F32
        )
        for i in range(2):
            gain = flags_ref[group * ROWS + 2 * pair + i].astype(F32)
            wide_ref[pl.ds(2 * pair + i, co_rows, stride=ROWS), :] = (
                product[:, i * span : (i + 1) * span] * gain
            )
        return carry

    lax.fori_loop(0, ROWS // 2, transform, 0, unroll=4)

    def send(out, place, row):
        out[place] = wide_ref[pl.ds(pl.multiple_of(row * ROWS, ROWS), ROWS), :].astype(BF16)

    count, gx_count = counts[0], out_refs[0].shape[0]

    chan_dev = count + counts[1]

    def send_rows(d, carry):
        for k in range(2 * count):
            send(out_refs[0], (d, k // 2, k % 2), d * 2 * chan_dev + k)
        return carry

    lax.fori_loop(0, gx_count, send_rows, 0)
    for k, out in enumerate(out_refs[1:]):
        for slot in range(2):
            owner = me_ref[0] ^ k ^ (slot * (gx_count // 2))
            for j in range(2 * counts[1]):
                send(out, (slot, j // 2, j % 2), (owner * chan_dev + count) * 2 + j)


def spectra_of(samples, flags, me, taper, analysis, gx_count, counts, first, steps, span):
    co_rows = analysis.shape[0]
    rows = steps * ROWS
    out_shape = [jax.ShapeDtypeStruct((gx_count, counts[0], 2, rows, span), BF16)]
    out_specs = [pl.BlockSpec((gx_count, counts[0], 2, ROWS, span), lambda g: (0, 0, 0, g, 0))]
    if counts[1]:
        half = gx_count // 2
        shape = (2, counts[1], 2, rows, span)
        out_shape += [jax.ShapeDtypeStruct(shape, BF16)] * half
        out_specs += [pl.BlockSpec((2, counts[1], 2, ROWS, span), lambda g: (0, 0, 0, g, 0))] * half
    width = samples.shape[2] if steps > 1 or first else (span + TAPS - 1) * POINTS
    return pl.pallas_call(
        functools.partial(spectra_kernel, first, counts),
        out_shape=out_shape,
        grid=(steps,),
        in_specs=[
            pl.BlockSpec(memory_space=pltpu.SMEM),
            pl.BlockSpec(memory_space=pltpu.SMEM),
            pl.BlockSpec((2, ROWS, width), lambda g: (0, (g + first) // 2, 0)),
            pl.BlockSpec((TAPS, POINTS), lambda g: (0, 0)),
            pl.BlockSpec((co_rows, 2 * POINTS), lambda g: (0, 0)),
        ],
        out_specs=out_specs,
        scratch_shapes=[
            pltpu.VMEM((2 * POINTS // 128, span * ROWS, 128), F32),
            pltpu.VMEM((co_rows * ROWS, span), F32),
        ],
        compiler_params=pltpu.CompilerParams(vmem_limit_bytes=VMEM),
        cost_estimate=pl.CostEstimate(
            flops=steps * ROWS * span * co_rows * 4 * POINTS * 3,
            bytes_accessed=steps * ROWS * (samples.shape[2] * 4 + co_rows * span * 2),
            transcendentals=0,
        ),
        name="spectra",
    )(me, flags, samples, taper, analysis)


def weights_kernel(kept_ref, delays_ref, out_ref):
    scale = kept_ref[pl.program_id(0)].astype(F32) * (1.0 / POINTS)
    input_scale = 1.0 / math.sqrt(delays_ref.shape[1])

    def rows(step, carry):
        at = pl.ds(pl.multiple_of(step * 16, 16), 16)
        turns = delays_ref[at, :] * scale
        turns = turns - jnp.floor(turns + 0.5)
        size = jnp.abs(turns)
        near = jnp.minimum(size, 0.5 - size)
        square = near * near
        sine = square * SINE_FIT[-1] + SINE_FIT[-2]
        for value in SINE_FIT[-3::-1]:
            sine = sine * square + value
        sine = sine * (near * input_scale)
        cosine = square * COSINE_FIT[-1] + COSINE_FIT[-2]
        for value in COSINE_FIT[-3::-1]:
            cosine = cosine * square + value
        cosine = cosine * input_scale
        out_ref[0, 0, at, :] = jnp.where(size > 0.25, -cosine, cosine).astype(BF16)
        out_ref[0, 1, at, :] = jnp.where(turns > 0.0, -sine, sine).astype(BF16)
        return carry

    lax.fori_loop(0, delays_ref.shape[0] // 16, rows, 0)


def weights_of(kept, delays):
    beams, inputs = delays.shape
    return pl.pallas_call(
        weights_kernel,
        out_shape=jax.ShapeDtypeStruct((kept.shape[0], 2, beams, inputs), BF16),
        grid=(kept.shape[0],),
        in_specs=[
            pl.BlockSpec(memory_space=pltpu.SMEM),
            pl.BlockSpec((beams, inputs), lambda c: (0, 0)),
        ],
        out_specs=pl.BlockSpec((1, 2, beams, inputs), lambda c: (c, 0, 0, 0)),
        compiler_params=pltpu.CompilerParams(vmem_limit_bytes=VMEM),
        cost_estimate=pl.CostEstimate(
            flops=kept.shape[0] * beams * inputs * 40,
            bytes_accessed=kept.shape[0] * beams * inputs * 4,
            transcendentals=0,
        ),
        name="weights",
    )(kept, delays)


def assemble(me_ref, lead, rest, c, joined_ref):
    sources, _, _, lead_rows, span = lead.shape
    ahead = lead_rows // ROWS
    steps = rest[-1].shape[-2] // ROWS + ahead
    share = steps // 2 * ROWS
    half = sources // 2

    def place(src, o, step, block):
        row = src * share + step // 2 * ROWS
        if not isinstance(row, int):
            row = pl.multiple_of(row, ROWS)
        joined_ref[o, pl.ds(row, ROWS), pl.ds(step % 2 * span, span)] = block

    for k in range(sources):
        for o in range(2):
            for step in range(ahead):
                place(k, o, step, lead[k, c, o, pl.ds(step * ROWS, ROWS), :])
            for step in range(ahead, steps):
                rows = pl.ds((step - ahead) * ROWS, ROWS)
                if len(rest) == 1:
                    place(k, o, step, rest[0][k, c, o, rows, :])
                elif k < half:
                    place(me_ref[0] ^ k, o, step, rest[k][0, c, o, rows, :])
                else:
                    place(me_ref[0] ^ k, o, step, rest[half][k - half, c, o, rows, :])


def beams_kernel(part_count, me_ref, lead, *refs):
    rest, (weights_ref, turn_ref) = refs[:part_count], refs[part_count : part_count + 2]
    each, _, beams, inputs = weights_ref.shape
    out_ref, joined_refs = refs[-1 - each], refs[-each:]
    for c in range(each):
        assemble(me_ref, lead, rest, c, joined_refs[c])
        weights = weights_ref[c].reshape(2 * beams, inputs)
        products = [jnp.dot(weights, joined_refs[c][o], preferred_element_type=F32) for o in range(2)]
        real_part = (products[0][:beams] - products[1][beams:]).astype(BF16).astype(F32)
        imag_part = (products[1][:beams] + products[0][beams:]).astype(BF16).astype(F32)
        cosine, sine = turn_ref[c, :, 0:1], turn_ref[c, :, 1:2]
        turned = [
            (real_part * cosine + imag_part * sine).astype(BF16),
            (imag_part * cosine - real_part * sine).astype(BF16),
        ]
        for x in range(2):
            if len(out_ref.shape) == 5:
                shape = (out_ref.shape[0],) + out_ref.shape[3:]
                out_ref[:, c, x] = turned[x].reshape(shape)
            else:
                out_ref[c, x] = turned[x]


def part_specs(lead, rest, first, at, each):
    specs = [
        pl.BlockSpec(memory_space=pltpu.SMEM),
        pl.BlockSpec((lead.shape[0], each) + lead.shape[2:], lambda c: (0, c + first // each, 0, 0, 0)),
    ]
    for a in rest[:-1]:
        specs.append(pl.BlockSpec((1, each) + a.shape[2:], lambda c: (0, c + at // each, 0, 0, 0)))
    far = rest[-1]
    specs.append(pl.BlockSpec((far.shape[0], each) + far.shape[2:], lambda c: (0, c, 0, 0, 0)))
    return specs


def beams_of(me, lead, rest, weights, turns, first, at, count, held):
    channels, _, beams, inputs = weights.shape
    gx_count, span = lead.shape[0], lead.shape[4]
    spectra_all = 2 * span
    beam_dev = beams // gx_count
    each = EACH if count % EACH == 0 and first % EACH == 0 and at % EACH == 0 else 1
    start = first // each
    if beam_dev % 16 == 0:
        out_shape = (gx_count, channels, 2, beam_dev, spectra_all)
        out_spec = pl.BlockSpec(
            (gx_count, each, 2, beam_dev, spectra_all), lambda c: (0, c + start, 0, 0, 0)
        )
    else:
        out_shape = (channels, 2, beams, spectra_all)
        out_spec = pl.BlockSpec((each, 2, beams, spectra_all), lambda c: (c + start, 0, 0, 0))
    more = [] if held is None else [held]
    return pl.pallas_call(
        functools.partial(beams_kernel, len(rest)),
        out_shape=jax.ShapeDtypeStruct(out_shape, BF16),
        grid=(count // each,),
        in_specs=part_specs(lead, rest, first, at, each)
        + [
            pl.BlockSpec((each, 2, beams, inputs), lambda c: (c + start, 0, 0, 0)),
            pl.BlockSpec((each, beams, 2), lambda c: (c + start, 0, 0)),
        ]
        + [pl.BlockSpec(memory_space=pl.ANY)] * len(more),
        out_specs=out_spec,
        scratch_shapes=[pltpu.VMEM((2, inputs, spectra_all), BF16)] * each,
        input_output_aliases={4 + len(rest): 0} if more else {},
        compiler_params=pltpu.CompilerParams(vmem_limit_bytes=BEAMS_VMEM),
        cost_estimate=pl.CostEstimate(
            flops=count * beams * inputs * spectra_all * 8,
            bytes_accessed=count * inputs * (spectra_all * 4 + beams * 4),
            transcendentals=0,
        ),
        name="beams",
    )(me, lead, *rest, weights, turns, *more)


def gram_kernel(part_count, me_ref, lead, *refs):
    (out_ref, joined_ref) = refs[-2:]
    rest = refs[:part_count]
    assemble(me_ref, lead, rest, 0, joined_ref)
    inputs, spectra_all = joined_ref.shape[1:]
    side = 256
    scale = 1.0 / spectra_all
    contract = (((1,), (1,)), ((), ()))

    def product(left, right, rows, columns):
        return lax.dot_general(
            joined_ref[left, rows], joined_ref[right, columns], contract, preferred_element_type=F32
        )

    for j in range(inputs // side):
        columns = slice(j * side, (j + 1) * side)
        above = slice(0, (j + 1) * side)
        below = slice(j * side, inputs)
        real_sum = product(0, 0, above, columns) + product(1, 1, above, columns)
        mixed = product(1, 0, below, columns) - product(0, 1, below, columns)
        if j:
            out_ref[0, : j * side, columns] = (real_sum[: j * side] * scale).astype(BF16)
        upper = lax.broadcasted_iota(jnp.int32, (side, side), 0) <= lax.broadcasted_iota(
            jnp.int32, (side, side), 1
        )
        out_ref[0, columns, columns] = (
            jnp.where(upper, real_sum[j * side :], mixed[:side]) * scale
        ).astype(BF16)
        if (j + 1) * side < inputs:
            out_ref[0, (j + 1) * side :, columns] = (mixed[side:] * scale).astype(BF16)


def gram_of(me, lead, rest, first, at, count, held):
    sources, channels, _, _, span = lead.shape
    inputs = sources * (rest[-1].shape[-2] + lead.shape[3]) // 2
    more = [] if held is None else [held]
    return pl.pallas_call(
        functools.partial(gram_kernel, len(rest)),
        out_shape=jax.ShapeDtypeStruct((channels, inputs, inputs), BF16),
        grid=(count,),
        in_specs=part_specs(lead, rest, first, at, 1) + [pl.BlockSpec(memory_space=pl.ANY)] * len(more),
        out_specs=pl.BlockSpec((1, inputs, inputs), lambda c: (c + first, 0, 0)),
        scratch_shapes=[pltpu.VMEM((2, inputs, 2 * span), BF16)],
        input_output_aliases={2 + len(rest): 0} if more else {},
        compiler_params=pltpu.CompilerParams(vmem_limit_bytes=VMEM),
        cost_estimate=pl.CostEstimate(
            flops=count * inputs * inputs * span * 10,
            bytes_accessed=count * inputs * (span * 8 + inputs * 2),
            transcendentals=0,
        ),
        name="gram",
    )(me, lead, *rest, *more)


def series_kernel(share, part_count, *refs):
    parts, (synthesis_ref, out_ref, wide_ref) = refs[:part_count], refs[part_count:]
    beam_dev, spectra_all = parts[0].shape[3:]
    rows = synthesis_ref.shape[0]
    halves = [slice(k * 128, (k + 1) * 128) for k in range(spectra_all // 128)]

    @pl.when(pl.program_id(0) == 0)
    def _():
        base = 0
        for part in parts:
            each = 2 * part.shape[1]

            def widen_source(d, carry, base=base, part=part, each=each):
                for j in range(each):
                    block = part[d, j // 2, j % 2]
                    row = pl.multiple_of((base + d * each + j) * beam_dev, beam_dev)
                    for k, half in enumerate(halves):
                        wide_ref[k, pl.ds(row, beam_dev), :] = block[:, half].astype(F32)
                return carry

            lax.fori_loop(0, part.shape[0], widen_source, 0)
            base += part.shape[0] * each

    for b in range(share):
        beam = pl.program_id(0) * share + b
        turned = jnp.concatenate(
            [
                wide_ref[k, pl.ds(beam, rows, stride=beam_dev), :].astype(BF16)
                for k in range(len(halves))
            ],
            axis=1,
        )
        product = lax.dot_general(
            turned, synthesis_ref[...], (((0,), (0,)), ((), ())), preferred_element_type=F32
        )
        for o in range(2):
            out_ref[o, b] = product[:, o * POINTS : (o + 1) * POINTS]


def series_of(parts, synthesis):
    beam_dev, spectra_all = parts[0].shape[3:]
    rows = synthesis.shape[0]
    share = SHARE
    return pl.pallas_call(
        functools.partial(series_kernel, share, len(parts)),
        out_shape=jax.ShapeDtypeStruct((2, beam_dev, spectra_all, POINTS), F32),
        grid=(beam_dev // share,),
        in_specs=[pl.BlockSpec(a.shape, lambda b: (0, 0, 0, 0, 0)) for a in parts]
        + [pl.BlockSpec(synthesis.shape, lambda b: (0, 0))],
        out_specs=pl.BlockSpec((2, share, spectra_all, POINTS), lambda b: (0, b, 0, 0)),
        scratch_shapes=[pltpu.VMEM((spectra_all // 128, rows * beam_dev, 128), F32)],
        compiler_params=pltpu.CompilerParams(vmem_limit_bytes=VMEM),
        cost_estimate=pl.CostEstimate(
            flops=2 * beam_dev * rows * spectra_all * 2 * POINTS,
            bytes_accessed=beam_dev * spectra_all * (rows * 2 + POINTS * 8),
            transcendentals=0,
        ),
        name="series",
    )(*parts, synthesis)


def exchange(array):
    return lax.all_to_all(array, "gx", split_axis=0, concat_axis=0, tiled=True)


tie = lax.optimization_barrier


def swap(array, k, count):
    return lax.ppermute(array, "gx", [(i, i ^ k) for i in range(count)])


def shards(samples, flags, kept_channels, beam_order, dm_bins, delays):
    gx_count = lax.axis_size("gx")
    me = lax.axis_index("gx").astype(jnp.int32)
    channels = kept_channels.shape[0]
    chan_dev = channels // gx_count
    span = (samples.shape[2] // POINTS - TAPS + 1) // 2
    steps = samples.shape[1] // ROWS * 2
    ahead = min(LEAD, steps // 2)
    apart = chan_dev // APART if gx_count <= 16 and gx_count & (gx_count - 1) == 0 else 0
    main = chan_dev - apart
    spot = me.reshape(1)

    taper = jnp.asarray(prototype_taper(TAPS, POINTS))
    cosine, sine = dft_tables(kept_channels, POINTS)
    table = jnp.stack(
        [jnp.concatenate([cosine, sine], 1), jnp.concatenate([-sine, cosine], 1)], 1
    ).astype(BF16)
    table_rows = table.reshape(-1, 2 * POINTS)
    (lead,) = spectra_of(
        samples, flags, spot, taper, table_rows, gx_count, (chan_dev, 0), 0, ahead, span
    )
    spot, lead = tie((spot, lead))
    rest, *near = spectra_of(
        samples, flags, spot, taper, table_rows, gx_count, (main, apart), ahead, steps - ahead, span
    )
    lead = exchange(lead)
    my_kept = lax.dynamic_slice_in_dim(kept_channels, me * chan_dev, chan_dev)
    my_kept, rest = tie((my_kept, rest))
    weights = weights_of(my_kept, jnp.take(delays, beam_order, axis=0))
    turns = jnp.stack(rotation(jnp.take(dm_bins, beam_order), my_kept), 2)

    half = gx_count // 2
    cuts = [(0, apart - 1), (apart - 1, apart)] if apart > 1 else [(0, apart)] * (apart > 0)
    relays = []
    if apart:
        near = near[:1] + [swap(near[k], k, gx_count) for k in range(1, half)]
        relays = [jnp.stack([n[1, a:b] for n in near], 0) for a, b in cuts]
    rest, lead = tie((rest, lead))
    rest = exchange(rest)

    beams, visibilities = None, None
    for order, (a, b) in enumerate(cuts):
        if order == len(cuts) - 1:
            if order:
                rest, relays, beams, visibilities = tie((rest, relays, beams, visibilities))
            else:
                rest, relays = tie((rest, relays))
            far = swap(relays[order], half, gx_count)
            beams = beams_of(spot, lead, [rest], weights, turns, 0, 0, main, beams)
        else:
            far = swap(relays[order], half, gx_count)
        parts = near + [far]
        beams = beams_of(spot, lead, parts, weights, turns, main + a, a, b - a, beams)
        if order < len(cuts) - 1:
            visibilities = gram_of(spot, lead, parts, main + a, a, b - a, visibilities)
    if not cuts:
        beams = beams_of(spot, lead, [rest], weights, turns, 0, 0, main, beams)
    spot, beams = tie((spot, beams))
    if beams.ndim == 4:
        beams = beams.reshape(chan_dev, 2, gx_count, -1, beams.shape[3]).transpose(2, 0, 1, 3, 4)
    sums = exchange(beams)
    visibilities = gram_of(spot, lead, [rest], 0, 0, main, visibilities)
    for a, b in cuts[-1:]:
        visibilities = gram_of(spot, lead, parts, main + a, a, b - a, visibilities)
    series = series_of([sums], table_rows)
    return (visibilities, series)


def solution(mesh):
    placed = (P(None, ("groups", "gx"), None), P("gx"), P(), P(), P("groups"), P("groups", None))
    return jax.shard_map(
        shards,
        mesh=mesh,
        in_specs=placed,
        out_specs=(P(("groups", "gx"), None, None), P(None, ("groups", "gx"), None, None)),
        check_vma=False,
    )
```

time: 434 us -> 394 us (0.908)
  blocking collectives: 150 us -> 0 us
  waiting for transfers between devices: 91.5 us -> 220 us
  Pallas kernels: 148 us -> 120 us
  starting transfers between devices: 26.8 us -> 41.3 us
    all_to_all x2 -> x0, blocking collectives: 150 us -> none  [exchange(): return lax.all_to_all(array, 'gx', split_axis=0, concat_axis=0, tiled=True)]
    ppermute x0 -> x8, waiting for transfers between devices: none -> 131 us  [swap(): return lax.ppermute(array, 'gx', [(i, i ^ k) for i in range(count)])]
    pallas_call x9 -> x7, Pallas kernels: 129 us -> 101 us  [the longest x2 46.6 us: spectra_of(): pl.pallas_call(functools.partial(spectra_kernel, first, counts), out_shap...]
    ppermute x0 -> x8, starting transfers between devices: none -> 21.6 us  [swap(): return lax.ppermute(array, 'gx', [(i, i ^ k) for i in range(count)])]
    all_to_all x5 -> x3, starting transfers between devices: 26.8 us -> 19.7 us  [exchange(): return lax.all_to_all(array, 'gx', split_axis=0, concat_axis=0, tiled=True)]
    all_to_all x5 -> x3, waiting for transfers between devices: 91.5 us -> 88.6 us  [exchange(): return lax.all_to_all(array, 'gx', split_axis=0, concat_axis=0, tiled=True)]
  transfers between devices with their start and end apart: 5 -> 11, of which waited for: 4 -> 8; matrix products, arithmetic and copies ran while one was open for 2% -> 2% of each run, Pallas kernels for 27% -> 25%
where the time goes in v2:
time: 394 us; the launch traced here: 393 us
  waiting for transfers between devices  220 us (56%)
  Pallas kernels  120 us (30%)
  starting transfers between devices  41.3 us (10%)
  local copies, waits for them, and re-layouts  8.24 us (2%)
    ppermute x8, waiting for transfers between devices, swap(): return lax.ppermute(array, 'gx', [(i, i ^ k) for i in range(count)])  131 us
    all_to_all x3, waiting for transfers between devices, exchange(): return lax.all_to_all(array, 'gx', split_axis=0, concat_axis=0, tiled=True)  88.6 us
    pallas_call x2, Pallas kernels, spectra_of(): pl.pallas_call(functools.partial(spectra_kernel, first, counts), out_shap...  46.6 us
    pallas_call x2, Pallas kernels, gram_of(): pl.pallas_call(functools.partial(gram_kernel, len(rest)), out_shape=jax.S...  26.7 us
    ppermute x8, starting transfers between devices, swap(): return lax.ppermute(array, 'gx', [(i, i ^ k) for i in range(count)])  21.6 us
    all_to_all x3, starting transfers between devices, exchange(): return lax.all_to_all(array, 'gx', split_axis=0, concat_axis=0, tiled=True)  19.7 us
    pallas_call x2, Pallas kernels, beams_of(): pl.pallas_call(functools.partial(beams_kernel, len(rest)), out_shape=jax....  19.1 us
    pallas_call x1, Pallas kernels, weights_of(): pl.pallas_call(weights_kernel, out_shape=jax.ShapeDtypeStruct((kept.shape...  18.7 us
  transfers between devices with their start and end apart: 11, of which 8 were waited for; matrix products, arithmetic and copies ran while one was open for 2% of the time, Pallas kernels for 25%

profile of v2, /device:TPU:13, one launch (start us, length us, event | category | flops | bytes accessed | tf_op | source)
XLA Modules:
  0.0 392.9 jit_solution(4340098304195444200)
XLA Ops:
  0.6 0.0 copy-start
  0.6 1.7 fusion.6
  2.4 0.4 copy.13
  2.8 0.9 convert_element_type.23.refs_4_.refs_1_
  3.7 7.8 %spectra.2 = bf16[16,12,2,16,128]{4,3,2,1,0:T(8,128)(2,1)} custom-call(s32[1]{0:T(128)} %bitcast.refs_0_.me_ref, s32[64]{0:T(128)} %refs_1_.3, bf16[2,64,67328]{2,1,0:T(8,128)(2,1)} %refs_2_.3, f32[8,256]{1,0:T(8,128)} %constant.80.clone.refs_3_, bf16[384,512]{1,0:T(8,128)(2,1)} %convert_element_type.23.refs_4_.refs_1_), custom_call_target="tpu_custom_call" | custom-call | flops 2415919104 | bytes 5881856 | tf_op jit(solution)/shard_map/spectra/pallas_call | solution.py:148
  11.5 6.6 %all-to-all-start = ((bf16[16,12,2,16,128]{4,3,2,1,0:T(8,128)(2,1)}), bf16[16,12,2,16,128]{4,3,2,1,0:T(8,128)(2,1)S(1)}, u32[]{:S(2)}, u32[]{:S(2)}) async-start(bf16[16,12,2,16,128]{4,3,2,1,0:T(8,128)(2,1)} %spectra.2), calls=%async_computation | async-start | bytes 3145728 | tf_op jit(solution)/shard_map/all_to_all | solution.py:438
  18.0 0.0 copy-done.14
  18.0 0.1 dynamic_slice.3.kept_ref
  18.1 38.9 %spectra.3 = (bf16[16,11,2,112,128]{4,3,2,1,0:T(8,128)(2,1)}, bf16[2,1,2,112,128]{4,3,2,1,0:T(8,128)(2,1)}, bf16[2,1,2,112,128]{4,3,2,1,0:T(8,128)(2,1)}, bf16[2...) custom-call(s32[1]{0:T(128)} %bitcast.refs_0_.me_ref, ...), custom_call_target="tpu_custom_call" | custom-call | flops 16911433728 | bytes 41172992 | tf_op jit(solution)/shard_map/spectra/pallas_call | solution.py:148
  57.0 0.0 copy-start.22
  57.0 0.0 copy-start.21
  57.0 0.0 copy-start.20
  57.0 0.0 copy-start.19
  57.0 0.0 copy-start.18
  57.1 0.0 copy-start.13
  57.1 0.0 copy-start.2
  57.1 0.0 all-to-all-done.lead
  57.1 0.0 copy-start.3
  57.1 1.2 copy-done.3
  58.3 6.0 %all-to-all-start.1 = ((bf16[16,11,2,112,128]{4,3,2,1,0:T(8,128)(2,1)}), bf16[16,11,2,112,128]{4,3,2,1,0:T(8,128)(2,1)}, u32[]{:S(2)}, u32[]{:S(2)}) async-start(bf16[16,11,2,112,128]{4,3,2,1,0:T(8,128)(2,1)} %get-tuple-element.34), calls=%async_computation.1 | async-start | bytes 20185088 | tf_op jit(solution)/shard_map/all_to_all | solution.py:438
  64.3 0.0 copy-done.22
  64.3 0.4 collective-permute-start
  64.7 0.0 copy-done.21
  64.7 0.3 collective-permute-start.1
  65.0 0.0 copy-done.20
  65.0 1.5 collective-permute-start.2
  66.5 0.0 copy-done.19
  66.5 0.3 collective-permute-start.3
  66.8 0.0 copy-done.18
  66.8 1.4 collective-permute-start.4
  68.2 0.0 copy-done.13
  68.3 0.0 copy-done.2
  68.3 1.9 gather_fusion.1
  70.2 0.0 copy-done
  70.2 1.1 gather_fusion
  71.3 0.0 copy-done.15
  71.3 0.5 fusion.12
  71.8 0.0 copy-done.5
  71.8 0.0 copy-start.17
  71.8 0.0 copy-start.16
  71.9 1.1 broadcast_select_fusion.delays_ref
  73.0 1.7 copy.15.refs_2_.refs_10_
  74.7 18.7 %weights.1.refs_1_.refs_9_ = bf16[12,2,256,1024]{3,2,1,0:T(8,128)(2,1)} custom-call(s32[12]{0:T(128)} %copy-done.15, f32[256,1024]{1,0:T(8,128)} %broadcast_select_fusion.delays_ref), custom_call_target="tpu_custom_call" | custom-call | flops 125829120 | bytes 12582912 | tf_op jit(solution)/shard_map/weights/pallas_call | solution.py:202
  93.4 0.0 collective-permute-done.refs_1_
  93.4 0.0 copy-done.17
  93.4 0.2 collective-permute-start.5
  93.6 15.5 %collective-permute-done.1.refs_2_ = bf16[2,1,2,112,128]{4,3,2,1,0:T(8,128)(2,1)S(1)} collective-permute-done((bf16[2,1,2,112,128]{4,3,2,1,0:T(8,128)(2,1)S(1)}, bf16[2,1,2,112,128]{4,3,2,1,0:T(8,128)(2,1)S(1)}, u32[]{:S(2)}, u32[]{:S(2)}) %collective-permute-start.1) | collective-permute-done | bytes 114720 | tf_op jit(solution)/shard_map/ppermute | solution.py:445
  109.1 16.4 %collective-permute-start.6 = (bf16[2,1,2,112,128]{4,3,2,1,0:T(8,128)(2,1)S(1)}, bf16[2,1,2,112,128]{4,3,2,1,0:T(8,128)(2,1)S(1)}, u32[]{:S(2)}, u32[]{:S(2)}) collective-permute-start(bf16[2,1,2,112,128]{4,3,2,1,0:T(8,128)(2,1)S(1)} %copy-done.16), channel_id=1, source_target_pairs={{0,7},{1,6},{2,5},{3,4},{4,3},{5,2},{6,1},{7,0},{8,15},{9,14},{10,... | collective-permute-start | bytes 344072 | tf_op jit(solution)/shard_map/ppermute | solution.py:445
  125.5 0.0 collective-permute-done.2.refs_3_
  125.5 105.8 %collective-permute-done.3.refs_4_ = bf16[2,1,2,112,128]{4,3,2,1,0:T(8,128)(2,1)S(1)} collective-permute-done((bf16[2,1,2,112,128]{4,3,2,1,0:T(8,128)(2,1)S(1)}, bf16[2,1,2,112,128]{4,3,2,1,0:T(8,128)(2,1)S(1)}, u32[]{:S(2)}, u32[]{:S(2)}) %collective-permute-start.3) | collective-permute-done | bytes 114720 | tf_op jit(solution)/shard_map/ppermute | solution.py:445
  231.4 3.4 collective-permute-done.4.refs_5_
  234.8 0.7 collective-permute-done.5.refs_6_
  235.5 2.4 collective-permute-done.6.refs_7_
  237.9 45.3 %all-to-all-done.1.refs_0_ = bf16[16,11,2,112,128]{4,3,2,1,0:T(8,128)(2,1)} async-done(((bf16[16,11,2,112,128]{4,3,2,1,0:T(8,128)(2,1)}), bf16[16,11,2,112,128]{4,3,2,1,0:T(8,128)(2,1)}, u32[]{:S(2)}, u32[]{:S(2)}) %all-to-all-start.1) | async-done | bytes 10092576 | tf_op jit(solution)/shard_map/all_to_all | solution.py:438
  283.2 1.1 collective-permute-start.7
  284.3 15.8 %beams.2.refs_11_ = bf16[16,12,2,16,256]{4,3,2,1,0:T(8,128)(2,1)} custom-call(s32[1]{0:T(128)} %bitcast.refs_0_.me_ref, bf16[16,12,2,16,128]{4,3,2,1,0:T(8,128)(2,1)} %copy-done.3, bf16[16,11,2,112,128]{4,3,2,1,0:T(8,128)(2,1)} %all-to-all-done.1.refs_0_, bf16[12,2,256,1024]{3,2,1,0:T(8,128)(2,1)} %weights.1.refs_1_.refs_9_, f32[12,256,2]{2,1,0:T(8,128)} %copy.15.refs_2_.refs_10_), custom_call_target="tpu_custom_call" | custom-call | flops 5905580032 | bytes 23068672 | tf_op jit(solution)/shard_map/beams/pallas_call | solution.py:299
  300.2 3.1 collective-permute-done.7.refs_8_
  303.3 0.8 copy-done.4
  304.1 3.3 beams.3
  307.4 7.1 %all-to-all-start.2 = ((bf16[16,12,2,16,256]{4,3,2,1,0:T(8,128)(2,1)}), bf16[16,12,2,16,256]{4,3,2,1,0:T(8,128)(2,1)}, u32[]{:S(2)}, u32[]{:S(2)}) async-start(bf16[16,12,2,16,256]{4,3,2,1,0:T(8,128)(2,1)} %beams.3), calls=%async_computation.2 | async-start | bytes 6291456 | tf_op jit(solution)/shard_map/all_to_all | solution.py:438
  314.5 22.2 %gram.2.refs_9_ = bf16[12,1024,1024]{2,1,0:T(8,128)(2,1)} custom-call(s32[1]{0:T(128)} %bitcast.refs_0_.me_ref, bf16[16,12,2,16,128]{4,3,2,1,0:T(8,128)(2,1)} %copy-done.3, bf16[16,11,2,112,128]{4,3,2,1,0:T(8,128)(2,1)} %all-to-all-done.1.refs_0_), custom_call_target="tpu_custom_call" | custom-call | flops 14763950080 | bytes 34603008 | tf_op jit(solution)/shard_map/gram/pallas_call | solution.py:358
  336.7 4.5 %gram.3 = bf16[12,1024,1024]{2,1,0:T(8,128)(2,1)} custom-call(s32[1]{0:T(128)} %bitcast.refs_0_.me_ref, bf16[16,12,2,16,128]{4,3,2,1,0:T(8,128)(2,1)} %copy-done.3, bf16[2,1,2,112,128]{4,3,2,1,0:T(8,128)(2,1)} %get-tuple-element.26.refs_0_, bf16[2,1,2,112,128]{4,3,2,1,0:T(8,128)(2,1)} %copy-done.6, ...), custom_call_target="tpu_custom_call", output_to_operand_aliasing={{}: (11, {})} | custom-call | flops 1342177280 | bytes 3145728 | tf_op jit(solution)/shard_map/gram/pallas_call | solution.py:358
  341.2 43.3 %all-to-all-done.2.refs_0_ = bf16[16,12,2,16,256]{4,3,2,1,0:T(8,128)(2,1)} async-done(((bf16[16,12,2,16,256]{4,3,2,1,0:T(8,128)(2,1)}), bf16[16,12,2,16,256]{4,3,2,1,0:T(8,128)(2,1)}, u32[]{:S(2)}, u32[]{:S(2)}) %all-to-all-start.2) | async-done | bytes 3145760 | tf_op jit(solution)/shard_map/all_to_all | solution.py:438
  384.5 8.4 %series.1 = f32[2,16,256,256]{3,2,1,0:T(8,128)} custom-call(bf16[16,12,2,16,256]{4,3,2,1,0:T(8,128)(2,1)} %all-to-all-done.2.refs_0_, bf16[384,512]{1,0:T(8,128)(2,1)} %convert_element_type.23.refs_4_.refs_1_), custom_call_target="tpu_custom_call" | custom-call | flops 1610612736 | bytes 11534336 | tf_op jit(solution)/shard_map/series/pallas_call | solution.py:419
  (36 shorter events, 0.2 us)
Async XLA Ops:
  0.6 69.6 %copy-start = (f32[256,1024]{1,0:T(8,128)S(1)}, f32[256,1024]{1,0:T(8,128)}, u32[]{:S(2)}) copy-start(f32[256,1024]{1,0:T(8,128)} %param.12) | copy-start | bytes 3145732
  3.7 14.3 %copy-start.14 = (s32[192]{0:T(256)S(1)}, s32[192]{0:T(256)}, u32[]{:S(2)}) copy-start(s32[192]{0:T(256)} %param.9) | copy-start | bytes 2308
  11.5 45.6 %all-to-all-start = ((bf16[16,12,2,16,128]{4,3,2,1,0:T(8,128)(2,1)}), bf16[16,12,2,16,128]{4,3,2,1,0:T(8,128)(2,1)S(1)}, u32[]{:S(2)}, u32[]{:S(2)}) async-start(bf16[16,12,2,16,128]{4,3,2,1,0:T(8,128)(2,1)} %spectra.2), calls=%async_computation | async-start | bytes 3145728 | tf_op jit(solution)/shard_map/all_to_all | solution.py:438
  18.1 53.2 %copy-start.15 = (s32[12]{0:T(128)}, s32[12]{0:T(128)S(1)}, u32[]{:S(2)}) copy-start(s32[12]{0:T(128)S(1)} %dynamic_slice.3.kept_ref) | copy-start | bytes 148
  57.0 7.3 %copy-start.22 = (bf16[2,1,2,112,128]{4,3,2,1,0:T(8,128)(2,1)S(1)}, bf16[2,1,2,112,128]{4,3,2,1,0:T(8,128)(2,1)}, u32[]{:S(2)}) copy-start(bf16[2,1,2,112,128]{4,3,2,1,0:T(8,128)(2,1)} %get-tuple-element.27) | copy-start | bytes 344068
  57.0 7.7 %copy-start.21 = (bf16[2,1,2,112,128]{4,3,2,1,0:T(8,128)(2,1)S(1)}, bf16[2,1,2,112,128]{4,3,2,1,0:T(8,128)(2,1)}, u32[]{:S(2)}) copy-start(bf16[2,1,2,112,128]{4,3,2,1,0:T(8,128)(2,1)} %get-tuple-element.28) | copy-start | bytes 344068
  57.0 8.0 %copy-start.20 = (bf16[2,1,2,112,128]{4,3,2,1,0:T(8,128)(2,1)S(1)}, bf16[2,1,2,112,128]{4,3,2,1,0:T(8,128)(2,1)}, u32[]{:S(2)}) copy-start(bf16[2,1,2,112,128]{4,3,2,1,0:T(8,128)(2,1)} %get-tuple-element.29) | copy-start | bytes 344068
  57.0 9.5 %copy-start.19 = (bf16[2,1,2,112,128]{4,3,2,1,0:T(8,128)(2,1)S(1)}, bf16[2,1,2,112,128]{4,3,2,1,0:T(8,128)(2,1)}, u32[]{:S(2)}) copy-start(bf16[2,1,2,112,128]{4,3,2,1,0:T(8,128)(2,1)} %get-tuple-element.30) | copy-start | bytes 344068
  57.0 9.8 %copy-start.18 = (bf16[2,1,2,112,128]{4,3,2,1,0:T(8,128)(2,1)S(1)}, bf16[2,1,2,112,128]{4,3,2,1,0:T(8,128)(2,1)}, u32[]{:S(2)}) copy-start(bf16[2,1,2,112,128]{4,3,2,1,0:T(8,128)(2,1)} %get-tuple-element.31) | copy-start | bytes 344068
  57.1 11.2 %copy-start.13 = (s32[256]{0:T(256)S(1)}, s32[256]{0:T(256)}, u32[]{:S(2)}) copy-start(s32[256]{0:T(256)} %param.10) | copy-start | bytes 3076
  57.1 11.2 %copy-start.2 = (s32[256]{0:T(256)S(1)}, s32[256]{0:T(256)}, u32[]{:S(2)}) copy-start(s32[256]{0:T(256)} %param.11) | copy-start | bytes 3076
  57.1 1.2 copy-start.3
  58.3 224.9 %all-to-all-start.1 = ((bf16[16,11,2,112,128]{4,3,2,1,0:T(8,128)(2,1)}), bf16[16,11,2,112,128]{4,3,2,1,0:T(8,128)(2,1)}, u32[]{:S(2)}, u32[]{:S(2)}) async-start(bf16[16,11,2,112,128]{4,3,2,1,0:T(8,128)(2,1)} %get-tuple-element.34), calls=%async_computation.1 | async-start | bytes 20185088 | tf_op jit(solution)/shard_map/all_to_all | solution.py:438
  64.3 7.5 %copy-start.5 = (bf16[2,1,2,112,128]{4,3,2,1,0:T(8,128)(2,1)S(1)}, bf16[2,1,2,112,128]{4,3,2,1,0:T(8,128)(2,1)}, u32[]{:S(2)}) copy-start(bf16[2,1,2,112,128]{4,3,2,1,0:T(8,128)(2,1)} %get-tuple-element.26.refs_0_) | copy-start | bytes 344068
  64.3 29.1 %collective-permute-start = (bf16[2,1,2,112,128]{4,3,2,1,0:T(8,128)(2,1)S(1)}, bf16[2,1,2,112,128]{4,3,2,1,0:T(8,128)(2,1)S(1)}, u32[]{:S(2)}, u32[]{:S(2)}) collective-permute-start(bf16[2,1,2,112,128]{4,3,2,1,0:T(8,128)(2,1)S(1)} %copy-done.22), channel_id=1, source_target_pairs={{0,1},{1,0},{2,3},{3,2},{4,5},{5,4},{6,7},{7,6},{8,9},{9,8},{10,11... | collective-permute-start | bytes 344072 | tf_op jit(solution)/shard_map/ppermute | solution.py:445
  64.7 44.4 %collective-permute-start.1 = (bf16[2,1,2,112,128]{4,3,2,1,0:T(8,128)(2,1)S(1)}, bf16[2,1,2,112,128]{4,3,2,1,0:T(8,128)(2,1)S(1)}, u32[]{:S(2)}, u32[]{:S(2)}) collective-permute-start(bf16[2,1,2,112,128]{4,3,2,1,0:T(8,128)(2,1)S(1)} %copy-done.21), channel_id=1, source_target_pairs={{0,2},{1,3},{2,0},{3,1},{4,6},{5,7},{6,4},{7,5},{8,10},{9,11},{10,... | collective-permute-start | bytes 344072 | tf_op jit(solution)/shard_map/ppermute | solution.py:445
  65.0 60.5 %collective-permute-start.2 = (bf16[2,1,2,112,128]{4,3,2,1,0:T(8,128)(2,1)S(1)}, bf16[2,1,2,112,128]{4,3,2,1,0:T(8,128)(2,1)S(1)}, u32[]{:S(2)}, u32[]{:S(2)}) collective-permute-start(bf16[2,1,2,112,128]{4,3,2,1,0:T(8,128)(2,1)S(1)} %copy-done.20), channel_id=1, source_target_pairs={{0,3},{1,2},{2,1},{3,0},{4,7},{5,6},{6,5},{7,4},{8,11},{9,10},{10,... | collective-permute-start | bytes 344072 | tf_op jit(solution)/shard_map/ppermute | solution.py:445
  66.5 164.8 %collective-permute-start.3 = (bf16[2,1,2,112,128]{4,3,2,1,0:T(8,128)(2,1)S(1)}, bf16[2,1,2,112,128]{4,3,2,1,0:T(8,128)(2,1)S(1)}, u32[]{:S(2)}, u32[]{:S(2)}) collective-permute-start(bf16[2,1,2,112,128]{4,3,2,1,0:T(8,128)(2,1)S(1)} %copy-done.19), channel_id=1, source_target_pairs={{0,4},{1,5},{2,6},{3,7},{4,0},{5,1},{6,2},{7,3},{8,12},{9,13},{10,... | collective-permute-start | bytes 344072 | tf_op jit(solution)/shard_map/ppermute | solution.py:445
  66.8 167.9 %collective-permute-start.4 = (bf16[2,1,2,112,128]{4,3,2,1,0:T(8,128)(2,1)S(1)}, bf16[2,1,2,112,128]{4,3,2,1,0:T(8,128)(2,1)S(1)}, u32[]{:S(2)}, u32[]{:S(2)}) collective-permute-start(bf16[2,1,2,112,128]{4,3,2,1,0:T(8,128)(2,1)S(1)} %copy-done.18), channel_id=1, source_target_pairs={{0,5},{1,4},{2,7},{3,6},{4,1},{5,0},{6,3},{7,2},{8,13},{9,12},{10,... | collective-permute-start | bytes 344072 | tf_op jit(solution)/shard_map/ppermute | solution.py:445
  71.8 21.6 %copy-start.17 = (bf16[2,1,2,112,128]{4,3,2,1,0:T(8,128)(2,1)S(1)}, bf16[2,1,2,112,128]{4,3,2,1,0:T(8,128)(2,1)}, u32[]{:S(2)}) copy-start(bf16[2,1,2,112,128]{4,3,2,1,0:T(8,128)(2,1)} %get-tuple-element.32) | copy-start | bytes 344068
  71.8 37.3 %copy-start.16 = (bf16[2,1,2,112,128]{4,3,2,1,0:T(8,128)(2,1)S(1)}, bf16[2,1,2,112,128]{4,3,2,1,0:T(8,128)(2,1)}, u32[]{:S(2)}) copy-start(bf16[2,1,2,112,128]{4,3,2,1,0:T(8,128)(2,1)} %get-tuple-element.33) | copy-start | bytes 344068
  93.4 206.7 %copy-start.6 = (bf16[2,1,2,112,128]{4,3,2,1,0:T(8,128)(2,1)}, bf16[2,1,2,112,128]{4,3,2,1,0:T(8,128)(2,1)S(1)}, u32[]{:S(2)}) copy-start(bf16[2,1,2,112,128]{4,3,2,1,0:T(8,128)(2,1)S(1)} %collective-permute-done.refs_1_) | copy-start | bytes 344068
  93.4 142.0 %collective-permute-start.5 = (bf16[2,1,2,112,128]{4,3,2,1,0:T(8,128)(2,1)S(1)}, bf16[2,1,2,112,128]{4,3,2,1,0:T(8,128)(2,1)S(1)}, u32[]{:S(2)}, u32[]{:S(2)}) collective-permute-start(bf16[2,1,2,112,128]{4,3,2,1,0:T(8,128)(2,1)S(1)} %copy-done.17), channel_id=1, source_target_pairs={{0,6},{1,7},{2,4},{3,5},{4,2},{5,3},{6,0},{7,1},{8,14},{9,15},{10,... | collective-permute-start | bytes 344072 | tf_op jit(solution)/shard_map/ppermute | solution.py:445
  109.1 191.0 %copy-start.7 = (bf16[2,1,2,112,128]{4,3,2,1,0:T(8,128)(2,1)}, bf16[2,1,2,112,128]{4,3,2,1,0:T(8,128)(2,1)S(1)}, u32[]{:S(2)}) copy-start(bf16[2,1,2,112,128]{4,3,2,1,0:T(8,128)(2,1)S(1)} %collective-permute-done.1.refs_2_) | copy-start | bytes 344068
  109.1 128.8 %collective-permute-start.6 = (bf16[2,1,2,112,128]{4,3,2,1,0:T(8,128)(2,1)S(1)}, bf16[2,1,2,112,128]{4,3,2,1,0:T(8,128)(2,1)S(1)}, u32[]{:S(2)}, u32[]{:S(2)}) collective-permute-start(bf16[2,1,2,112,128]{4,3,2,1,0:T(8,128)(2,1)S(1)} %copy-done.16), channel_id=1, source_target_pairs={{0,7},{1,6},{2,5},{3,4},{4,3},{5,2},{6,1},{7,0},{8,15},{9,14},{10,... | collective-permute-start | bytes 344072 | tf_op jit(solution)/shard_map/ppermute | solution.py:445
  125.5 174.6 %copy-start.8 = (bf16[2,1,2,112,128]{4,3,2,1,0:T(8,128)(2,1)}, bf16[2,1,2,112,128]{4,3,2,1,0:T(8,128)(2,1)S(1)}, u32[]{:S(2)}) copy-start(bf16[2,1,2,112,128]{4,3,2,1,0:T(8,128)(2,1)S(1)} %collective-permute-done.2.refs_3_) | copy-start | bytes 344068
  231.4 68.8 %copy-start.9 = (bf16[2,1,2,112,128]{4,3,2,1,0:T(8,128)(2,1)}, bf16[2,1,2,112,128]{4,3,2,1,0:T(8,128)(2,1)S(1)}, u32[]{:S(2)}) copy-start(bf16[2,1,2,112,128]{4,3,2,1,0:T(8,128)(2,1)S(1)} %collective-permute-done.3.refs_4_) | copy-start | bytes 344068
  234.8 65.4 %copy-start.10 = (bf16[2,1,2,112,128]{4,3,2,1,0:T(8,128)(2,1)}, bf16[2,1,2,112,128]{4,3,2,1,0:T(8,128)(2,1)S(1)}, u32[]{:S(2)}) copy-start(bf16[2,1,2,112,128]{4,3,2,1,0:T(8,128)(2,1)S(1)} %collective-permute-done.4.refs_5_) | copy-start | bytes 344068
  235.4 64.7 %copy-start.11 = (bf16[2,1,2,112,128]{4,3,2,1,0:T(8,128)(2,1)}, bf16[2,1,2,112,128]{4,3,2,1,0:T(8,128)(2,1)S(1)}, u32[]{:S(2)}) copy-start(bf16[2,1,2,112,128]{4,3,2,1,0:T(8,128)(2,1)S(1)} %collective-permute-done.5.refs_6_) | copy-start | bytes 344068
  237.9 62.3 %copy-start.12 = (bf16[2,1,2,112,128]{4,3,2,1,0:T(8,128)(2,1)}, bf16[2,1,2,112,128]{4,3,2,1,0:T(8,128)(2,1)S(1)}, u32[]{:S(2)}) copy-start(bf16[2,1,2,112,128]{4,3,2,1,0:T(8,128)(2,1)S(1)} %collective-permute-done.6.refs_7_) | copy-start | bytes 344068
  283.2 20.1 %collective-permute-start.7 = (bf16[8,1,2,112,128]{4,3,2,1,0:T(8,128)(2,1)S(1)}, bf16[8,1,2,112,128]{4,3,2,1,0:T(8,128)(2,1)S(1)}, u32[]{:S(2)}, u32[]{:S(2)}) collective-permute-start(bf16[8,1,2,112,128]{4,3,2,1,0:T(8,128)(2,1)S(1)} %slice_dynamic-update-slice_fusion), channel_id=1, source_target_pairs={{0,8},{1,9},{2,10},{3,11},{4,12},{5,13},{6,14},{7,15},{8,0},{9,1},... | collective-permute-start | bytes 1376264 | tf_op jit(solution)/shard_map/ppermute | solution.py:445
  303.3 0.8 copy-start.4
  307.4 77.1 %all-to-all-start.2 = ((bf16[16,12,2,16,256]{4,3,2,1,0:T(8,128)(2,1)}), bf16[16,12,2,16,256]{4,3,2,1,0:T(8,128)(2,1)}, u32[]{:S(2)}, u32[]{:S(2)}) async-start(bf16[16,12,2,16,256]{4,3,2,1,0:T(8,128)(2,1)} %beams.3), calls=%async_computation.2 | async-start | bytes 6291456 | tf_op jit(solution)/shard_map/all_to_all | solution.py:438
  336.7 56.2 %copy-start.1 = (f32[256,1024]{1,0:T(8,128)S(1)}, f32[256,1024]{1,0:T(8,128)}, u32[]{:S(2)}) copy-start(f32[256,1024]{1,0:T(8,128)} %param.12) | copy-start | bytes 3145732

commit v3 on v2

--- a/solution.py
+++ b/solution.py
@@ -13,9 +13,10 @@
 TAPS = 8
 ROWS = 16
 EACH = 3
-SHARE = 4
+SHARE = 8
 APART = 12
 LEAD = 1
+PITCH = 24
 STRETCH = 16
 F32 = jnp.float32
 BF16 = jnp.bfloat16
@@ -61,7 +62,7 @@
 def spectra_kernel(first, counts, *refs):
     me_ref, flags_ref, samples_ref, taper_ref, analysis_ref = refs[:5]
     out_refs, (frames_ref, wide_ref) = refs[5:-2], refs[-2:]
-    span = frames_ref.shape[1] // ROWS
+    span = frames_ref.shape[1] // PITCH
     co_rows = analysis_ref.shape[0]
     step = pl.program_id(0) + first
     group, begin = step // 2, (step % 2) * span
@@ -82,7 +83,7 @@
                     total = tiles[s] * tapers[0]
                     for t in range(1, TAPS):
                         total = total + tiles[s + t] * tapers[t]
-                    row = pl.multiple_of((at + s) * ROWS, ROWS)
+                    row = pl.multiple_of((at + s) * PITCH, 8)
                     frames_ref[x * (POINTS // 128) + half, pl.ds(row, ROWS), :] = total
         return carry
 
@@ -93,7 +94,7 @@
             [
                 jnp.concatenate(
                     [
-                        frames_ref[k, pl.ds(2 * pair + i, span, stride=ROWS), :].astype(BF16)
+                        frames_ref[k, pl.ds(2 * pair + i, span, stride=PITCH), :].astype(BF16)
                         for k in range(2 * POINTS // 128)
                     ],
                     axis=1,
@@ -107,7 +108,7 @@
         )
         for i in range(2):
             gain = flags_ref[group * ROWS + 2 * pair + i].astype(F32)
-            wide_ref[pl.ds(2 * pair + i, co_rows, stride=ROWS), :] = (
+            wide_ref[pl.ds(2 * pair + i, co_rows, stride=PITCH), :] = (
                 product[:, i * span : (i + 1) * span] * gain
             )
         return carry
@@ -115,7 +116,7 @@
     lax.fori_loop(0, ROWS // 2, transform, 0, unroll=4)
 
     def send(out, place, row):
-        out[place] = wide_ref[pl.ds(pl.multiple_of(row * ROWS, ROWS), ROWS), :].astype(BF16)
+        out[place] = wide_ref[pl.ds(pl.multiple_of(row * PITCH, 8), ROWS), :].astype(BF16)
 
     count, gx_count = counts[0], out_refs[0].shape[0]
 
@@ -158,8 +159,8 @@
         ],
         out_specs=out_specs,
         scratch_shapes=[
-            pltpu.VMEM((2 * POINTS // 128, span * ROWS, 128), F32),
-            pltpu.VMEM((co_rows * ROWS, span), F32),
+            pltpu.VMEM((2 * POINTS // 128, span * PITCH, 128), F32),
+            pltpu.VMEM((co_rows * PITCH, span), F32),
         ],
         compiler_params=pltpu.CompilerParams(vmem_limit_bytes=VMEM),
         cost_estimate=pl.CostEstimate(
@@ -377,6 +378,7 @@
     parts, (synthesis_ref, out_ref, wide_ref) = refs[:part_count], refs[part_count:]
     beam_dev, spectra_all = parts[0].shape[3:]
     rows = synthesis_ref.shape[0]
+    pitch = wide_ref.shape[1] // rows
     halves = [slice(k * 128, (k + 1) * 128) for k in range(spectra_all // 128)]
 
     @pl.when(pl.program_id(0) == 0)
@@ -388,7 +390,7 @@
             def widen_source(d, carry, base=base, part=part, each=each):
                 for j in range(each):
                     block = part[d, j // 2, j % 2]
-                    row = pl.multiple_of((base + d * each + j) * beam_dev, beam_dev)
+                    row = pl.multiple_of((base + d * each + j) * pitch, 8)
                     for k, half in enumerate(halves):
                         wide_ref[k, pl.ds(row, beam_dev), :] = block[:, half].astype(F32)
                 return carry
@@ -400,7 +402,7 @@
         beam = pl.program_id(0) * share + b
         turned = jnp.concatenate(
             [
-                wide_ref[k, pl.ds(beam, rows, stride=beam_dev), :].astype(BF16)
+                wide_ref[k, pl.ds(beam, rows, stride=pitch), :].astype(BF16)
                 for k in range(len(halves))
             ],
             axis=1,
@@ -415,6 +417,7 @@
 def series_of(parts, synthesis):
     beam_dev, spectra_all = parts[0].shape[3:]
     rows = synthesis.shape[0]
+    pitch = (beam_dev + 7) // 8 // 2 * 16 + 8
     share = SHARE
     return pl.pallas_call(
         functools.partial(series_kernel, share, len(parts)),
@@ -423,7 +426,7 @@
         in_specs=[pl.BlockSpec(a.shape, lambda b: (0, 0, 0, 0, 0)) for a in parts]
         + [pl.BlockSpec(synthesis.shape, lambda b: (0, 0))],
         out_specs=pl.BlockSpec((2, share, spectra_all, POINTS), lambda b: (0, b, 0, 0)),
-        scratch_shapes=[pltpu.VMEM((spectra_all // 128, rows * beam_dev, 128), F32)],
+        scratch_shapes=[pltpu.VMEM((spectra_all // 128, rows * pitch, 128), F32)],
         compiler_params=pltpu.CompilerParams(vmem_limit_bytes=VMEM),
         cost_estimate=pl.CostEstimate(
             flops=2 * beam_dev * rows * spectra_all * 2 * POINTS,

time: 394 us -> 388 us (0.985)
  Pallas kernels: 120 us -> 111 us
    pallas_call x2, Pallas kernels: 46.6 us -> 39.1 us  [spectra_of(): pl.pallas_call(functools.partial(spectra_kernel, first, counts), out_shap...]
  transfers between devices with their start and end apart: 11 -> 11, of which waited for: 8 -> 9; matrix products, arithmetic and copies ran while one was open for 2% -> 2% of each run, Pallas kernels for 25% -> 24%
where the time goes in v3:
time: 388 us; the launch traced here: 387 us
  waiting for transfers between devices  223 us (57%)
  Pallas kernels  111 us (29%)
  starting transfers between devices  40.2 us (10%)
  local copies, waits for them, and re-layouts  8.24 us (2%)
    ppermute x8, waiting for transfers between devices, swap(): return lax.ppermute(array, 'gx', [(i, i ^ k) for i in range(count)])  131 us
    all_to_all x3, waiting for transfers between devices, exchange(): return lax.all_to_all(array, 'gx', split_axis=0, concat_axis=0, tiled=True)  92.3 us
    pallas_call x2, Pallas kernels, spectra_of(): pl.pallas_call(functools.partial(spectra_kernel, first, counts), out_shap...  39.1 us
    pallas_call x2, Pallas kernels, gram_of(): pl.pallas_call(functools.partial(gram_kernel, len(rest)), out_shape=jax.S...  26.7 us
    ppermute x8, starting transfers between devices, swap(): return lax.ppermute(array, 'gx', [(i, i ^ k) for i in range(count)])  21.6 us
    pallas_call x2, Pallas kernels, beams_of(): pl.pallas_call(functools.partial(beams_kernel, len(rest)), out_shape=jax....  19.1 us
    pallas_call x1, Pallas kernels, weights_of(): pl.pallas_call(weights_kernel, out_shape=jax.ShapeDtypeStruct((kept.shape...  18.7 us
    all_to_all x3, starting transfers between devices, exchange(): return lax.all_to_all(array, 'gx', split_axis=0, concat_axis=0, tiled=True)  18.6 us
  transfers between devices with their start and end apart: 11, of which 9 were waited for; matrix products, arithmetic and copies ran while one was open for 2% of the time, Pallas kernels for 24%

profile of v3, /device:TPU:13, one launch (start us, length us, event | category | flops | bytes accessed | tf_op | source)
XLA Modules:
  0.0 386.7 jit_solution(13557435023081023330)
XLA Ops:
  0.6 0.0 copy-start
  0.6 1.7 fusion.6
  2.4 0.4 copy.13
  2.8 0.9 convert_element_type.23.refs_4_.refs_1_
  3.7 6.8 %spectra.2 = bf16[16,12,2,16,128]{4,3,2,1,0:T(8,128)(2,1)} custom-call(s32[1]{0:T(128)} %bitcast.refs_0_.me_ref, s32[64]{0:T(128)} %refs_1_.3, bf16[2,64,67328]{2,1,0:T(8,128)(2,1)} %refs_2_.3, f32[8,256]{1,0:T(8,128)} %constant.80.clone.refs_3_, bf16[384,512]{1,0:T(8,128)(2,1)} %convert_element_type.23.refs_4_.refs_1_), custom_call_target="tpu_custom_call" | custom-call | flops 2415919104 | bytes 5881856 | tf_op jit(solution)/shard_map/spectra/pallas_call | solution.py:149
  10.5 6.6 %all-to-all-start = ((bf16[16,12,2,16,128]{4,3,2,1,0:T(8,128)(2,1)}), bf16[16,12,2,16,128]{4,3,2,1,0:T(8,128)(2,1)S(1)}, u32[]{:S(2)}, u32[]{:S(2)}) async-start(bf16[16,12,2,16,128]{4,3,2,1,0:T(8,128)(2,1)} %spectra.2), calls=%async_computation | async-start | bytes 3145728 | tf_op jit(solution)/shard_map/all_to_all | solution.py:441
  17.1 0.0 copy-done.14
  17.1 0.1 dynamic_slice.3.kept_ref
  17.2 32.3 %spectra.3 = (bf16[16,11,2,112,128]{4,3,2,1,0:T(8,128)(2,1)}, bf16[2,1,2,112,128]{4,3,2,1,0:T(8,128)(2,1)}, bf16[2,1,2,112,128]{4,3,2,1,0:T(8,128)(2,1)}, bf16[2...) custom-call(s32[1]{0:T(128)} %bitcast.refs_0_.me_ref, ...), custom_call_target="tpu_custom_call" | custom-call | flops 16911433728 | bytes 41172992 | tf_op jit(solution)/shard_map/spectra/pallas_call | solution.py:149
  49.5 0.0 copy-start.22
  49.5 0.0 copy-start.21
  49.5 0.0 copy-start.20
  49.5 0.0 copy-start.19
  49.5 0.0 copy-start.18
  49.5 0.0 copy-start.13
  49.5 0.0 copy-start.2
  49.6 3.7 all-to-all-done.lead
  53.3 1.2 copy-done.3
  54.4 4.9 %all-to-all-start.1 = ((bf16[16,11,2,112,128]{4,3,2,1,0:T(8,128)(2,1)}), bf16[16,11,2,112,128]{4,3,2,1,0:T(8,128)(2,1)}, u32[]{:S(2)}, u32[]{:S(2)}) async-start(bf16[16,11,2,112,128]{4,3,2,1,0:T(8,128)(2,1)} %get-tuple-element.34), calls=%async_computation.1 | async-start | bytes 20185088 | tf_op jit(solution)/shard_map/all_to_all | solution.py:441
  59.4 0.0 copy-done.22
  59.4 0.4 collective-permute-start
  59.8 0.0 copy-done.21
  59.8 0.3 collective-permute-start.1
  60.1 0.0 copy-done.20
  60.1 1.5 collective-permute-start.2
  61.6 0.0 copy-done.19
  61.6 0.3 collective-permute-start.3
  61.9 0.0 copy-done.18
  61.9 1.4 collective-permute-start.4
  63.3 0.0 copy-done.13
  63.3 0.0 copy-done.2
  63.3 1.9 gather_fusion.1
  65.3 0.0 copy-done
  65.3 1.1 gather_fusion
  66.4 0.0 copy-done.15
  66.4 0.5 fusion.12
  66.9 0.0 copy-done.5
  66.9 0.0 copy-start.17
  66.9 0.0 copy-start.16
  66.9 1.1 broadcast_select_fusion.delays_ref
  68.1 1.7 copy.15.refs_2_.refs_10_
  69.7 18.7 %weights.1.refs_1_.refs_9_ = bf16[12,2,256,1024]{3,2,1,0:T(8,128)(2,1)} custom-call(s32[12]{0:T(128)} %copy-done.15, f32[256,1024]{1,0:T(8,128)} %broadcast_select_fusion.delays_ref), custom_call_target="tpu_custom_call" | custom-call | flops 125829120 | bytes 12582912 | tf_op jit(solution)/shard_map/weights/pallas_call | solution.py:203
  88.5 0.0 collective-permute-done.refs_1_
  88.5 0.0 copy-done.17
  88.5 0.2 collective-permute-start.5
  88.7 15.5 %collective-permute-done.1.refs_2_ = bf16[2,1,2,112,128]{4,3,2,1,0:T(8,128)(2,1)S(1)} collective-permute-done((bf16[2,1,2,112,128]{4,3,2,1,0:T(8,128)(2,1)S(1)}, bf16[2,1,2,112,128]{4,3,2,1,0:T(8,128)(2,1)S(1)}, u32[]{:S(2)}, u32[]{:S(2)}) %collective-permute-start.1) | collective-permute-done | bytes 114720 | tf_op jit(solution)/shard_map/ppermute | solution.py:448
  104.2 0.0 copy-done.16
  104.2 16.4 %collective-permute-start.6 = (bf16[2,1,2,112,128]{4,3,2,1,0:T(8,128)(2,1)S(1)}, bf16[2,1,2,112,128]{4,3,2,1,0:T(8,128)(2,1)S(1)}, u32[]{:S(2)}, u32[]{:S(2)}) collective-permute-start(bf16[2,1,2,112,128]{4,3,2,1,0:T(8,128)(2,1)S(1)} %copy-done.16), channel_id=1, source_target_pairs={{0,7},{1,6},{2,5},{3,4},{4,3},{5,2},{6,1},{7,0},{8,15},{9,14},{10,... | collective-permute-start | bytes 344072 | tf_op jit(solution)/shard_map/ppermute | solution.py:448
  120.6 0.0 collective-permute-done.2.refs_3_
  120.6 105.8 %collective-permute-done.3.refs_4_ = bf16[2,1,2,112,128]{4,3,2,1,0:T(8,128)(2,1)S(1)} collective-permute-done((bf16[2,1,2,112,128]{4,3,2,1,0:T(8,128)(2,1)S(1)}, bf16[2,1,2,112,128]{4,3,2,1,0:T(8,128)(2,1)S(1)}, u32[]{:S(2)}, u32[]{:S(2)}) %collective-permute-start.3) | collective-permute-done | bytes 114720 | tf_op jit(solution)/shard_map/ppermute | solution.py:448
  226.4 3.4 collective-permute-done.4.refs_5_
  229.8 0.7 collective-permute-done.5.refs_6_
  230.5 2.4 collective-permute-done.6.refs_7_
  233.0 45.3 %all-to-all-done.1.refs_0_ = bf16[16,11,2,112,128]{4,3,2,1,0:T(8,128)(2,1)} async-done(((bf16[16,11,2,112,128]{4,3,2,1,0:T(8,128)(2,1)}), bf16[16,11,2,112,128]{4,3,2,1,0:T(8,128)(2,1)}, u32[]{:S(2)}, u32[]{:S(2)}) %all-to-all-start.1) | async-done | bytes 10092576 | tf_op jit(solution)/shard_map/all_to_all | solution.py:441
  278.3 1.1 collective-permute-start.7
  279.4 15.8 %beams.2.refs_11_ = bf16[16,12,2,16,256]{4,3,2,1,0:T(8,128)(2,1)} custom-call(s32[1]{0:T(128)} %bitcast.refs_0_.me_ref, bf16[16,12,2,16,128]{4,3,2,1,0:T(8,128)(2,1)} %copy-done.3, bf16[16,11,2,112,128]{4,3,2,1,0:T(8,128)(2,1)} %all-to-all-done.1.refs_0_, bf16[12,2,256,1024]{3,2,1,0:T(8,128)(2,1)} %weights.1.refs_1_.refs_9_, f32[12,256,2]{2,1,0:T(8,128)} %copy.15.refs_2_.refs_10_), custom_call_target="tpu_custom_call" | custom-call | flops 5905580032 | bytes 23068672 | tf_op jit(solution)/shard_map/beams/pallas_call | solution.py:300
  295.2 3.1 collective-permute-done.7.refs_8_
  298.4 0.8 copy-done.4
  299.1 3.3 beams.3
  302.4 7.1 %all-to-all-start.2 = ((bf16[16,12,2,16,256]{4,3,2,1,0:T(8,128)(2,1)}), bf16[16,12,2,16,256]{4,3,2,1,0:T(8,128)(2,1)}, u32[]{:S(2)}, u32[]{:S(2)}) async-start(bf16[16,12,2,16,256]{4,3,2,1,0:T(8,128)(2,1)} %beams.3), calls=%async_computation.2 | async-start | bytes 6291456 | tf_op jit(solution)/shard_map/all_to_all | solution.py:441
  309.6 22.2 %gram.2.refs_9_ = bf16[12,1024,1024]{2,1,0:T(8,128)(2,1)} custom-call(s32[1]{0:T(128)} %bitcast.refs_0_.me_ref, bf16[16,12,2,16,128]{4,3,2,1,0:T(8,128)(2,1)} %copy-done.3, bf16[16,11,2,112,128]{4,3,2,1,0:T(8,128)(2,1)} %all-to-all-done.1.refs_0_), custom_call_target="tpu_custom_call" | custom-call | flops 14763950080 | bytes 34603008 | tf_op jit(solution)/shard_map/gram/pallas_call | solution.py:359
  331.8 4.5 %gram.3 = bf16[12,1024,1024]{2,1,0:T(8,128)(2,1)} custom-call(s32[1]{0:T(128)} %bitcast.refs_0_.me_ref, bf16[16,12,2,16,128]{4,3,2,1,0:T(8,128)(2,1)} %copy-done.3, bf16[2,1,2,112,128]{4,3,2,1,0:T(8,128)(2,1)} %get-tuple-element.26.refs_0_, bf16[2,1,2,112,128]{4,3,2,1,0:T(8,128)(2,1)} %copy-done.6, ...), custom_call_target="tpu_custom_call", output_to_operand_aliasing={{}: (11, {})} | custom-call | flops 1342177280 | bytes 3145728 | tf_op jit(solution)/shard_map/gram/pallas_call | solution.py:359
  336.2 43.3 %all-to-all-done.2.refs_0_ = bf16[16,12,2,16,256]{4,3,2,1,0:T(8,128)(2,1)} async-done(((bf16[16,12,2,16,256]{4,3,2,1,0:T(8,128)(2,1)}), bf16[16,12,2,16,256]{4,3,2,1,0:T(8,128)(2,1)}, u32[]{:S(2)}, u32[]{:S(2)}) %all-to-all-start.2) | async-done | bytes 3145760 | tf_op jit(solution)/shard_map/all_to_all | solution.py:441
  379.6 7.1 %series.1 = f32[2,16,256,256]{3,2,1,0:T(8,128)} custom-call(bf16[16,12,2,16,256]{4,3,2,1,0:T(8,128)(2,1)} %all-to-all-done.2.refs_0_, bf16[384,512]{1,0:T(8,128)(2,1)} %convert_element_type.23.refs_4_.refs_1_), custom_call_target="tpu_custom_call" | custom-call | flops 1610612736 | bytes 11534336 | tf_op jit(solution)/shard_map/series/pallas_call | solution.py:422
  (36 shorter events, 0.2 us)
Async XLA Ops:
  0.6 64.7 %copy-start = (f32[256,1024]{1,0:T(8,128)S(1)}, f32[256,1024]{1,0:T(8,128)}, u32[]{:S(2)}) copy-start(f32[256,1024]{1,0:T(8,128)} %param.12) | copy-start | bytes 3145732
  3.7 13.4 %copy-start.14 = (s32[192]{0:T(256)S(1)}, s32[192]{0:T(256)}, u32[]{:S(2)}) copy-start(s32[192]{0:T(256)} %param.9) | copy-start | bytes 2308
  10.5 42.7 %all-to-all-start = ((bf16[16,12,2,16,128]{4,3,2,1,0:T(8,128)(2,1)}), bf16[16,12,2,16,128]{4,3,2,1,0:T(8,128)(2,1)S(1)}, u32[]{:S(2)}, u32[]{:S(2)}) async-start(bf16[16,12,2,16,128]{4,3,2,1,0:T(8,128)(2,1)} %spectra.2), calls=%async_computation | async-start | bytes 3145728 | tf_op jit(solution)/shard_map/all_to_all | solution.py:441
  17.2 49.2 %copy-start.15 = (s32[12]{0:T(128)}, s32[12]{0:T(128)S(1)}, u32[]{:S(2)}) copy-start(s32[12]{0:T(128)S(1)} %dynamic_slice.3.kept_ref) | copy-start | bytes 148
  49.5 9.9 %copy-start.22 = (bf16[2,1,2,112,128]{4,3,2,1,0:T(8,128)(2,1)S(1)}, bf16[2,1,2,112,128]{4,3,2,1,0:T(8,128)(2,1)}, u32[]{:S(2)}) copy-start(bf16[2,1,2,112,128]{4,3,2,1,0:T(8,128)(2,1)} %get-tuple-element.27) | copy-start | bytes 344068
  49.5 10.3 %copy-start.21 = (bf16[2,1,2,112,128]{4,3,2,1,0:T(8,128)(2,1)S(1)}, bf16[2,1,2,112,128]{4,3,2,1,0:T(8,128)(2,1)}, u32[]{:S(2)}) copy-start(bf16[2,1,2,112,128]{4,3,2,1,0:T(8,128)(2,1)} %get-tuple-element.28) | copy-start | bytes 344068
  49.5 10.6 %copy-start.20 = (bf16[2,1,2,112,128]{4,3,2,1,0:T(8,128)(2,1)S(1)}, bf16[2,1,2,112,128]{4,3,2,1,0:T(8,128)(2,1)}, u32[]{:S(2)}) copy-start(bf16[2,1,2,112,128]{4,3,2,1,0:T(8,128)(2,1)} %get-tuple-element.29) | copy-start | bytes 344068
  49.5 12.1 %copy-start.19 = (bf16[2,1,2,112,128]{4,3,2,1,0:T(8,128)(2,1)S(1)}, bf16[2,1,2,112,128]{4,3,2,1,0:T(8,128)(2,1)}, u32[]{:S(2)}) copy-start(bf16[2,1,2,112,128]{4,3,2,1,0:T(8,128)(2,1)} %get-tuple-element.30) | copy-start | bytes 344068
  49.5 12.4 %copy-start.18 = (bf16[2,1,2,112,128]{4,3,2,1,0:T(8,128)(2,1)S(1)}, bf16[2,1,2,112,128]{4,3,2,1,0:T(8,128)(2,1)}, u32[]{:S(2)}) copy-start(bf16[2,1,2,112,128]{4,3,2,1,0:T(8,128)(2,1)} %get-tuple-element.31) | copy-start | bytes 344068
  49.5 13.8 %copy-start.13 = (s32[256]{0:T(256)S(1)}, s32[256]{0:T(256)}, u32[]{:S(2)}) copy-start(s32[256]{0:T(256)} %param.10) | copy-start | bytes 3076
  49.5 13.8 %copy-start.2 = (s32[256]{0:T(256)S(1)}, s32[256]{0:T(256)}, u32[]{:S(2)}) copy-start(s32[256]{0:T(256)} %param.11) | copy-start | bytes 3076
  53.3 1.2 copy-start.3
  54.4 223.8 %all-to-all-start.1 = ((bf16[16,11,2,112,128]{4,3,2,1,0:T(8,128)(2,1)}), bf16[16,11,2,112,128]{4,3,2,1,0:T(8,128)(2,1)}, u32[]{:S(2)}, u32[]{:S(2)}) async-start(bf16[16,11,2,112,128]{4,3,2,1,0:T(8,128)(2,1)} %get-tuple-element.34), calls=%async_computation.1 | async-start | bytes 20185088 | tf_op jit(solution)/shard_map/all_to_all | solution.py:441
  59.4 7.5 %copy-start.5 = (bf16[2,1,2,112,128]{4,3,2,1,0:T(8,128)(2,1)S(1)}, bf16[2,1,2,112,128]{4,3,2,1,0:T(8,128)(2,1)}, u32[]{:S(2)}) copy-start(bf16[2,1,2,112,128]{4,3,2,1,0:T(8,128)(2,1)} %get-tuple-element.26.refs_0_) | copy-start | bytes 344068
  59.4 29.1 %collective-permute-start = (bf16[2,1,2,112,128]{4,3,2,1,0:T(8,128)(2,1)S(1)}, bf16[2,1,2,112,128]{4,3,2,1,0:T(8,128)(2,1)S(1)}, u32[]{:S(2)}, u32[]{:S(2)}) collective-permute-start(bf16[2,1,2,112,128]{4,3,2,1,0:T(8,128)(2,1)S(1)} %copy-done.22), channel_id=1, source_target_pairs={{0,1},{1,0},{2,3},{3,2},{4,5},{5,4},{6,7},{7,6},{8,9},{9,8},{10,11... | collective-permute-start | bytes 344072 | tf_op jit(solution)/shard_map/ppermute | solution.py:448
  59.8 44.4 %collective-permute-start.1 = (bf16[2,1,2,112,128]{4,3,2,1,0:T(8,128)(2,1)S(1)}, bf16[2,1,2,112,128]{4,3,2,1,0:T(8,128)(2,1)S(1)}, u32[]{:S(2)}, u32[]{:S(2)}) collective-permute-start(bf16[2,1,2,112,128]{4,3,2,1,0:T(8,128)(2,1)S(1)} %copy-done.21), channel_id=1, source_target_pairs={{0,2},{1,3},{2,0},{3,1},{4,6},{5,7},{6,4},{7,5},{8,10},{9,11},{10,... | collective-permute-start | bytes 344072 | tf_op jit(solution)/shard_map/ppermute | solution.py:448
  60.1 60.5 %collective-permute-start.2 = (bf16[2,1,2,112,128]{4,3,2,1,0:T(8,128)(2,1)S(1)}, bf16[2,1,2,112,128]{4,3,2,1,0:T(8,128)(2,1)S(1)}, u32[]{:S(2)}, u32[]{:S(2)}) collective-permute-start(bf16[2,1,2,112,128]{4,3,2,1,0:T(8,128)(2,1)S(1)} %copy-done.20), channel_id=1, source_target_pairs={{0,3},{1,2},{2,1},{3,0},{4,7},{5,6},{6,5},{7,4},{8,11},{9,10},{10,... | collective-permute-start | bytes 344072 | tf_op jit(solution)/shard_map/ppermute | solution.py:448
  61.6 164.8 %collective-permute-start.3 = (bf16[2,1,2,112,128]{4,3,2,1,0:T(8,128)(2,1)S(1)}, bf16[2,1,2,112,128]{4,3,2,1,0:T(8,128)(2,1)S(1)}, u32[]{:S(2)}, u32[]{:S(2)}) collective-permute-start(bf16[2,1,2,112,128]{4,3,2,1,0:T(8,128)(2,1)S(1)} %copy-done.19), channel_id=1, source_target_pairs={{0,4},{1,5},{2,6},{3,7},{4,0},{5,1},{6,2},{7,3},{8,12},{9,13},{10,... | collective-permute-start | bytes 344072 | tf_op jit(solution)/shard_map/ppermute | solution.py:448
  61.9 167.9 %collective-permute-start.4 = (bf16[2,1,2,112,128]{4,3,2,1,0:T(8,128)(2,1)S(1)}, bf16[2,1,2,112,128]{4,3,2,1,0:T(8,128)(2,1)S(1)}, u32[]{:S(2)}, u32[]{:S(2)}) collective-permute-start(bf16[2,1,2,112,128]{4,3,2,1,0:T(8,128)(2,1)S(1)} %copy-done.18), channel_id=1, source_target_pairs={{0,5},{1,4},{2,7},{3,6},{4,1},{5,0},{6,3},{7,2},{8,13},{9,12},{10,... | collective-permute-start | bytes 344072 | tf_op jit(solution)/shard_map/ppermute | solution.py:448
  66.9 21.6 %copy-start.17 = (bf16[2,1,2,112,128]{4,3,2,1,0:T(8,128)(2,1)S(1)}, bf16[2,1,2,112,128]{4,3,2,1,0:T(8,128)(2,1)}, u32[]{:S(2)}) copy-start(bf16[2,1,2,112,128]{4,3,2,1,0:T(8,128)(2,1)} %get-tuple-element.32) | copy-start | bytes 344068
  66.9 37.3 %copy-start.16 = (bf16[2,1,2,112,128]{4,3,2,1,0:T(8,128)(2,1)S(1)}, bf16[2,1,2,112,128]{4,3,2,1,0:T(8,128)(2,1)}, u32[]{:S(2)}) copy-start(bf16[2,1,2,112,128]{4,3,2,1,0:T(8,128)(2,1)} %get-tuple-element.33) | copy-start | bytes 344068
  88.5 206.7 %copy-start.6 = (bf16[2,1,2,112,128]{4,3,2,1,0:T(8,128)(2,1)}, bf16[2,1,2,112,128]{4,3,2,1,0:T(8,128)(2,1)S(1)}, u32[]{:S(2)}) copy-start(bf16[2,1,2,112,128]{4,3,2,1,0:T(8,128)(2,1)S(1)} %collective-permute-done.refs_1_) | copy-start | bytes 344068
  88.5 142.0 %collective-permute-start.5 = (bf16[2,1,2,112,128]{4,3,2,1,0:T(8,128)(2,1)S(1)}, bf16[2,1,2,112,128]{4,3,2,1,0:T(8,128)(2,1)S(1)}, u32[]{:S(2)}, u32[]{:S(2)}) collective-permute-start(bf16[2,1,2,112,128]{4,3,2,1,0:T(8,128)(2,1)S(1)} %copy-done.17), channel_id=1, source_target_pairs={{0,6},{1,7},{2,4},{3,5},{4,2},{5,3},{6,0},{7,1},{8,14},{9,15},{10,... | collective-permute-start | bytes 344072 | tf_op jit(solution)/shard_map/ppermute | solution.py:448
  104.2 191.0 %copy-start.7 = (bf16[2,1,2,112,128]{4,3,2,1,0:T(8,128)(2,1)}, bf16[2,1,2,112,128]{4,3,2,1,0:T(8,128)(2,1)S(1)}, u32[]{:S(2)}) copy-start(bf16[2,1,2,112,128]{4,3,2,1,0:T(8,128)(2,1)S(1)} %collective-permute-done.1.refs_2_) | copy-start | bytes 344068
  104.2 128.8 %collective-permute-start.6 = (bf16[2,1,2,112,128]{4,3,2,1,0:T(8,128)(2,1)S(1)}, bf16[2,1,2,112,128]{4,3,2,1,0:T(8,128)(2,1)S(1)}, u32[]{:S(2)}, u32[]{:S(2)}) collective-permute-start(bf16[2,1,2,112,128]{4,3,2,1,0:T(8,128)(2,1)S(1)} %copy-done.16), channel_id=1, source_target_pairs={{0,7},{1,6},{2,5},{3,4},{4,3},{5,2},{6,1},{7,0},{8,15},{9,14},{10,... | collective-permute-start | bytes 344072 | tf_op jit(solution)/shard_map/ppermute | solution.py:448
  120.6 174.6 %copy-start.8 = (bf16[2,1,2,112,128]{4,3,2,1,0:T(8,128)(2,1)}, bf16[2,1,2,112,128]{4,3,2,1,0:T(8,128)(2,1)S(1)}, u32[]{:S(2)}) copy-start(bf16[2,1,2,112,128]{4,3,2,1,0:T(8,128)(2,1)S(1)} %collective-permute-done.2.refs_3_) | copy-start | bytes 344068
  226.4 68.8 %copy-start.9 = (bf16[2,1,2,112,128]{4,3,2,1,0:T(8,128)(2,1)}, bf16[2,1,2,112,128]{4,3,2,1,0:T(8,128)(2,1)S(1)}, u32[]{:S(2)}) copy-start(bf16[2,1,2,112,128]{4,3,2,1,0:T(8,128)(2,1)S(1)} %collective-permute-done.3.refs_4_) | copy-start | bytes 344068
  229.8 65.4 %copy-start.10 = (bf16[2,1,2,112,128]{4,3,2,1,0:T(8,128)(2,1)}, bf16[2,1,2,112,128]{4,3,2,1,0:T(8,128)(2,1)S(1)}, u32[]{:S(2)}) copy-start(bf16[2,1,2,112,128]{4,3,2,1,0:T(8,128)(2,1)S(1)} %collective-permute-done.4.refs_5_) | copy-start | bytes 344068
  230.5 64.7 %copy-start.11 = (bf16[2,1,2,112,128]{4,3,2,1,0:T(8,128)(2,1)}, bf16[2,1,2,112,128]{4,3,2,1,0:T(8,128)(2,1)S(1)}, u32[]{:S(2)}) copy-start(bf16[2,1,2,112,128]{4,3,2,1,0:T(8,128)(2,1)S(1)} %collective-permute-done.5.refs_6_) | copy-start | bytes 344068
  233.0 62.3 %copy-start.12 = (bf16[2,1,2,112,128]{4,3,2,1,0:T(8,128)(2,1)}, bf16[2,1,2,112,128]{4,3,2,1,0:T(8,128)(2,1)S(1)}, u32[]{:S(2)}) copy-start(bf16[2,1,2,112,128]{4,3,2,1,0:T(8,128)(2,1)S(1)} %collective-permute-done.6.refs_7_) | copy-start | bytes 344068
  278.3 20.1 %collective-permute-start.7 = (bf16[8,1,2,112,128]{4,3,2,1,0:T(8,128)(2,1)S(1)}, bf16[8,1,2,112,128]{4,3,2,1,0:T(8,128)(2,1)S(1)}, u32[]{:S(2)}, u32[]{:S(2)}) collective-permute-start(bf16[8,1,2,112,128]{4,3,2,1,0:T(8,128)(2,1)S(1)} %slice_dynamic-update-slice_fusion), channel_id=1, source_target_pairs={{0,8},{1,9},{2,10},{3,11},{4,12},{5,13},{6,14},{7,15},{8,0},{9,1},... | collective-permute-start | bytes 1376264 | tf_op jit(solution)/shard_map/ppermute | solution.py:448
  298.4 0.8 copy-start.4
  302.4 77.1 %all-to-all-start.2 = ((bf16[16,12,2,16,256]{4,3,2,1,0:T(8,128)(2,1)}), bf16[16,12,2,16,256]{4,3,2,1,0:T(8,128)(2,1)}, u32[]{:S(2)}, u32[]{:S(2)}) async-start(bf16[16,12,2,16,256]{4,3,2,1,0:T(8,128)(2,1)} %beams.3), calls=%async_computation.2 | async-start | bytes 6291456 | tf_op jit(solution)/shard_map/all_to_all | solution.py:441
  331.8 54.9 %copy-start.1 = (f32[256,1024]{1,0:T(8,128)S(1)}, f32[256,1024]{1,0:T(8,128)}, u32[]{:S(2)}) copy-start(f32[256,1024]{1,0:T(8,128)} %param.12) | copy-start | bytes 3145732

commit v4 on v3

--- a/solution.py
+++ b/solution.py
@@ -44,12 +44,29 @@
     return shaped.reshape(tap_count, point_count).astype(np.float32)
 
 
-def dft_tables(kept, point_count):
-    spots = jnp.arange(point_count, dtype=jnp.int32)
-    turns = kept[:, None] * spots[None, :] % point_count
-    angle = turns.astype(F32) * (2.0 * math.pi / point_count)
-    scale = 1.0 / math.sqrt(point_count)
-    return jnp.cos(angle) * scale, jnp.sin(angle) * scale
+def form_table(kept_ref, table_ref):
+    shape = (16, table_ref.shape[1])
+    row = lax.broadcasted_iota(jnp.int32, shape, 0)
+    column = lax.broadcasted_iota(jnp.int32, shape, 1)
+    spot = column & (POINTS - 1)
+    quarter = ((row & 1) - jnp.where(column >= POINTS, 1, 0)) * (POINTS // 4)
+
+    def some_rows(block, carry):
+        bins = jnp.zeros(shape, jnp.int32)
+        for k in range(8):
+            bins = jnp.where((row >= 2 * k) & (row < 2 * k + 2), kept_ref[block * 8 + k], bins)
+        step = (bins * spot + quarter) & (POINTS - 1)
+        step = jnp.minimum(step, POINTS - step)
+        near = jnp.minimum(step, POINTS // 2 - step).astype(F32) * (1.0 / POINTS)
+        square = near * near
+        value = square * COSINE_FIT[-1] + COSINE_FIT[-2]
+        for factor in COSINE_FIT[-3::-1]:
+            value = value * square + factor
+        value = jnp.where(step > POINTS // 4, -value, value) * (1.0 / math.sqrt(POINTS))
+        table_ref[pl.ds(pl.multiple_of(block * 16, 16), 16), :] = value.astype(BF16)
+        return carry
+
+    lax.fori_loop(0, table_ref.shape[0] // 16, some_rows, 0)
 
 
 def rotation(dm_rows, kept):
@@ -60,8 +77,17 @@
 
 
 def spectra_kernel(first, counts, *refs):
-    me_ref, flags_ref, samples_ref, taper_ref, analysis_ref = refs[:5]
-    out_refs, (frames_ref, wide_ref) = refs[5:-2], refs[-2:]
+    me_ref, flags_ref, samples_ref, taper_ref = refs[:4]
+    (frames_ref, wide_ref) = refs[-2:]
+    if first:
+        analysis_ref, out_refs = refs[4], refs[5:-2]
+    else:
+        kept_ref, analysis_ref, out_refs = refs[4], refs[5], refs[6:-2]
+
+        @pl.when(pl.program_id(0) == 0)
+        def _():
+            form_table(kept_ref, analysis_ref)
+
     span = frames_ref.shape[1] // PITCH
     co_rows = analysis_ref.shape[0]
     step = pl.program_id(0) + first
@@ -135,8 +161,8 @@
                 send(out, (slot, j // 2, j % 2), (owner * chan_dev + count) * 2 + j)
 
 
-def spectra_of(samples, flags, me, taper, analysis, gx_count, counts, first, steps, span):
-    co_rows = analysis.shape[0]
+def spectra_of(samples, flags, me, taper, given, gx_count, counts, first, steps, span):
+    co_rows = given.shape[0] if first else 2 * given.shape[0]
     rows = steps * ROWS
     out_shape = [jax.ShapeDtypeStruct((gx_count, counts[0], 2, rows, span), BF16)]
     out_specs = [pl.BlockSpec((gx_count, counts[0], 2, ROWS, span), lambda g: (0, 0, 0, g, 0))]
@@ -145,6 +171,10 @@
         shape = (2, counts[1], 2, rows, span)
         out_shape += [jax.ShapeDtypeStruct(shape, BF16)] * half
         out_specs += [pl.BlockSpec((2, counts[1], 2, ROWS, span), lambda g: (0, 0, 0, g, 0))] * half
+    table_spec = pl.BlockSpec((co_rows, 2 * POINTS), lambda g: (0, 0))
+    if not first:
+        out_shape = [jax.ShapeDtypeStruct((co_rows, 2 * POINTS), BF16)] + out_shape
+        out_specs = [table_spec] + out_specs
     width = samples.shape[2] if steps > 1 or first else (span + TAPS - 1) * POINTS
     return pl.pallas_call(
         functools.partial(spectra_kernel, first, counts),
@@ -155,7 +185,7 @@
             pl.BlockSpec(memory_space=pltpu.SMEM),
             pl.BlockSpec((2, ROWS, width), lambda g: (0, (g + first) // 2, 0)),
             pl.BlockSpec((TAPS, POINTS), lambda g: (0, 0)),
-            pl.BlockSpec((co_rows, 2 * POINTS), lambda g: (0, 0)),
+            table_spec if first else pl.BlockSpec(memory_space=pltpu.SMEM),
         ],
         out_specs=out_specs,
         scratch_shapes=[
@@ -169,7 +199,7 @@
             transcendentals=0,
         ),
         name="spectra",
-    )(me, flags, samples, taper, analysis)
+    )(me, flags, samples, taper, given)
 
 
 def weights_kernel(kept_ref, delays_ref, out_ref):
@@ -461,13 +491,8 @@
     spot = me.reshape(1)
 
     taper = jnp.asarray(prototype_taper(TAPS, POINTS))
-    cosine, sine = dft_tables(kept_channels, POINTS)
-    table = jnp.stack(
-        [jnp.concatenate([cosine, sine], 1), jnp.concatenate([-sine, cosine], 1)], 1
-    ).astype(BF16)
-    table_rows = table.reshape(-1, 2 * POINTS)
-    (lead,) = spectra_of(
-        samples, flags, spot, taper, table_rows, gx_count, (chan_dev, 0), 0, ahead, span
+    table_rows, lead = spectra_of(
+        samples, flags, spot, taper, kept_channels, gx_count, (chan_dev, 0), 0, ahead, span
     )
     spot, lead = tie((spot, lead))
     rest, *near = spectra_of(

time: 388 us -> 386 us (level)
  no operation moved by 1% of the time
where the time goes in v4:
time: 386 us; the launch traced here: 385 us
  waiting for transfers between devices  223 us (58%)
  Pallas kernels  112 us (29%)
  starting transfers between devices  40.2 us (10%)
  local copies, waits for them, and re-layouts  6.91 us (2%)
    ppermute x8, waiting for transfers between devices, swap(): return lax.ppermute(array, 'gx', [(i, i ^ k) for i in range(count)])  131 us
    all_to_all x3, waiting for transfers between devices, exchange(): return lax.all_to_all(array, 'gx', split_axis=0, concat_axis=0, tiled=True)  92.4 us
    pallas_call x2, Pallas kernels, spectra_of(): pl.pallas_call(functools.partial(spectra_kernel, first, counts), out_shap...  40.3 us
    pallas_call x2, Pallas kernels, gram_of(): pl.pallas_call(functools.partial(gram_kernel, len(rest)), out_shape=jax.S...  26.7 us
    ppermute x8, starting transfers between devices, swap(): return lax.ppermute(array, 'gx', [(i, i ^ k) for i in range(count)])  21.6 us
    pallas_call x2, Pallas kernels, beams_of(): pl.pallas_call(functools.partial(beams_kernel, len(rest)), out_shape=jax....  19.1 us
    pallas_call x1, Pallas kernels, weights_of(): pl.pallas_call(weights_kernel, out_shape=jax.ShapeDtypeStruct((kept.shape...  18.7 us
    all_to_all x3, starting transfers between devices, exchange(): return lax.all_to_all(array, 'gx', split_axis=0, concat_axis=0, tiled=True)  18.6 us
  transfers between devices with their start and end apart: 11, of which 9 were waited for; matrix products, arithmetic and copies ran while one was open for 2% of the time, Pallas kernels for 24%

profile of v4, /device:TPU:13, one launch (start us, length us, event | category | flops | bytes accessed | tf_op | source)
XLA Modules:
  0.0 384.8 jit_solution(15348655649617257033)
XLA Ops:
  0.6 0.0 copy-start
  0.7 0.0 copy-start.14
  0.7 8.0 %spectra.2 = (bf16[384,512]{1,0:T(8,128)(2,1)}, bf16[16,12,2,16,128]{4,3,2,1,0:T(8,128)(2,1)}) custom-call(s32[1]{0:T(128)} %bitcast.refs_0_.me_ref, s32[64]{0:T(128)} %refs_1_.3, bf16[2,64,67328]{2,1,0:T(8,128)(2,1)} %refs_2_.3, f32[8,256]{1,0:T(8,128)} %constant.64.clone.refs_3_, s32[192]{0:T(256)} %refs_4_.1), custom_call_target="tpu_custom_call" | custom-call | flops 2415919104 | bytes 5881856 | tf_op jit(solution)/shard_map/spectra/pallas_call | solution.py:179
  8.6 6.6 %all-to-all-start = ((bf16[16,12,2,16,128]{4,3,2,1,0:T(8,128)(2,1)}), bf16[16,12,2,16,128]{4,3,2,1,0:T(8,128)(2,1)S(1)}, u32[]{:S(2)}, u32[]{:S(2)}) async-start(bf16[16,12,2,16,128]{4,3,2,1,0:T(8,128)(2,1)} %get-tuple-element.28), calls=%async_computation | async-start | bytes 3145728 | tf_op jit(solution)/shard_map/all_to_all | solution.py:471
  15.2 0.0 copy-done.14
  15.2 0.1 dynamic_slice.3.kept_ref
  15.3 32.3 %spectra.3 = (bf16[16,11,2,112,128]{4,3,2,1,0:T(8,128)(2,1)}, bf16[2,1,2,112,128]{4,3,2,1,0:T(8,128)(2,1)}, bf16[2,1,2,112,128]{4,3,2,1,0:T(8,128)(2,1)}, bf16[2...) custom-call(s32[1]{0:T(128)} %bitcast.refs_0_.me_ref, ...), custom_call_target="tpu_custom_call" | custom-call | flops 16911433728 | bytes 41172992 | tf_op jit(solution)/shard_map/spectra/pallas_call | solution.py:179
  47.6 0.0 copy-start.22
  47.6 0.0 copy-start.21
  47.6 0.0 copy-start.20
  47.6 0.0 copy-start.19
  47.6 0.0 copy-start.18
  47.6 0.0 copy-start.13
  47.6 0.0 copy-start.2
  47.6 3.7 all-to-all-done.lead
  51.4 1.2 copy-done.3
  52.6 4.9 %all-to-all-start.1 = ((bf16[16,11,2,112,128]{4,3,2,1,0:T(8,128)(2,1)}), bf16[16,11,2,112,128]{4,3,2,1,0:T(8,128)(2,1)}, u32[]{:S(2)}, u32[]{:S(2)}) async-start(bf16[16,11,2,112,128]{4,3,2,1,0:T(8,128)(2,1)} %get-tuple-element.38), calls=%async_computation.1 | async-start | bytes 20185088 | tf_op jit(solution)/shard_map/all_to_all | solution.py:471
  57.5 0.0 copy-done.22
  57.5 0.4 collective-permute-start
  57.9 0.0 copy-done.21
  57.9 0.3 collective-permute-start.1
  58.2 0.0 copy-done.20
  58.2 1.5 collective-permute-start.2
  59.7 0.0 copy-done.19
  59.7 0.3 collective-permute-start.3
  60.0 0.0 copy-done.18
  60.0 1.4 collective-permute-start.4
  61.4 0.0 copy-done.13
  61.4 0.0 copy-done.2
  61.5 1.9 gather_fusion.1
  63.4 0.0 copy-done
  63.4 1.1 gather_fusion
  64.5 0.0 copy-done.15
  64.5 0.5 fusion.5
  65.0 0.0 copy-done.5
  65.0 0.0 copy-start.17
  65.0 0.0 copy-start.16
  65.0 1.1 broadcast_select_fusion.delays_ref
  66.2 1.7 copy.12.refs_2_.refs_10_
  67.9 18.7 %weights.1.refs_1_.refs_9_ = bf16[12,2,256,1024]{3,2,1,0:T(8,128)(2,1)} custom-call(s32[12]{0:T(128)} %copy-done.15, f32[256,1024]{1,0:T(8,128)} %broadcast_select_fusion.delays_ref), custom_call_target="tpu_custom_call" | custom-call | flops 125829120 | bytes 12582912 | tf_op jit(solution)/shard_map/weights/pallas_call | solution.py:233
  86.6 0.0 collective-permute-done.refs_1_
  86.6 0.0 copy-done.17
  86.6 0.2 collective-permute-start.5
  86.8 15.5 %collective-permute-done.1.refs_2_ = bf16[2,1,2,112,128]{4,3,2,1,0:T(8,128)(2,1)S(1)} collective-permute-done((bf16[2,1,2,112,128]{4,3,2,1,0:T(8,128)(2,1)S(1)}, bf16[2,1,2,112,128]{4,3,2,1,0:T(8,128)(2,1)S(1)}, u32[]{:S(2)}, u32[]{:S(2)}) %collective-permute-start.1) | collective-permute-done | bytes 114720 | tf_op jit(solution)/shard_map/ppermute | solution.py:478
  102.3 0.0 copy-done.16
  102.3 16.4 %collective-permute-start.6 = (bf16[2,1,2,112,128]{4,3,2,1,0:T(8,128)(2,1)S(1)}, bf16[2,1,2,112,128]{4,3,2,1,0:T(8,128)(2,1)S(1)}, u32[]{:S(2)}, u32[]{:S(2)}) collective-permute-start(bf16[2,1,2,112,128]{4,3,2,1,0:T(8,128)(2,1)S(1)} %copy-done.16), channel_id=1, source_target_pairs={{0,7},{1,6},{2,5},{3,4},{4,3},{5,2},{6,1},{7,0},{8,15},{9,14},{10,... | collective-permute-start | bytes 344072 | tf_op jit(solution)/shard_map/ppermute | solution.py:478
  118.7 0.0 collective-permute-done.2.refs_3_
  118.7 0.0 copy-start.8
  118.7 105.8 %collective-permute-done.3.refs_4_ = bf16[2,1,2,112,128]{4,3,2,1,0:T(8,128)(2,1)S(1)} collective-permute-done((bf16[2,1,2,112,128]{4,3,2,1,0:T(8,128)(2,1)S(1)}, bf16[2,1,2,112,128]{4,3,2,1,0:T(8,128)(2,1)S(1)}, u32[]{:S(2)}, u32[]{:S(2)}) %collective-permute-start.3) | collective-permute-done | bytes 114720 | tf_op jit(solution)/shard_map/ppermute | solution.py:478
  224.6 3.4 collective-permute-done.4.refs_5_
  228.0 0.7 collective-permute-done.5.refs_6_
  228.6 2.4 collective-permute-done.6.refs_7_
  231.1 45.3 %all-to-all-done.1.refs_0_ = bf16[16,11,2,112,128]{4,3,2,1,0:T(8,128)(2,1)} async-done(((bf16[16,11,2,112,128]{4,3,2,1,0:T(8,128)(2,1)}), bf16[16,11,2,112,128]{4,3,2,1,0:T(8,128)(2,1)}, u32[]{:S(2)}, u32[]{:S(2)}) %all-to-all-start.1) | async-done | bytes 10092576 | tf_op jit(solution)/shard_map/all_to_all | solution.py:471
  276.4 1.1 collective-permute-start.7
  277.5 15.8 %beams.2.refs_11_ = bf16[16,12,2,16,256]{4,3,2,1,0:T(8,128)(2,1)} custom-call(s32[1]{0:T(128)} %bitcast.refs_0_.me_ref, bf16[16,12,2,16,128]{4,3,2,1,0:T(8,128)(2,1)} %copy-done.3, bf16[16,11,2,112,128]{4,3,2,1,0:T(8,128)(2,1)} %all-to-all-done.1.refs_0_, bf16[12,2,256,1024]{3,2,1,0:T(8,128)(2,1)} %weights.1.refs_1_.refs_9_, f32[12,256,2]{2,1,0:T(8,128)} %copy.12.refs_2_.refs_10_), custom_call_target="tpu_custom_call" | custom-call | flops 5905580032 | bytes 23068672 | tf_op jit(solution)/shard_map/beams/pallas_call | solution.py:330
  293.4 3.1 collective-permute-done.7.refs_8_
  296.5 0.8 copy-done.4
  297.3 3.3 beams.3
  300.6 7.1 %all-to-all-start.2 = ((bf16[16,12,2,16,256]{4,3,2,1,0:T(8,128)(2,1)}), bf16[16,12,2,16,256]{4,3,2,1,0:T(8,128)(2,1)}, u32[]{:S(2)}, u32[]{:S(2)}) async-start(bf16[16,12,2,16,256]{4,3,2,1,0:T(8,128)(2,1)} %beams.3), calls=%async_computation.2 | async-start | bytes 6291456 | tf_op jit(solution)/shard_map/all_to_all | solution.py:471
  307.7 22.2 %gram.2.refs_9_ = bf16[12,1024,1024]{2,1,0:T(8,128)(2,1)} custom-call(s32[1]{0:T(128)} %bitcast.refs_0_.me_ref, bf16[16,12,2,16,128]{4,3,2,1,0:T(8,128)(2,1)} %copy-done.3, bf16[16,11,2,112,128]{4,3,2,1,0:T(8,128)(2,1)} %all-to-all-done.1.refs_0_), custom_call_target="tpu_custom_call" | custom-call | flops 14763950080 | bytes 34603008 | tf_op jit(solution)/shard_map/gram/pallas_call | solution.py:389
  329.9 4.5 %gram.3 = bf16[12,1024,1024]{2,1,0:T(8,128)(2,1)} custom-call(s32[1]{0:T(128)} %bitcast.refs_0_.me_ref, bf16[16,12,2,16,128]{4,3,2,1,0:T(8,128)(2,1)} %copy-done.3, bf16[2,1,2,112,128]{4,3,2,1,0:T(8,128)(2,1)} %get-tuple-element.30.refs_0_, bf16[2,1,2,112,128]{4,3,2,1,0:T(8,128)(2,1)} %copy-done.6, ...), custom_call_target="tpu_custom_call", output_to_operand_aliasing={{}: (11, {})} | custom-call | flops 1342177280 | bytes 3145728 | tf_op jit(solution)/shard_map/gram/pallas_call | solution.py:389
  334.3 43.3 %all-to-all-done.2.refs_0_ = bf16[16,12,2,16,256]{4,3,2,1,0:T(8,128)(2,1)} async-done(((bf16[16,12,2,16,256]{4,3,2,1,0:T(8,128)(2,1)}), bf16[16,12,2,16,256]{4,3,2,1,0:T(8,128)(2,1)}, u32[]{:S(2)}, u32[]{:S(2)}) %all-to-all-start.2) | async-done | bytes 3145760 | tf_op jit(solution)/shard_map/all_to_all | solution.py:471
  377.7 7.1 %series.1 = f32[2,16,256,256]{3,2,1,0:T(8,128)} custom-call(bf16[16,12,2,16,256]{4,3,2,1,0:T(8,128)(2,1)} %all-to-all-done.2.refs_0_, bf16[384,512]{1,0:T(8,128)(2,1)} %get-tuple-element.25.refs_4_.refs_1_), custom_call_target="tpu_custom_call" | custom-call | flops 1610612736 | bytes 11534336 | tf_op jit(solution)/shard_map/series/pallas_call | solution.py:452
  384.8 0.0 copy-done.1
  (31 shorter events, 0.2 us)
Async XLA Ops:
  0.6 62.8 %copy-start = (f32[256,1024]{1,0:T(8,128)S(1)}, f32[256,1024]{1,0:T(8,128)}, u32[]{:S(2)}) copy-start(f32[256,1024]{1,0:T(8,128)} %param.12) | copy-start | bytes 3145732
  0.7 14.6 %copy-start.14 = (s32[192]{0:T(256)S(1)}, s32[192]{0:T(256)}, u32[]{:S(2)}) copy-start(s32[192]{0:T(256)} %refs_4_.1) | copy-start | bytes 2308
  8.6 42.7 %all-to-all-start = ((bf16[16,12,2,16,128]{4,3,2,1,0:T(8,128)(2,1)}), bf16[16,12,2,16,128]{4,3,2,1,0:T(8,128)(2,1)S(1)}, u32[]{:S(2)}, u32[]{:S(2)}) async-start(bf16[16,12,2,16,128]{4,3,2,1,0:T(8,128)(2,1)} %get-tuple-element.28), calls=%async_computation | async-start | bytes 3145728 | tf_op jit(solution)/shard_map/all_to_all | solution.py:471
  15.3 49.2 %copy-start.15 = (s32[12]{0:T(128)}, s32[12]{0:T(128)S(1)}, u32[]{:S(2)}) copy-start(s32[12]{0:T(128)S(1)} %dynamic_slice.3.kept_ref) | copy-start | bytes 148
  47.6 9.9 %copy-start.22 = (bf16[2,1,2,112,128]{4,3,2,1,0:T(8,128)(2,1)S(1)}, bf16[2,1,2,112,128]{4,3,2,1,0:T(8,128)(2,1)}, u32[]{:S(2)}) copy-start(bf16[2,1,2,112,128]{4,3,2,1,0:T(8,128)(2,1)} %get-tuple-element.31) | copy-start | bytes 344068
  47.6 10.4 %copy-start.21 = (bf16[2,1,2,112,128]{4,3,2,1,0:T(8,128)(2,1)S(1)}, bf16[2,1,2,112,128]{4,3,2,1,0:T(8,128)(2,1)}, u32[]{:S(2)}) copy-start(bf16[2,1,2,112,128]{4,3,2,1,0:T(8,128)(2,1)} %get-tuple-element.32) | copy-start | bytes 344068
  47.6 10.6 %copy-start.20 = (bf16[2,1,2,112,128]{4,3,2,1,0:T(8,128)(2,1)S(1)}, bf16[2,1,2,112,128]{4,3,2,1,0:T(8,128)(2,1)}, u32[]{:S(2)}) copy-start(bf16[2,1,2,112,128]{4,3,2,1,0:T(8,128)(2,1)} %get-tuple-element.33) | copy-start | bytes 344068
  47.6 12.1 %copy-start.19 = (bf16[2,1,2,112,128]{4,3,2,1,0:T(8,128)(2,1)S(1)}, bf16[2,1,2,112,128]{4,3,2,1,0:T(8,128)(2,1)}, u32[]{:S(2)}) copy-start(bf16[2,1,2,112,128]{4,3,2,1,0:T(8,128)(2,1)} %get-tuple-element.34) | copy-start | bytes 344068
  47.6 12.4 %copy-start.18 = (bf16[2,1,2,112,128]{4,3,2,1,0:T(8,128)(2,1)S(1)}, bf16[2,1,2,112,128]{4,3,2,1,0:T(8,128)(2,1)}, u32[]{:S(2)}) copy-start(bf16[2,1,2,112,128]{4,3,2,1,0:T(8,128)(2,1)} %get-tuple-element.35) | copy-start | bytes 344068
  47.6 13.8 %copy-start.13 = (s32[256]{0:T(256)S(1)}, s32[256]{0:T(256)}, u32[]{:S(2)}) copy-start(s32[256]{0:T(256)} %param.10) | copy-start | bytes 3076
  47.6 13.8 %copy-start.2 = (s32[256]{0:T(256)S(1)}, s32[256]{0:T(256)}, u32[]{:S(2)}) copy-start(s32[256]{0:T(256)} %param.11) | copy-start | bytes 3076
  51.4 1.2 copy-start.3
  52.6 223.8 %all-to-all-start.1 = ((bf16[16,11,2,112,128]{4,3,2,1,0:T(8,128)(2,1)}), bf16[16,11,2,112,128]{4,3,2,1,0:T(8,128)(2,1)}, u32[]{:S(2)}, u32[]{:S(2)}) async-start(bf16[16,11,2,112,128]{4,3,2,1,0:T(8,128)(2,1)} %get-tuple-element.38), calls=%async_computation.1 | async-start | bytes 20185088 | tf_op jit(solution)/shard_map/all_to_all | solution.py:471
  57.5 7.5 %copy-start.5 = (bf16[2,1,2,112,128]{4,3,2,1,0:T(8,128)(2,1)S(1)}, bf16[2,1,2,112,128]{4,3,2,1,0:T(8,128)(2,1)}, u32[]{:S(2)}) copy-start(bf16[2,1,2,112,128]{4,3,2,1,0:T(8,128)(2,1)} %get-tuple-element.30.refs_0_) | copy-start | bytes 344068
  57.5 29.1 %collective-permute-start = (bf16[2,1,2,112,128]{4,3,2,1,0:T(8,128)(2,1)S(1)}, bf16[2,1,2,112,128]{4,3,2,1,0:T(8,128)(2,1)S(1)}, u32[]{:S(2)}, u32[]{:S(2)}) collective-permute-start(bf16[2,1,2,112,128]{4,3,2,1,0:T(8,128)(2,1)S(1)} %copy-done.22), channel_id=1, source_target_pairs={{0,1},{1,0},{2,3},{3,2},{4,5},{5,4},{6,7},{7,6},{8,9},{9,8},{10,11... | collective-permute-start | bytes 344072 | tf_op jit(solution)/shard_map/ppermute | solution.py:478
  57.9 44.4 %collective-permute-start.1 = (bf16[2,1,2,112,128]{4,3,2,1,0:T(8,128)(2,1)S(1)}, bf16[2,1,2,112,128]{4,3,2,1,0:T(8,128)(2,1)S(1)}, u32[]{:S(2)}, u32[]{:S(2)}) collective-permute-start(bf16[2,1,2,112,128]{4,3,2,1,0:T(8,128)(2,1)S(1)} %copy-done.21), channel_id=1, source_target_pairs={{0,2},{1,3},{2,0},{3,1},{4,6},{5,7},{6,4},{7,5},{8,10},{9,11},{10,... | collective-permute-start | bytes 344072 | tf_op jit(solution)/shard_map/ppermute | solution.py:478
  58.2 60.5 %collective-permute-start.2 = (bf16[2,1,2,112,128]{4,3,2,1,0:T(8,128)(2,1)S(1)}, bf16[2,1,2,112,128]{4,3,2,1,0:T(8,128)(2,1)S(1)}, u32[]{:S(2)}, u32[]{:S(2)}) collective-permute-start(bf16[2,1,2,112,128]{4,3,2,1,0:T(8,128)(2,1)S(1)} %copy-done.20), channel_id=1, source_target_pairs={{0,3},{1,2},{2,1},{3,0},{4,7},{5,6},{6,5},{7,4},{8,11},{9,10},{10,... | collective-permute-start | bytes 344072 | tf_op jit(solution)/shard_map/ppermute | solution.py:478
  59.7 164.8 %collective-permute-start.3 = (bf16[2,1,2,112,128]{4,3,2,1,0:T(8,128)(2,1)S(1)}, bf16[2,1,2,112,128]{4,3,2,1,0:T(8,128)(2,1)S(1)}, u32[]{:S(2)}, u32[]{:S(2)}) collective-permute-start(bf16[2,1,2,112,128]{4,3,2,1,0:T(8,128)(2,1)S(1)} %copy-done.19), channel_id=1, source_target_pairs={{0,4},{1,5},{2,6},{3,7},{4,0},{5,1},{6,2},{7,3},{8,12},{9,13},{10,... | collective-permute-start | bytes 344072 | tf_op jit(solution)/shard_map/ppermute | solution.py:478
  60.0 167.9 %collective-permute-start.4 = (bf16[2,1,2,112,128]{4,3,2,1,0:T(8,128)(2,1)S(1)}, bf16[2,1,2,112,128]{4,3,2,1,0:T(8,128)(2,1)S(1)}, u32[]{:S(2)}, u32[]{:S(2)}) collective-permute-start(bf16[2,1,2,112,128]{4,3,2,1,0:T(8,128)(2,1)S(1)} %copy-done.18), channel_id=1, source_target_pairs={{0,5},{1,4},{2,7},{3,6},{4,1},{5,0},{6,3},{7,2},{8,13},{9,12},{10,... | collective-permute-start | bytes 344072 | tf_op jit(solution)/shard_map/ppermute | solution.py:478
  65.0 21.6 %copy-start.17 = (bf16[2,1,2,112,128]{4,3,2,1,0:T(8,128)(2,1)S(1)}, bf16[2,1,2,112,128]{4,3,2,1,0:T(8,128)(2,1)}, u32[]{:S(2)}) copy-start(bf16[2,1,2,112,128]{4,3,2,1,0:T(8,128)(2,1)} %get-tuple-element.36) | copy-start | bytes 344068
  65.0 37.3 %copy-start.16 = (bf16[2,1,2,112,128]{4,3,2,1,0:T(8,128)(2,1)S(1)}, bf16[2,1,2,112,128]{4,3,2,1,0:T(8,128)(2,1)}, u32[]{:S(2)}) copy-start(bf16[2,1,2,112,128]{4,3,2,1,0:T(8,128)(2,1)} %get-tuple-element.37) | copy-start | bytes 344068
  86.6 206.7 %copy-start.6 = (bf16[2,1,2,112,128]{4,3,2,1,0:T(8,128)(2,1)}, bf16[2,1,2,112,128]{4,3,2,1,0:T(8,128)(2,1)S(1)}, u32[]{:S(2)}) copy-start(bf16[2,1,2,112,128]{4,3,2,1,0:T(8,128)(2,1)S(1)} %collective-permute-done.refs_1_) | copy-start | bytes 344068
  86.6 142.0 %collective-permute-start.5 = (bf16[2,1,2,112,128]{4,3,2,1,0:T(8,128)(2,1)S(1)}, bf16[2,1,2,112,128]{4,3,2,1,0:T(8,128)(2,1)S(1)}, u32[]{:S(2)}, u32[]{:S(2)}) collective-permute-start(bf16[2,1,2,112,128]{4,3,2,1,0:T(8,128)(2,1)S(1)} %copy-done.17), channel_id=1, source_target_pairs={{0,6},{1,7},{2,4},{3,5},{4,2},{5,3},{6,0},{7,1},{8,14},{9,15},{10,... | collective-permute-start | bytes 344072 | tf_op jit(solution)/shard_map/ppermute | solution.py:478
  102.3 191.0 %copy-start.7 = (bf16[2,1,2,112,128]{4,3,2,1,0:T(8,128)(2,1)}, bf16[2,1,2,112,128]{4,3,2,1,0:T(8,128)(2,1)S(1)}, u32[]{:S(2)}) copy-start(bf16[2,1,2,112,128]{4,3,2,1,0:T(8,128)(2,1)S(1)} %collective-permute-done.1.refs_2_) | copy-start | bytes 344068
  102.3 128.8 %collective-permute-start.6 = (bf16[2,1,2,112,128]{4,3,2,1,0:T(8,128)(2,1)S(1)}, bf16[2,1,2,112,128]{4,3,2,1,0:T(8,128)(2,1)S(1)}, u32[]{:S(2)}, u32[]{:S(2)}) collective-permute-start(bf16[2,1,2,112,128]{4,3,2,1,0:T(8,128)(2,1)S(1)} %copy-done.16), channel_id=1, source_target_pairs={{0,7},{1,6},{2,5},{3,4},{4,3},{5,2},{6,1},{7,0},{8,15},{9,14},{10,... | collective-permute-start | bytes 344072 | tf_op jit(solution)/shard_map/ppermute | solution.py:478
  118.7 174.6 %copy-start.8 = (bf16[2,1,2,112,128]{4,3,2,1,0:T(8,128)(2,1)}, bf16[2,1,2,112,128]{4,3,2,1,0:T(8,128)(2,1)S(1)}, u32[]{:S(2)}) copy-start(bf16[2,1,2,112,128]{4,3,2,1,0:T(8,128)(2,1)S(1)} %collective-permute-done.2.refs_3_) | copy-start | bytes 344068
  224.5 68.8 %copy-start.9 = (bf16[2,1,2,112,128]{4,3,2,1,0:T(8,128)(2,1)}, bf16[2,1,2,112,128]{4,3,2,1,0:T(8,128)(2,1)S(1)}, u32[]{:S(2)}) copy-start(bf16[2,1,2,112,128]{4,3,2,1,0:T(8,128)(2,1)S(1)} %collective-permute-done.3.refs_4_) | copy-start | bytes 344068
  228.0 65.4 %copy-start.10 = (bf16[2,1,2,112,128]{4,3,2,1,0:T(8,128)(2,1)}, bf16[2,1,2,112,128]{4,3,2,1,0:T(8,128)(2,1)S(1)}, u32[]{:S(2)}) copy-start(bf16[2,1,2,112,128]{4,3,2,1,0:T(8,128)(2,1)S(1)} %collective-permute-done.4.refs_5_) | copy-start | bytes 344068
  228.6 64.7 %copy-start.11 = (bf16[2,1,2,112,128]{4,3,2,1,0:T(8,128)(2,1)}, bf16[2,1,2,112,128]{4,3,2,1,0:T(8,128)(2,1)S(1)}, u32[]{:S(2)}) copy-start(bf16[2,1,2,112,128]{4,3,2,1,0:T(8,128)(2,1)S(1)} %collective-permute-done.5.refs_6_) | copy-start | bytes 344068
  231.1 62.3 %copy-start.12 = (bf16[2,1,2,112,128]{4,3,2,1,0:T(8,128)(2,1)}, bf16[2,1,2,112,128]{4,3,2,1,0:T(8,128)(2,1)S(1)}, u32[]{:S(2)}) copy-start(bf16[2,1,2,112,128]{4,3,2,1,0:T(8,128)(2,1)S(1)} %collective-permute-done.6.refs_7_) | copy-start | bytes 344068
  276.4 20.1 %collective-permute-start.7 = (bf16[8,1,2,112,128]{4,3,2,1,0:T(8,128)(2,1)S(1)}, bf16[8,1,2,112,128]{4,3,2,1,0:T(8,128)(2,1)S(1)}, u32[]{:S(2)}, u32[]{:S(2)}) collective-permute-start(bf16[8,1,2,112,128]{4,3,2,1,0:T(8,128)(2,1)S(1)} %slice_dynamic-update-slice_fusion), channel_id=1, source_target_pairs={{0,8},{1,9},{2,10},{3,11},{4,12},{5,13},{6,14},{7,15},{8,0},{9,1},... | collective-permute-start | bytes 1376264 | tf_op jit(solution)/shard_map/ppermute | solution.py:478
  296.5 0.8 copy-start.4
  300.6 77.1 %all-to-all-start.2 = ((bf16[16,12,2,16,256]{4,3,2,1,0:T(8,128)(2,1)}), bf16[16,12,2,16,256]{4,3,2,1,0:T(8,128)(2,1)}, u32[]{:S(2)}, u32[]{:S(2)}) async-start(bf16[16,12,2,16,256]{4,3,2,1,0:T(8,128)(2,1)} %beams.3), calls=%async_computation.2 | async-start | bytes 6291456 | tf_op jit(solution)/shard_map/all_to_all | solution.py:471
  329.9 54.9 %copy-start.1 = (f32[256,1024]{1,0:T(8,128)S(1)}, f32[256,1024]{1,0:T(8,128)}, u32[]{:S(2)}) copy-start(f32[256,1024]{1,0:T(8,128)} %param.12) | copy-start | bytes 3145732

commit v5 on v4

--- a/solution.py
+++ b/solution.py
@@ -510,7 +510,8 @@
     if apart:
         near = near[:1] + [swap(near[k], k, gx_count) for k in range(1, half)]
         relays = [jnp.stack([n[1, a:b] for n in near], 0) for a, b in cuts]
-    rest, lead = tie((rest, lead))
+    rest, mark = tie((rest, lead[:1, :1, :1, :ROWS, :]))
+    lead = lax.dynamic_update_slice(lead, mark, (0, 0, 0, 0, 0))
     rest = exchange(rest)
 
     beams, visibilities = None, None

time: 386 us -> 385 us (level)
  no operation moved by 1% of the time
where the time goes in v5:
time: 385 us; the launch traced here: 384 us
  waiting for transfers between devices  221 us (57%)
  Pallas kernels  112 us (29%)
  starting transfers between devices  40.3 us (10%)
  local copies, waits for them, and re-layouts  6.65 us (2%)
    ppermute x8, waiting for transfers between devices, swap(): return lax.ppermute(array, 'gx', [(i, i ^ k) for i in range(count)])  129 us
    all_to_all x3, waiting for transfers between devices, exchange(): return lax.all_to_all(array, 'gx', split_axis=0, concat_axis=0, tiled=True)  92.4 us
    pallas_call x2, Pallas kernels, spectra_of(): pl.pallas_call(functools.partial(spectra_kernel, first, counts), out_shap...  40.3 us
    pallas_call x2, Pallas kernels, gram_of(): pl.pallas_call(functools.partial(gram_kernel, len(rest)), out_shape=jax.S...  26.7 us
    ppermute x8, starting transfers between devices, swap(): return lax.ppermute(array, 'gx', [(i, i ^ k) for i in range(count)])  21.5 us
    pallas_call x2, Pallas kernels, beams_of(): pl.pallas_call(functools.partial(beams_kernel, len(rest)), out_shape=jax....  19.1 us
    all_to_all x3, starting transfers between devices, exchange(): return lax.all_to_all(array, 'gx', split_axis=0, concat_axis=0, tiled=True)  18.9 us
    pallas_call x1, Pallas kernels, weights_of(): pl.pallas_call(weights_kernel, out_shape=jax.ShapeDtypeStruct((kept.shape...  18.8 us
  transfers between devices with their start and end apart: 11, of which 9 were waited for; matrix products, arithmetic and copies ran while one was open for 2% of the time, Pallas kernels for 24%

profile of v5, /device:TPU:13, one launch (start us, length us, event | category | flops | bytes accessed | tf_op | source)
XLA Modules:
  0.0 383.9 jit_solution(4541116239180896569)
XLA Ops:
  0.6 0.0 copy-start
  0.7 8.0 %spectra.2 = (bf16[384,512]{1,0:T(8,128)(2,1)}, bf16[16,12,2,16,128]{4,3,2,1,0:T(8,128)(2,1)}) custom-call(s32[1]{0:T(128)} %bitcast.refs_0_.me_ref, s32[64]{0:T(128)} %refs_1_.3, bf16[2,64,67328]{2,1,0:T(8,128)(2,1)} %refs_2_.3, f32[8,256]{1,0:T(8,128)} %constant.64.clone.refs_3_, s32[192]{0:T(256)} %refs_4_.1), custom_call_target="tpu_custom_call" | custom-call | flops 2415919104 | bytes 5881856 | tf_op jit(solution)/shard_map/spectra/pallas_call | solution.py:179
  8.6 0.0 copy-start.14
  8.6 6.7 %all-to-all-start = ((bf16[16,12,2,16,128]{4,3,2,1,0:T(8,128)(2,1)}), bf16[16,12,2,16,128]{4,3,2,1,0:T(8,128)(2,1)S(1)}, u32[]{:S(2)}, u32[]{:S(2)}) async-start(bf16[16,12,2,16,128]{4,3,2,1,0:T(8,128)(2,1)} %get-tuple-element.25), calls=%async_computation | async-start | bytes 3145728 | tf_op jit(solution)/shard_map/all_to_all | solution.py:471
  15.3 0.0 copy-done.14
  15.3 0.1 dynamic_slice.3.kept_ref
  15.4 0.0 copy-start.15
  15.4 32.3 %spectra.3 = (bf16[16,11,2,112,128]{4,3,2,1,0:T(8,128)(2,1)}, bf16[2,1,2,112,128]{4,3,2,1,0:T(8,128)(2,1)}, bf16[2,1,2,112,128]{4,3,2,1,0:T(8,128)(2,1)}, bf16[2...) custom-call(s32[1]{0:T(128)} %bitcast.refs_0_.me_ref, ...), custom_call_target="tpu_custom_call" | custom-call | flops 16911433728 | bytes 41172992 | tf_op jit(solution)/shard_map/spectra/pallas_call | solution.py:179
  47.7 3.8 all-to-all-done
  51.5 0.0 copy-start.18
  51.5 0.0 copy-start.13
  51.5 0.0 copy-start.2
  51.5 5.1 %all-to-all-start.1 = ((bf16[16,11,2,112,128]{4,3,2,1,0:T(8,128)(2,1)}), bf16[16,11,2,112,128]{4,3,2,1,0:T(8,128)(2,1)}, u32[]{:S(2)}, u32[]{:S(2)}) async-start(bf16[16,11,2,112,128]{4,3,2,1,0:T(8,128)(2,1)} %get-tuple-element.38), calls=%async_computation.1 | async-start | bytes 20185088 | tf_op jit(solution)/shard_map/all_to_all | solution.py:471
  56.6 0.4 collective-permute-start
  56.9 0.3 collective-permute-start.1
  57.2 1.5 collective-permute-start.2
  58.7 0.3 collective-permute-start.3
  59.0 0.0 copy-done.18
  59.0 1.4 collective-permute-start.4
  60.4 0.0 copy-done.13
  60.4 0.0 copy-done.2
  60.5 1.9 gather_fusion.1
  62.4 0.0 copy-done
  62.4 0.0 copy-start.5
  62.4 2.0 gather_fusion
  64.4 0.0 copy-done.15
  64.5 0.5 fusion.5
  64.9 0.0 copy-done.5
  65.0 2.3 broadcast_select_fusion.delays_ref
  67.3 1.7 copy.12.refs_2_.refs_10_
  69.0 18.8 %weights.1.refs_1_.refs_9_ = bf16[12,2,256,1024]{3,2,1,0:T(8,128)(2,1)} custom-call(s32[12]{0:T(128)} %copy-done.15, f32[256,1024]{1,0:T(8,128)} %broadcast_select_fusion.delays_ref), custom_call_target="tpu_custom_call" | custom-call | flops 125829120 | bytes 12582912 | tf_op jit(solution)/shard_map/weights/pallas_call | solution.py:233
  87.8 0.0 collective-permute-done.refs_1_
  87.8 0.0 copy-done.17
  87.8 0.1 collective-permute-start.5
  87.9 13.5 %collective-permute-done.1.refs_2_ = bf16[2,1,2,112,128]{4,3,2,1,0:T(8,128)(2,1)S(1)} collective-permute-done((bf16[2,1,2,112,128]{4,3,2,1,0:T(8,128)(2,1)}, bf16[2,1,2,112,128]{4,3,2,1,0:T(8,128)(2,1)S(1)}, u32[]{:S(2)}, u32[]{:S(2)}) %collective-permute-start.1) | collective-permute-done | bytes 114720 | tf_op jit(solution)/shard_map/ppermute | solution.py:478
  101.4 0.0 copy-done.16
  101.4 16.4 %collective-permute-start.6 = (bf16[2,1,2,112,128]{4,3,2,1,0:T(8,128)(2,1)S(1)}, bf16[2,1,2,112,128]{4,3,2,1,0:T(8,128)(2,1)S(1)}, u32[]{:S(2)}, u32[]{:S(2)}) collective-permute-start(bf16[2,1,2,112,128]{4,3,2,1,0:T(8,128)(2,1)S(1)} %copy-done.16), channel_id=1, source_target_pairs={{0,7},{1,6},{2,5},{3,4},{4,3},{5,2},{6,1},{7,0},{8,15},{9,14},{10,... | collective-permute-start | bytes 344072 | tf_op jit(solution)/shard_map/ppermute | solution.py:478
  117.8 0.0 collective-permute-done.2.refs_3_
  117.8 0.0 copy-start.8
  117.8 105.8 %collective-permute-done.3.refs_4_ = bf16[2,1,2,112,128]{4,3,2,1,0:T(8,128)(2,1)S(1)} collective-permute-done((bf16[2,1,2,112,128]{4,3,2,1,0:T(8,128)(2,1)}, bf16[2,1,2,112,128]{4,3,2,1,0:T(8,128)(2,1)S(1)}, u32[]{:S(2)}, u32[]{:S(2)}) %collective-permute-start.3) | collective-permute-done | bytes 114720 | tf_op jit(solution)/shard_map/ppermute | solution.py:478
  223.6 3.4 collective-permute-done.4.refs_5_
  227.1 0.7 collective-permute-done.5.refs_6_
  227.7 2.4 collective-permute-done.6.refs_7_
  230.2 0.0 copy-start.3
  230.2 45.3 %all-to-all-done.1.refs_0_ = bf16[16,11,2,112,128]{4,3,2,1,0:T(8,128)(2,1)} async-done(((bf16[16,11,2,112,128]{4,3,2,1,0:T(8,128)(2,1)}), bf16[16,11,2,112,128]{4,3,2,1,0:T(8,128)(2,1)}, u32[]{:S(2)}, u32[]{:S(2)}) %all-to-all-start.1) | async-done | bytes 10092576 | tf_op jit(solution)/shard_map/all_to_all | solution.py:471
  275.5 1.1 collective-permute-start.7
  276.6 0.0 copy-done.3
  276.6 15.8 %beams.2.refs_11_ = bf16[16,12,2,16,256]{4,3,2,1,0:T(8,128)(2,1)} custom-call(s32[1]{0:T(128)} %bitcast.refs_0_.me_ref, bf16[16,12,2,16,128]{4,3,2,1,0:T(8,128)(2,1)} %copy-done.3, bf16[16,11,2,112,128]{4,3,2,1,0:T(8,128)(2,1)} %all-to-all-done.1.refs_0_, bf16[12,2,256,1024]{3,2,1,0:T(8,128)(2,1)} %weights.1.refs_1_.refs_9_, f32[12,256,2]{2,1,0:T(8,128)} %copy.12.refs_2_.refs_10_), custom_call_target="tpu_custom_call" | custom-call | flops 5905580032 | bytes 23068672 | tf_op jit(solution)/shard_map/beams/pallas_call | solution.py:330
  292.4 0.0 copy-done.6
  292.4 0.0 copy-done.7
  292.4 0.0 copy-done.8
  292.4 0.0 copy-done.9
  292.4 0.0 copy-done.10
  292.4 0.0 copy-done.11
  292.5 0.0 copy-done.12
  292.5 3.1 collective-permute-done.7.refs_8_
  295.6 0.8 copy-done.4
  296.3 3.3 beams.3
  299.6 7.1 %all-to-all-start.2 = ((bf16[16,12,2,16,256]{4,3,2,1,0:T(8,128)(2,1)}), bf16[16,12,2,16,256]{4,3,2,1,0:T(8,128)(2,1)}, u32[]{:S(2)}, u32[]{:S(2)}) async-start(bf16[16,12,2,16,256]{4,3,2,1,0:T(8,128)(2,1)} %beams.3), calls=%async_computation.2 | async-start | bytes 6291456 | tf_op jit(solution)/shard_map/all_to_all | solution.py:471
  306.8 22.2 %gram.2.refs_9_ = bf16[12,1024,1024]{2,1,0:T(8,128)(2,1)} custom-call(s32[1]{0:T(128)} %bitcast.refs_0_.me_ref, bf16[16,12,2,16,128]{4,3,2,1,0:T(8,128)(2,1)} %copy-done.3, bf16[16,11,2,112,128]{4,3,2,1,0:T(8,128)(2,1)} %all-to-all-done.1.refs_0_), custom_call_target="tpu_custom_call" | custom-call | flops 14763950080 | bytes 34603008 | tf_op jit(solution)/shard_map/gram/pallas_call | solution.py:389
  329.0 4.5 %gram.3 = bf16[12,1024,1024]{2,1,0:T(8,128)(2,1)} custom-call(s32[1]{0:T(128)} %bitcast.refs_0_.me_ref, bf16[16,12,2,16,128]{4,3,2,1,0:T(8,128)(2,1)} %copy-done.3, bf16[2,1,2,112,128]{4,3,2,1,0:T(8,128)(2,1)} %get-tuple-element.30.refs_0_, bf16[2,1,2,112,128]{4,3,2,1,0:T(8,128)(2,1)} %copy-done.6, ...), custom_call_target="tpu_custom_call", output_to_operand_aliasing={{}: (11, {})} | custom-call | flops 1342177280 | bytes 3145728 | tf_op jit(solution)/shard_map/gram/pallas_call | solution.py:389
  333.4 43.3 %all-to-all-done.2.refs_0_ = bf16[16,12,2,16,256]{4,3,2,1,0:T(8,128)(2,1)} async-done(((bf16[16,12,2,16,256]{4,3,2,1,0:T(8,128)(2,1)}), bf16[16,12,2,16,256]{4,3,2,1,0:T(8,128)(2,1)}, u32[]{:S(2)}, u32[]{:S(2)}) %all-to-all-start.2) | async-done | bytes 3145760 | tf_op jit(solution)/shard_map/all_to_all | solution.py:471
  376.8 7.1 %series.1 = f32[2,16,256,256]{3,2,1,0:T(8,128)} custom-call(bf16[16,12,2,16,256]{4,3,2,1,0:T(8,128)(2,1)} %all-to-all-done.2.refs_0_, bf16[384,512]{1,0:T(8,128)(2,1)} %get-tuple-element.26.refs_4_.refs_1_), custom_call_target="tpu_custom_call" | custom-call | flops 1610612736 | bytes 11534336 | tf_op jit(solution)/shard_map/series/pallas_call | solution.py:452
  383.9 0.0 copy-done.1
  (25 shorter events, 0.2 us)
Async XLA Ops:
  0.6 61.8 %copy-start = (f32[256,1024]{1,0:T(8,128)S(1)}, f32[256,1024]{1,0:T(8,128)}, u32[]{:S(2)}) copy-start(f32[256,1024]{1,0:T(8,128)} %param.12) | copy-start | bytes 3145732
  8.6 6.7 %copy-start.14 = (s32[192]{0:T(256)S(1)}, s32[192]{0:T(256)}, u32[]{:S(2)}) copy-start(s32[192]{0:T(256)} %refs_4_.1) | copy-start | bytes 2308
  8.6 42.9 %all-to-all-start = ((bf16[16,12,2,16,128]{4,3,2,1,0:T(8,128)(2,1)}), bf16[16,12,2,16,128]{4,3,2,1,0:T(8,128)(2,1)S(1)}, u32[]{:S(2)}, u32[]{:S(2)}) async-start(bf16[16,12,2,16,128]{4,3,2,1,0:T(8,128)(2,1)} %get-tuple-element.25), calls=%async_computation | async-start | bytes 3145728 | tf_op jit(solution)/shard_map/all_to_all | solution.py:471
  15.4 49.0 %copy-start.15 = (s32[12]{0:T(128)}, s32[12]{0:T(128)S(1)}, u32[]{:S(2)}) copy-start(s32[12]{0:T(128)S(1)} %dynamic_slice.3.kept_ref) | copy-start | bytes 148
  51.5 7.5 %copy-start.18 = (bf16[2,1,2,112,128]{4,3,2,1,0:T(8,128)(2,1)S(1)}, bf16[2,1,2,112,128]{4,3,2,1,0:T(8,128)(2,1)}, u32[]{:S(2)}) copy-start(bf16[2,1,2,112,128]{4,3,2,1,0:T(8,128)(2,1)} %get-tuple-element.35) | copy-start | bytes 344068
  51.5 8.9 %copy-start.13 = (s32[256]{0:T(256)S(1)}, s32[256]{0:T(256)}, u32[]{:S(2)}) copy-start(s32[256]{0:T(256)} %param.10) | copy-start | bytes 3076
  51.5 8.9 %copy-start.2 = (s32[256]{0:T(256)S(1)}, s32[256]{0:T(256)}, u32[]{:S(2)}) copy-start(s32[256]{0:T(256)} %param.11) | copy-start | bytes 3076
  51.5 224.0 %all-to-all-start.1 = ((bf16[16,11,2,112,128]{4,3,2,1,0:T(8,128)(2,1)}), bf16[16,11,2,112,128]{4,3,2,1,0:T(8,128)(2,1)}, u32[]{:S(2)}, u32[]{:S(2)}) async-start(bf16[16,11,2,112,128]{4,3,2,1,0:T(8,128)(2,1)} %get-tuple-element.38), calls=%async_computation.1 | async-start | bytes 20185088 | tf_op jit(solution)/shard_map/all_to_all | solution.py:471
  56.6 31.2 %collective-permute-start = (bf16[2,1,2,112,128]{4,3,2,1,0:T(8,128)(2,1)}, bf16[2,1,2,112,128]{4,3,2,1,0:T(8,128)(2,1)S(1)}, u32[]{:S(2)}, u32[]{:S(2)}) collective-permute-start(bf16[2,1,2,112,128]{4,3,2,1,0:T(8,128)(2,1)} %get-tuple-element.31), channel_id=1, source_target_pairs={{0,1},{1,0},{2,3},{3,2},{4,5},{5,4},{6,7},{7,6},{8,9},{9,8},{10,11... | collective-permute-start | bytes 344072 | tf_op jit(solution)/shard_map/ppermute | solution.py:478
  56.9 44.5 %collective-permute-start.1 = (bf16[2,1,2,112,128]{4,3,2,1,0:T(8,128)(2,1)}, bf16[2,1,2,112,128]{4,3,2,1,0:T(8,128)(2,1)S(1)}, u32[]{:S(2)}, u32[]{:S(2)}) collective-permute-start(bf16[2,1,2,112,128]{4,3,2,1,0:T(8,128)(2,1)} %get-tuple-element.32), channel_id=1, source_target_pairs={{0,2},{1,3},{2,0},{3,1},{4,6},{5,7},{6,4},{7,5},{8,10},{9,11},{10,... | collective-permute-start | bytes 344072 | tf_op jit(solution)/shard_map/ppermute | solution.py:478
  57.2 60.6 %collective-permute-start.2 = (bf16[2,1,2,112,128]{4,3,2,1,0:T(8,128)(2,1)}, bf16[2,1,2,112,128]{4,3,2,1,0:T(8,128)(2,1)S(1)}, u32[]{:S(2)}, u32[]{:S(2)}) collective-permute-start(bf16[2,1,2,112,128]{4,3,2,1,0:T(8,128)(2,1)} %get-tuple-element.33), channel_id=1, source_target_pairs={{0,3},{1,2},{2,1},{3,0},{4,7},{5,6},{6,5},{7,4},{8,11},{9,10},{10,... | collective-permute-start | bytes 344072 | tf_op jit(solution)/shard_map/ppermute | solution.py:478
  58.7 164.9 %collective-permute-start.3 = (bf16[2,1,2,112,128]{4,3,2,1,0:T(8,128)(2,1)}, bf16[2,1,2,112,128]{4,3,2,1,0:T(8,128)(2,1)S(1)}, u32[]{:S(2)}, u32[]{:S(2)}) collective-permute-start(bf16[2,1,2,112,128]{4,3,2,1,0:T(8,128)(2,1)} %get-tuple-element.34), channel_id=1, source_target_pairs={{0,4},{1,5},{2,6},{3,7},{4,0},{5,1},{6,2},{7,3},{8,12},{9,13},{10,... | collective-permute-start | bytes 344072 | tf_op jit(solution)/shard_map/ppermute | solution.py:478
  59.0 168.0 %collective-permute-start.4 = (bf16[2,1,2,112,128]{4,3,2,1,0:T(8,128)(2,1)S(1)}, bf16[2,1,2,112,128]{4,3,2,1,0:T(8,128)(2,1)S(1)}, u32[]{:S(2)}, u32[]{:S(2)}) collective-permute-start(bf16[2,1,2,112,128]{4,3,2,1,0:T(8,128)(2,1)S(1)} %copy-done.18), channel_id=1, source_target_pairs={{0,5},{1,4},{2,7},{3,6},{4,1},{5,0},{6,3},{7,2},{8,13},{9,12},{10,... | collective-permute-start | bytes 344072 | tf_op jit(solution)/shard_map/ppermute | solution.py:478
  62.4 2.5 copy-start.5
  69.0 18.8 %copy-start.17 = (bf16[2,1,2,112,128]{4,3,2,1,0:T(8,128)(2,1)S(1)}, bf16[2,1,2,112,128]{4,3,2,1,0:T(8,128)(2,1)}, u32[]{:S(2)}) copy-start(bf16[2,1,2,112,128]{4,3,2,1,0:T(8,128)(2,1)} %get-tuple-element.36) | copy-start | bytes 344068
  69.0 32.4 %copy-start.16 = (bf16[2,1,2,112,128]{4,3,2,1,0:T(8,128)(2,1)S(1)}, bf16[2,1,2,112,128]{4,3,2,1,0:T(8,128)(2,1)}, u32[]{:S(2)}) copy-start(bf16[2,1,2,112,128]{4,3,2,1,0:T(8,128)(2,1)} %get-tuple-element.37) | copy-start | bytes 344068
  87.8 204.6 %copy-start.6 = (bf16[2,1,2,112,128]{4,3,2,1,0:T(8,128)(2,1)}, bf16[2,1,2,112,128]{4,3,2,1,0:T(8,128)(2,1)S(1)}, u32[]{:S(2)}) copy-start(bf16[2,1,2,112,128]{4,3,2,1,0:T(8,128)(2,1)S(1)} %collective-permute-done.refs_1_) | copy-start | bytes 344068
  87.8 139.9 %collective-permute-start.5 = (bf16[2,1,2,112,128]{4,3,2,1,0:T(8,128)(2,1)S(1)}, bf16[2,1,2,112,128]{4,3,2,1,0:T(8,128)(2,1)S(1)}, u32[]{:S(2)}, u32[]{:S(2)}) collective-permute-start(bf16[2,1,2,112,128]{4,3,2,1,0:T(8,128)(2,1)S(1)} %copy-done.17), channel_id=1, source_target_pairs={{0,6},{1,7},{2,4},{3,5},{4,2},{5,3},{6,0},{7,1},{8,14},{9,15},{10,... | collective-permute-start | bytes 344072 | tf_op jit(solution)/shard_map/ppermute | solution.py:478
  101.4 191.0 %copy-start.7 = (bf16[2,1,2,112,128]{4,3,2,1,0:T(8,128)(2,1)}, bf16[2,1,2,112,128]{4,3,2,1,0:T(8,128)(2,1)S(1)}, u32[]{:S(2)}) copy-start(bf16[2,1,2,112,128]{4,3,2,1,0:T(8,128)(2,1)S(1)} %collective-permute-done.1.refs_2_) | copy-start | bytes 344068
  101.4 128.8 %collective-permute-start.6 = (bf16[2,1,2,112,128]{4,3,2,1,0:T(8,128)(2,1)S(1)}, bf16[2,1,2,112,128]{4,3,2,1,0:T(8,128)(2,1)S(1)}, u32[]{:S(2)}, u32[]{:S(2)}) collective-permute-start(bf16[2,1,2,112,128]{4,3,2,1,0:T(8,128)(2,1)S(1)} %copy-done.16), channel_id=1, source_target_pairs={{0,7},{1,6},{2,5},{3,4},{4,3},{5,2},{6,1},{7,0},{8,15},{9,14},{10,... | collective-permute-start | bytes 344072 | tf_op jit(solution)/shard_map/ppermute | solution.py:478
  117.8 174.6 %copy-start.8 = (bf16[2,1,2,112,128]{4,3,2,1,0:T(8,128)(2,1)}, bf16[2,1,2,112,128]{4,3,2,1,0:T(8,128)(2,1)S(1)}, u32[]{:S(2)}) copy-start(bf16[2,1,2,112,128]{4,3,2,1,0:T(8,128)(2,1)S(1)} %collective-permute-done.2.refs_3_) | copy-start | bytes 344068
  223.6 68.8 %copy-start.9 = (bf16[2,1,2,112,128]{4,3,2,1,0:T(8,128)(2,1)}, bf16[2,1,2,112,128]{4,3,2,1,0:T(8,128)(2,1)S(1)}, u32[]{:S(2)}) copy-start(bf16[2,1,2,112,128]{4,3,2,1,0:T(8,128)(2,1)S(1)} %collective-permute-done.3.refs_4_) | copy-start | bytes 344068
  227.0 65.4 %copy-start.10 = (bf16[2,1,2,112,128]{4,3,2,1,0:T(8,128)(2,1)}, bf16[2,1,2,112,128]{4,3,2,1,0:T(8,128)(2,1)S(1)}, u32[]{:S(2)}) copy-start(bf16[2,1,2,112,128]{4,3,2,1,0:T(8,128)(2,1)S(1)} %collective-permute-done.4.refs_5_) | copy-start | bytes 344068
  227.7 64.7 %copy-start.11 = (bf16[2,1,2,112,128]{4,3,2,1,0:T(8,128)(2,1)}, bf16[2,1,2,112,128]{4,3,2,1,0:T(8,128)(2,1)S(1)}, u32[]{:S(2)}) copy-start(bf16[2,1,2,112,128]{4,3,2,1,0:T(8,128)(2,1)S(1)} %collective-permute-done.5.refs_6_) | copy-start | bytes 344068
  230.2 62.3 %copy-start.12 = (bf16[2,1,2,112,128]{4,3,2,1,0:T(8,128)(2,1)}, bf16[2,1,2,112,128]{4,3,2,1,0:T(8,128)(2,1)S(1)}, u32[]{:S(2)}) copy-start(bf16[2,1,2,112,128]{4,3,2,1,0:T(8,128)(2,1)S(1)} %collective-permute-done.6.refs_7_) | copy-start | bytes 344068
  230.2 46.4 %copy-start.3 = (bf16[16,12,2,16,128]{4,3,2,1,0:T(8,128)(2,1)}, bf16[16,12,2,16,128]{4,3,2,1,0:T(8,128)(2,1)S(1)}, u32[]{:S(2)}) copy-start(bf16[16,12,2,16,128]{4,3,2,1,0:T(8,128)(2,1)S(1)} %constant_dynamic-update-slice_fusion.lead) | copy-start | bytes 4718596
  275.5 20.1 %collective-permute-start.7 = (bf16[8,1,2,112,128]{4,3,2,1,0:T(8,128)(2,1)S(1)}, bf16[8,1,2,112,128]{4,3,2,1,0:T(8,128)(2,1)S(1)}, u32[]{:S(2)}, u32[]{:S(2)}) collective-permute-start(bf16[8,1,2,112,128]{4,3,2,1,0:T(8,128)(2,1)S(1)} %slice_dynamic-update-slice_fusion), channel_id=1, source_target_pairs={{0,8},{1,9},{2,10},{3,11},{4,12},{5,13},{6,14},{7,15},{8,0},{9,1},... | collective-permute-start | bytes 1376264 | tf_op jit(solution)/shard_map/ppermute | solution.py:478
  295.6 0.8 copy-start.4
  299.6 77.1 %all-to-all-start.2 = ((bf16[16,12,2,16,256]{4,3,2,1,0:T(8,128)(2,1)}), bf16[16,12,2,16,256]{4,3,2,1,0:T(8,128)(2,1)}, u32[]{:S(2)}, u32[]{:S(2)}) async-start(bf16[16,12,2,16,256]{4,3,2,1,0:T(8,128)(2,1)} %beams.3), calls=%async_computation.2 | async-start | bytes 6291456 | tf_op jit(solution)/shard_map/all_to_all | solution.py:471
  329.0 54.9 %copy-start.1 = (f32[256,1024]{1,0:T(8,128)S(1)}, f32[256,1024]{1,0:T(8,128)}, u32[]{:S(2)}) copy-start(f32[256,1024]{1,0:T(8,128)} %param.12) | copy-start | bytes 3145732
